TPU v7x, 32 devices: a whole 2x2x4 slice. The times are simulated.
32 devices in a mesh: dp: 8 (over y, x, core), group: 4 (over z).
Axes of the slice: x: 2, y: 2, z: 4, core: 2. Of those that a mesh axis runs over, the one named last changes fastest.
Arguments:
- act_query: bfloat16 [8192, 768], P(('dp', 'group')), may hold values from -6 to 6
- grad_query: bfloat16 [8192, 768], P(('dp', 'group')), may hold values from -6 to 6
- act_keyval: bfloat16 [8192, 768], P(('dp', 'group')), may hold values from -6 to 6
- grad_keyval: bfloat16 [8192, 128], P(('dp', 'group')), may hold values from -6 to 6
- sample_rows: int32 [4096], P(('dp', 'group')), may hold values from 0 to 255
- state_aq: float32 [768, 768], P('dp'), as said below
- state_gq: float32 [768, 768], P('dp'), as said below
- state_akv: float32 [768, 768], P('dp'), as said below
- state_gkv: float32 [128, 128], P('dp'), as said below
- weight_query: float32 [768, 768], P('dp'), may hold values from -0.21875 to 0.21875
- weight_keyval: float32 [768, 128], P('dp'), may hold values from -0.21875 to 0.21875
- moment_query: float32 [768, 768], P('dp'), may hold values from -6 to 6
- moment_keyval: float32 [768, 128], P('dp'), may hold values from -6 to 6
Outputs:
- new_state_aq: float32 [768, 768], P('dp')
- new_state_gq: float32 [768, 768], P('dp')
- new_state_akv: float32 [768, 768], P('dp')
- new_state_gkv: float32 [128, 128], P('dp')
- new_weight_query: float32 [768, 768], P('dp')
- new_weight_keyval: float32 [768, 128], P('dp')
- new_moment_query: float32 [768, 768], P('dp')
- new_moment_keyval: float32 [768, 128], P('dp')
Inputs may be any that keep to these rules, and one draw needn't show every extreme that they name: `sample_rows`: each entry indexes one of the 256 tokens of the device that holds it. `state_aq`: symmetric positive definite. `state_gq`: symmetric positive definite. `state_akv`: symmetric positive definite. `state_gkv`: symmetric positive definite.
All inputs are finite; a program needn't handle non-finite values. Where the computation divides by a largest or mean magnitude, that divisor is 1e-20 or more.
Results may differ from a plain program's by a relative error of at most 0.0003.
Values sent between devices are 32-bit elements; how exact they have to be, the bound alone decides.
No kernel may reach another device: no remote copies, remote signals or barrier semaphores. Data moves between devices by JAX's collectives and lax.ppermute only.
A program may use at most 128 MiB of HBM per device.

v0:
```python
import jax
import jax.numpy as jnp
from jax import lax
from jax.sharding import PartitionSpec as P

PRECISE = lax.Precision.HIGHEST
BLEND_RATE = 0.8
DAMPING = 0.05
MOMENTUM = 0.9
LEARNING_RATE = 0.001
TRUST_BOUND = 0.5


def from_root(value, axis, source):
    kept = jnp.where(lax.axis_index(axis) == source, value, 0).astype(value.dtype)
    return lax.psum(kept, axis)


def newton(damped):
    extent = damped.shape[0]
    identity = jnp.eye(extent, dtype=jnp.float32)
    inverse_norm = 1.0 / jnp.max(jnp.sum(jnp.abs(damped), axis=1))
    iterate = inverse_norm * (2.0 * identity - inverse_norm * damped)
    product = jnp.dot(damped, iterate, precision=PRECISE)
    iterate = jnp.dot(iterate, 2.0 * identity - product, precision=PRECISE)
    return iterate


def damped_inverse(factor):
    extent = factor.shape[0]
    identity = jnp.eye(extent, dtype=jnp.float32)
    return newton(factor + DAMPING * jnp.trace(factor) / extent * identity)


def precondition(left_inverse, gradient, right_inverse):
    return jnp.dot(
        jnp.dot(left_inverse, gradient, precision=PRECISE), right_inverse, precision=PRECISE
    )


def inner_rows(first_block, second_block):
    return lax.dot_general(
        first_block, second_block, (((0,), (0,)), ((), ())), preferred_element_type=jnp.float32
    )


def deliver(matrix, holder):
    return from_root(matrix, ("dp", "group"), holder)


def owner_step(left_factor, right_factor, gradient):
    return precondition(damped_inverse(left_factor), gradient, damped_inverse(right_factor))


def shards(
    act_query,
    grad_query,
    act_keyval,
    grad_keyval,
    sample_rows,
    state_aq,
    state_gq,
    state_akv,
    state_gkv,
    weight_query,
    weight_keyval,
    moment_query,
    moment_keyval,
):
    devices = lax.axis_size("dp") * lax.axis_size("group")
    total_samples = sample_rows.shape[0] * devices
    flat_index = lax.axis_index("dp") * lax.axis_size("group") + lax.axis_index("group")
    extent = state_aq.shape[0]
    start = lax.axis_index("dp") * extent

    def covariance(tokens_block):
        chosen = jnp.take(tokens_block, sample_rows, axis=0)
        return inner_rows(chosen, chosen)

    local_terms = (
        covariance(act_query),
        covariance(grad_query),
        covariance(act_keyval),
        covariance(grad_keyval),
        inner_rows(act_query, grad_query),
        inner_rows(act_keyval, grad_keyval),
    )
    shares = (
        lax.psum_scatter(local_terms[0], "dp", scatter_dimension=0, tiled=True),
        lax.psum_scatter(local_terms[1], "dp", scatter_dimension=0, tiled=True),
        lax.psum_scatter(local_terms[2], "dp", scatter_dimension=0, tiled=True),
        lax.psum_scatter(local_terms[3], "dp", scatter_dimension=0, tiled=True),
        lax.psum_scatter(local_terms[4], "dp", scatter_dimension=0, tiled=True),
        lax.psum_scatter(local_terms[5], "dp", scatter_dimension=0, tiled=True),
    )
    totals = lax.psum((shares[0], shares[1], shares[2], shares[3], shares[4], shares[5]), "group")
    cov_aq, cov_gq, cov_akv, cov_gkv, rows_q, rows_kv = totals
    new_aq = BLEND_RATE * state_aq + (1.0 - BLEND_RATE) * (cov_aq / total_samples)
    new_gq = BLEND_RATE * state_gq + (1.0 - BLEND_RATE) * (cov_gq / total_samples)
    new_akv = BLEND_RATE * state_akv + (1.0 - BLEND_RATE) * (cov_akv / total_samples)
    new_gkv = BLEND_RATE * state_gkv + (1.0 - BLEND_RATE) * (cov_gkv / total_samples)
    gathered = (
        lax.all_gather(new_aq, "dp", axis=0, tiled=True),
        lax.all_gather(new_gq, "dp", axis=0, tiled=True),
        lax.all_gather(new_akv, "dp", axis=0, tiled=True),
        lax.all_gather(new_gkv, "dp", axis=0, tiled=True),
        lax.all_gather(rows_q, "dp", axis=0, tiled=True),
        lax.all_gather(rows_kv, "dp", axis=0, tiled=True),
    )
    whole_aq, whole_gq, whole_akv, whole_gkv, whole_sum_q, whole_sum_kv = gathered
    holders = (0, 0, 1, 1)
    pairs = (
        (whole_aq, whole_gq, whole_sum_q, rows_q, holders[0], holders[1]),
        (whole_akv, whole_gkv, whole_sum_kv, rows_kv, holders[2], holders[3]),
    )
    step_rows = []
    fitness = jnp.zeros((), jnp.float32)
    for left_factor, right_factor, gradient, gradient_rows, left_holder, right_holder in pairs:
        whole_step = lax.cond(
            flat_index == left_holder,
            owner_step,
            lambda first, second, third: jnp.zeros_like(third),
            left_factor,
            right_factor,
            gradient,
        )
        whole_step = deliver(whole_step, left_holder)
        fitness = fitness + jnp.sum(whole_step * gradient)
        step_rows.append(lax.dynamic_slice_in_dim(whole_step, start, extent, 0))
    scale = jnp.sqrt(TRUST_BOUND / (LEARNING_RATE * LEARNING_RATE * fitness))
    moment_q = MOMENTUM * moment_query + scale * step_rows[0]
    moment_kv = MOMENTUM * moment_keyval + scale * step_rows[1]
    weight_q = weight_query - LEARNING_RATE * moment_q
    weight_kv = weight_keyval - LEARNING_RATE * moment_kv
    return (new_aq, new_gq, new_akv, new_gkv, weight_q, weight_kv, moment_q, moment_kv)


def solution(mesh):
    placed = (
        P(("dp", "group"), None),
        P(("dp", "group"), None),
        P(("dp", "group"), None),
        P(("dp", "group"), None),
        P(("dp", "group")),
        P("dp", None),
        P("dp", None),
        P("dp", None),
        P("dp", None),
        P("dp", None),
        P("dp", None),
        P("dp", None),
        P("dp", None),
    )
    return jax.shard_map(
        shards,
        mesh=mesh,
        in_specs=placed,
        out_specs=(
            P("dp", None),
            P("dp", None),
            P("dp", None),
            P("dp", None),
            P("dp", None),
            P("dp", None),
            P("dp", None),
            P("dp", None),
        ),
        check_vma=False,
    )
```

profile of v0, /device:TPU:0, one launch (start us, length us, event | category | flops | bytes accessed | tf_op | source)
XLA Modules:
  0.0 630.8 jit_solution(17541259942685726937)
XLA Ops:
  20.6 37.4 %reduce-scatter.11.cloned.1.call-done = f32[96,768]{1,0:T(8,128)} async-done(((f32[768,768]{1,0:T(8,128)}), f32[96,768]{1,0:T(8,128)}) %reduce-scatter.11.cloned.1.call-update) | async-done | bytes 294928 | tf_op jit(solution)/shard_map/reduce_scatter | solution.py:91
  58.0 46.2 %reduce-scatter.7.cloned.1.call-done = f32[96,768]{1,0:T(8,128)} async-done(((f32[768,768]{1,0:T(8,128)}), f32[96,768]{1,0:T(8,128)}) %reduce-scatter.7.cloned.1.call-update) | async-done | bytes 294928 | tf_op jit(solution)/shard_map/reduce_scatter | solution.py:89
  104.2 45.9 %reduce-scatter.9.cloned.1.call-done = f32[96,768]{1,0:T(8,128)} async-done(((f32[768,768]{1,0:T(8,128)}), f32[96,768]{1,0:T(8,128)}) %reduce-scatter.9.cloned.1.call-update) | async-done | bytes 294928 | tf_op jit(solution)/shard_map/reduce_scatter | solution.py:90
  150.1 46.1 %reduce-scatter.15.cloned.1.call-done = f32[96,768]{1,0:T(8,128)} async-done(((f32[768,768]{1,0:T(8,128)}), f32[96,768]{1,0:T(8,128)}) %reduce-scatter.15.cloned.1.call-update) | async-done | bytes 294928 | tf_op jit(solution)/shard_map/reduce_scatter | solution.py:93
  199.1 56.5 %all-reduce.8.cloned.1.call-done = (f32[96,768]{1,0:T(8,128)}, f32[96,768]{1,0:T(8,128)}, f32[96,768]{1,0:T(8,128)}, f32[96,768]{1,0:T(8,128)}) async-done(((f32[96,768]{1,0:T(8,128)}, f32[96,768]{1,0:T(8,128)}, f32[96,768]{1,0:T(8,128)}, f32[96,768]{1,0:T(8,128)}), (f32[96,768]{1,0:T(8,128)}, f32[96,768]{1,0:T(8,128)}, f32[96,768]{1,0:T(8,128)}, f32[96,768]{1,0:T(8,128)})) %all-reduce.8.cloned.1.call-update) | async-done | bytes 1179664 | tf_op jit(solution)/shard_map/psum | solution.py:96
  260.7 31.2 %reduce-scatter.13.cloned.1.call-done = f32[16,128]{1,0:T(8,128)} async-done(((f32[128,128]{1,0:T(8,128)}), f32[16,128]{1,0:T(8,128)}) %reduce-scatter.13.cloned.1.call-update) | async-done | bytes 8208 | tf_op jit(solution)/shard_map/reduce_scatter | solution.py:92
  291.9 37.2 %reduce-scatter.17.cloned.1.call-done = f32[96,128]{1,0:T(8,128)} async-done(((f32[768,128]{1,0:T(8,128)}), f32[96,128]{1,0:T(8,128)}) %reduce-scatter.17.cloned.1.call-update) | async-done | bytes 49168 | tf_op jit(solution)/shard_map/reduce_scatter | solution.py:94
  329.1 20.2 %all-reduce.1 = (f32[16,128]{1,0:T(8,128)S(1)}, f32[96,128]{1,0:T(8,128)S(1)}) all-reduce(f32[16,128]{1,0:T(8,128)} %reduce-scatter.13.cloned.1.call-done, f32[96,128]{1,0:T(8,128)} %reduce-scatter.17.cloned.1.call-done), channel_id=1, replica_groups=mesh['dp'=8,'group'=4] {'group'}, use_global_device_ids=true, to_apply=%region_7.9 | all-reduce | flops 14336 | bytes 114688 | tf_op jit(solution)/shard_map/psum | solution.py:96
  349.4 10.3 %all_gather.23 = f32[128,128]{1,0:T(8,128)} all-gather(f32[16,128]{1,0:T(8,128)S(1)} %multiply_add_fusion.5), channel_id=1, replica_groups=mesh['dp'=8,'group'=4] {'dp'}, dimensions={0}, use_global_device_ids=true | all-gather | bytes 73728 | tf_op jit(solution)/shard_map/all_gather | solution.py:106
  359.6 8.6 %all_gather.22 = f32[768,128]{1,0:T(8,128)S(1)} all-gather(f32[96,128]{1,0:T(8,128)S(1)} %get-tuple-element.36), channel_id=1, replica_groups=mesh['dp'=8,'group'=4] {'dp'}, dimensions={0}, use_global_device_ids=true | all-gather | bytes 442368 | tf_op jit(solution)/shard_map/all_gather | solution.py:108
  368.3 24.3 %all-gather.9.cloned.1.call-done = f32[768,768]{1,0:T(8,128)} async-done(((f32[96,768]{1,0:T(8,128)}), f32[768,768]{1,0:T(8,128)}) %all-gather.9.cloned.1.call-update) | async-done | bytes 2359312 | tf_op jit(solution)/shard_map/all_gather | solution.py:104
  392.6 30.9 %all-gather.7.cloned.1.call-done = f32[768,768]{1,0:T(8,128)} async-done(((f32[96,768]{1,0:T(8,128)}), f32[768,768]{1,0:T(8,128)}) %all-gather.7.cloned.1.call-update) | async-done | bytes 2359312 | tf_op jit(solution)/shard_map/all_gather | solution.py:107
  423.5 52.6 %conditional.2 = (f32[768,768]{1,0:T(8,128)}) conditional(s32[]{:T(128)} %convert_element_type.11, () %tuple.21, (f32[768,768]{1,0:T(8,128)}, f32[768,768]{1,0:T(8,128)}, f32[768,768]{1,0:T(8,128)}) %tuple.22), branch_computations={%region_10.12_spmd, %region_11.19_spmd} | conditional | flops 32647348224 | bytes 75509960 | solution.py:119
  424.1 2.5 select_reduce_fusion.1
  427.2 2.4 select_reduce_fusion
  433.7 6.1 fusion.8
  439.8 6.4 %fusion.1 = f32[768,768]{1,0:T(8,128)S(1)} fusion(f32[768,768]{1,0:T(8,128)S(1)} %fusion.8, f32[768,768]{1,0:T(8,128)S(1)} %copy-done.6, f32[]{:T(128)S(6)} %div.3, f32[]{:T(128)S(6)} %div.2), kind=kOutput, calls=%fused_computation.9 | convolution fusion | flops 5441716224 | bytes 7077896 | tf_op jit(solution)/shard_map/cond/branch_1_fun/dot_general | solution.py:25
  446.2 5.8 fusion.87
  453.4 8.7 %fusion.5 = f32[768,768]{1,0:T(8,128)S(1)} fusion(f32[768,768]{1,0:T(8,128)} %get-tuple-element.17, f32[]{:T(128)S(6)} %div.16, f32[]{:T(128)S(6)} %div.8), kind=kOutput, calls=%fused_computation.12 | convolution fusion | flops 5441716224 | bytes 4718600 | tf_op jit(solution)/shard_map/cond/branch_1_fun/dot_general | solution.py:24
  462.1 6.4 %fusion.3 = f32[768,768]{1,0:T(8,128)S(1)} fusion(f32[768,768]{1,0:T(8,128)S(1)} %fusion.5, f32[768,768]{1,0:T(8,128)S(1)} %copy-done.7, f32[]{:T(128)S(6)} %div.16, f32[]{:T(128)S(6)} %div.8), kind=kOutput, calls=%fused_computation.11 | convolution fusion | flops 5441716224 | bytes 7077896 | tf_op jit(solution)/shard_map/cond/branch_1_fun/dot_general | solution.py:25
  468.5 7.2 %fusion.88 = f32[768,768]{1,0:T(8,128)} fusion(f32[768,768]{1,0:T(8,128)S(1)} %fusion.87, f32[768,768]{1,0:T(8,128)S(1)} %fusion.3), kind=kOutput, calls=%fused_computation.122 | convolution fusion | flops 5435817984 | bytes 7077888 | tf_op jit(solution)/shard_map/cond/branch_1_fun/dot_general | solution.py:36
  476.1 3.2 broadcast_select_fusion
  481.7 132.7 %all-reduce.6.cloned.1.call-done = (f32[768,768]{1,0:T(8,128)}, f32[768,128]{1,0:T(8,128)}) async-done(((f32[768,768]{1,0:T(8,128)}, f32[768,128]{1,0:T(8,128)}), (f32[768,768]{1,0:T(8,128)}, f32[768,128]{1,0:T(8,128)})) %all-reduce.6.cloned.1.call-update) | async-done | bytes 2752528 | tf_op jit(solution)/shard_map/psum | solution.py:16
  616.1 2.9 multiply_reduce_fusion
  (88 shorter events, 31.9 us)
Async XLA Ops:
  7.2 50.8 %reduce-scatter.11.cloned.1.call-start = ((), (), s32[]{:S(2)}) async-start(), calls=%async_computation.8 | async-start | bytes 2654208 | tf_op jit(solution)/shard_map/reduce_scatter | solution.py:91
  12.6 91.6 %reduce-scatter.7.cloned.1.call-start = ((), (), s32[]{:S(2)}) async-start(), calls=%async_computation.6 | async-start | bytes 2654208 | tf_op jit(solution)/shard_map/reduce_scatter | solution.py:89
  15.5 134.6 %reduce-scatter.9.cloned.1.call-start = ((), (), s32[]{:S(2)}) async-start(), calls=%async_computation.7 | async-start | bytes 2654208 | tf_op jit(solution)/shard_map/reduce_scatter | solution.py:90
  18.5 177.7 %reduce-scatter.15.cloned.1.call-start = ((), (), s32[]{:S(2)}) async-start(), calls=%async_computation.11 | async-start | bytes 2654208 | tf_op jit(solution)/shard_map/reduce_scatter | solution.py:93
  20.5 175.8 %copy-start.8 = (bf16[256,128]{1,0:T(8,128)(2,1)S(1)}, bf16[256,128]{1,0:T(8,128)(2,1)}, u32[]{:S(2)}) copy-start(bf16[256,128]{1,0:T(8,128)(2,1)} %param.22) | copy-start | bytes 196612
  20.5 177.4 %copy-start.2 = (bf16[256,768]{1,0:T(8,128)(2,1)S(1)}, bf16[256,768]{1,0:T(8,128)(2,1)}, u32[]{:S(2)}) copy-start(bf16[256,768]{1,0:T(8,128)(2,1)} %param.21) | copy-start | bytes 1179652
  20.5 235.1 %copy-start.10 = (f32[96,768]{1,0:T(8,128)S(1)}, f32[96,768]{1,0:T(8,128)}, u32[]{:S(2)}) copy-start(f32[96,768]{1,0:T(8,128)} %param.24) | copy-start | bytes 884740
  20.6 236.9 %copy-start.11 = (f32[96,768]{1,0:T(8,128)S(1)}, f32[96,768]{1,0:T(8,128)}, u32[]{:S(2)}) copy-start(f32[96,768]{1,0:T(8,128)} %param.25) | copy-start | bytes 884740
  20.6 235.1 %all-reduce.8.cloned.1.call-start = ((), (), s32[]{:S(2)}) async-start(), calls=%async_computation.17 | async-start | bytes 2359296 | tf_op jit(solution)/shard_map/psum | solution.py:96
  196.2 63.6 %copy-start.12 = (f32[96,768]{1,0:T(8,128)S(1)}, f32[96,768]{1,0:T(8,128)}, u32[]{:S(2)}) copy-start(f32[96,768]{1,0:T(8,128)} %param.26) | copy-start | bytes 884740
  196.3 95.6 %reduce-scatter.13.cloned.1.call-start = ((), (), s32[]{:S(2)}) async-start(), calls=%async_computation.9 | async-start | bytes 73728 | tf_op jit(solution)/shard_map/reduce_scatter | solution.py:92
  197.9 131.2 %reduce-scatter.17.cloned.1.call-start = ((), (), s32[]{:S(2)}) async-start(), calls=%async_computation.15 | async-start | bytes 442368 | tf_op jit(solution)/shard_map/reduce_scatter | solution.py:94
  199.0 150.3 %copy-start.19 = (f32[16,128]{1,0:T(8,128)S(1)}, f32[16,128]{1,0:T(8,128)}, u32[]{:S(2)}) copy-start(f32[16,128]{1,0:T(8,128)} %param.27) | copy-start | bytes 24580
  199.1 169.2 %all-gather.5.cloned.1.call-start = ((), (), s32[]{:S(2)}) async-start(), calls=%async_computation.10 | async-start | bytes 2654208 | tf_op jit(solution)/shard_map/all_gather | solution.py:103
  257.4 135.1 %all-gather.9.cloned.1.call-start = ((), (), s32[]{:S(2)}) async-start(), calls=%async_computation.13 | async-start | bytes 2654208 | tf_op jit(solution)/shard_map/all_gather | solution.py:104
  259.2 164.2 %all-gather.7.cloned.1.call-start = ((), (), s32[]{:S(2)}) async-start(), calls=%async_computation.12 | async-start | bytes 2654208 | tf_op jit(solution)/shard_map/all_gather | solution.py:107
  259.8 219.5 %all-gather.11.cloned.1.call-start = ((), (), s32[]{:S(2)}) async-start(), calls=%async_computation.14 | async-start | bytes 2654208 | tf_op jit(solution)/shard_map/all_gather | solution.py:105
  260.7 353.7 %all-reduce.6.cloned.1.call-start = ((), (), s32[]{:S(2)}) async-start(), calls=%async_computation.16 | async-start | bytes 5505024 | tf_op jit(solution)/shard_map/psum | solution.py:16
  349.4 74.1 %copy-start.18 = (f32[16,128]{1,0:T(8,128)}, f32[16,128]{1,0:T(8,128)S(1)}, u32[]{:S(2)}) copy-start(f32[16,128]{1,0:T(8,128)S(1)} %multiply_add_fusion.5) | copy-start | bytes 24580
  424.1 6.2 copy-start.6
  439.8 6.4 %copy-start.4 = (f32[768,768]{1,0:T(8,128)S(1)}, f32[768,768]{1,0:T(8,128)}, u32[]{:S(2)}) copy-start(f32[768,768]{1,0:T(8,128)} %get-tuple-element.16) | copy-start | bytes 7077892 | tf_op jit(solution)/shard_map/cond
  453.4 8.7 %copy-start.7 = (f32[768,768]{1,0:T(8,128)S(1)}, f32[768,768]{1,0:T(8,128)}, u32[]{:S(2)}) copy-start(f32[768,768]{1,0:T(8,128)} %get-tuple-element.17) | copy-start | bytes 7077892 | tf_op jit(solution)/shard_map/cond
  480.8 135.3 %copy-start.3 = (f32[768,768]{1,0:T(8,128)S(1)}, f32[768,768]{1,0:T(8,128)}, u32[]{:S(2)}) copy-start(f32[768,768]{1,0:T(8,128)} %all-gather.7.cloned.1.call-done) | copy-start | bytes 7077892
  616.1 5.8 copy-start.13
  (6 other events, 26.3 us)
Sparse Core Ops, SparseCore 0:
  12.7 45.1 reduce-scatter.10
  61.7 42.4 reduce-scatter.6
  107.6 42.4 reduce-scatter.8
  153.7 42.4 reduce-scatter.14
  198.7 56.9 all-reduce.7
  259.1 32.7 reduce-scatter.12
  295.2 33.8 reduce-scatter.16
  331.7 29.2 all-gather.4
  363.7 28.8 all-gather.8
  394.4 29.0 all-gather.6
  426.1 29.0 all-gather.10
  481.8 132.5 all-reduce.5
where the time goes:
time: 636 us; the launch traced here: 631 us
  waiting for transfers between devices  489 us (77%)
  matrix products  50.5 us (8%)
  blocking collectives  39.1 us (6%)
  other arithmetic  25.8 us (4%)
  between operations  16 us (3%)
    psum x1, waiting for transfers between devices, from_root(): return lax.psum(kept, axis)  133 us
    psum x1, waiting for transfers between devices, shards(): lax.psum((shares[0], shares[1], shares[2], shares[3], shares[4], shares[5...  56.5 us
    reduce_scatter x1, waiting for transfers between devices, shards(): lax.psum_scatter(local_terms[0], 'dp', scatter_dimension=0, tiled=True)  46.2 us
    reduce_scatter x1, waiting for transfers between devices, shards(): lax.psum_scatter(local_terms[4], 'dp', scatter_dimension=0, tiled=True)  46.1 us
    reduce_scatter x1, waiting for transfers between devices, shards(): lax.psum_scatter(local_terms[1], 'dp', scatter_dimension=0, tiled=True)  45.9 us
    reduce_scatter x1, waiting for transfers between devices, shards(): lax.psum_scatter(local_terms[2], 'dp', scatter_dimension=0, tiled=True)  37.4 us
    reduce_scatter x1, waiting for transfers between devices, shards(): lax.psum_scatter(local_terms[5], 'dp', scatter_dimension=0, tiled=True)  37.2 us
    reduce_scatter x1, waiting for transfers between devices, shards(): lax.psum_scatter(local_terms[3], 'dp', scatter_dimension=0, tiled=True)  31.2 us
  transfers between devices with their start and end apart: 12, of which 10 were waited for; matrix products, arithmetic and copies ran while one was open for 11% of the time, Pallas kernels for 0%

commit v1 on v0

--- a/solution.py
+++ b/solution.py
@@ -1,6 +1,10 @@
+import functools
+
 import jax
 import jax.numpy as jnp
 from jax import lax
+from jax.experimental import pallas as pl
+from jax.experimental.pallas import tpu as pltpu
 from jax.sharding import PartitionSpec as P
 
 PRECISE = lax.Precision.HIGHEST
@@ -9,6 +13,379 @@
 MOMENTUM = 0.9
 LEARNING_RATE = 0.001
 TRUST_BOUND = 0.5
+LANES = 128
+F32 = jnp.float32
+BF16 = jnp.bfloat16
+VMEM_LIMIT = 48 * 1024 * 1024
+
+
+def rolled(block, shift):
+    return pltpu.roll(block, shift, 1)
+
+
+def window_tiles(block, start, width):
+    extent = block.shape[1]
+    shift = lax.rem(extent - start, extent)
+    turned = rolled(block, shift)
+    return [turned[:, LANES * t:LANES * (t + 1)] for t in range(width // LANES)]
+
+
+def plain_tiles(block):
+    return [block[:, LANES * t:LANES * (t + 1)] for t in range(block.shape[1] // LANES)]
+
+
+def write_tiles(ref, lead, tiles, at=0):
+    for tile in tiles:
+        ref[lead, at:at + tile.shape[0], :] = tile
+        at += tile.shape[0]
+    return at
+
+
+def product(first, second):
+    return lax.dot_general(
+        first, second, (((1,), (0,)), ((), ())), preferred_element_type=F32
+    )
+
+
+def gram_kernel(
+    n, k, width, scale,
+    pos, rows_own, rows_other, aq, gq, akv, gkv, other, st_aq, st_gq, st_akv, st_gkv,
+    a_send, a_keep, b_send, b_keep, s_send, s_keep, k_send, k_keep,
+    t_q, t_kv, u_aq, u_gq, u_akv, u_gkv, g_kv,
+):
+    q, c = pos[0], pos[1]
+    D = aq.shape[1]
+    tokens = aq.shape[0]
+    samples = rows_own.shape[1]
+
+    def picker(rows):
+        token = lax.broadcasted_iota(jnp.int32, (tokens, samples), 0)
+        return (token == rows[...]).astype(F32).T.astype(BF16)
+
+    pick_own, pick_other = picker(rows_own), picker(rows_other)
+
+    def both(own, lo, hi):
+        return jnp.concatenate([own[...], other[:, lo:hi].astype(BF16)], axis=0)
+
+    def sampled(own, lo, hi):
+        return jnp.concatenate(
+            [product(pick_own, own[...]), product(pick_other, other[:, lo:hi].astype(BF16))],
+            axis=0,
+        )
+
+    def turn(ref, values):
+        ref[...] = values.astype(F32).T.astype(BF16)
+
+    y_aq = sampled(aq, 0, D)
+    y_gq = sampled(gq, D, 2 * D)
+    y_akv = sampled(akv, 2 * D, 3 * D)
+    y_gkv = sampled(gkv, 3 * D, 3 * D + gkv.shape[1])
+    turn(u_aq, y_aq)
+    turn(u_gq, y_gq)
+    turn(u_akv, y_akv)
+    turn(u_gkv, y_gkv)
+    turn(t_q, both(aq, 0, D))
+    turn(t_kv, both(akv, 2 * D, 3 * D))
+    y_aq, y_gq = y_aq.astype(BF16), y_gq.astype(BF16)
+    y_akv, y_gkv = y_akv.astype(BF16), y_gkv.astype(BF16)
+
+    blocks = [2 * jnp.bitwise_xor(q, r) + c for r in range(4)]
+
+    def left(ref):
+        parts = [ref[pl.ds(pl.multiple_of(n * b, 32), n), :] for b in blocks]
+        return jnp.concatenate(parts, axis=0)
+
+    def four(values):
+        return [values[n * r:n * (r + 1)] for r in range(4)]
+
+    share = BLEND_RATE / 4.0
+
+    def window(values, r):
+        return window_tiles(values, n * blocks[r], width)
+
+    def place(send, keep, first, tiles, at=0):
+        second = 3 - first
+        write_tiles(send, 0, tiles[first], at)
+        write_tiles(send, 1, tiles[3], at)
+        write_tiles(keep, 0, tiles[0], at)
+        return write_tiles(keep, 1, tiles[second], at)
+
+    def factor(ref, y, state):
+        parts = four(product(left(ref), y) * scale)
+        parts[0] = parts[0] + share * state[...]
+        return [window(parts[r], r) for r in range(4)]
+
+    place(a_send, a_keep, 1, factor(u_aq, y_aq, st_aq))
+    place(b_send, b_keep, 2, factor(u_gq, y_gq, st_gq))
+    sum_q = four(product(left(t_q), both(gq, D, 2 * D)))
+    place(s_send, s_keep, 1, [plain_tiles(part) for part in sum_q])
+    at = place(k_send, k_keep, 2, factor(u_akv, y_akv, st_akv))
+    sum_kv = four(product(left(t_kv), both(gkv, 3 * D, 3 * D + gkv.shape[1])))
+    at = place(k_send, k_keep, 2, [plain_tiles(part) for part in sum_kv], at)
+    g_kv[...] = product(u_gkv[...], y_gkv) * scale
+    small = [g_kv[pl.ds(pl.multiple_of(k * b, 8), k), :] for b in blocks]
+    small[0] = small[0] + share * st_gkv[...]
+    place(k_send, k_keep, 2, [[part] for part in small], at)
+
+
+def identity_rows(rows, extent, start):
+    row = lax.broadcasted_iota(jnp.int32, (rows, extent), 0) + start
+    column = lax.broadcasted_iota(jnp.int32, (rows, extent), 1)
+    return row == column
+
+
+def scaled_inverse_terms(matrix):
+    extent = matrix.shape[0]
+    on_diagonal = identity_rows(extent, extent, 0)
+    trace = jnp.sum(jnp.where(on_diagonal, matrix, 0.0))
+    damped = matrix + jnp.where(on_diagonal, DAMPING * trace / extent, 0.0)
+    c = 1.0 / jnp.max(jnp.sum(jnp.abs(damped), axis=1))
+    return c, c * damped
+
+
+def halves(values):
+    high = values.astype(BF16)
+    return high, (values - high.astype(F32)).astype(BF16)
+
+
+def times(values, high, low):
+    v_high, v_low = halves(values)
+    rows = values.shape[0]
+    stacked = product(jnp.concatenate([v_high, v_low], axis=0), high)
+    return stacked[:rows] + stacked[rows:] + product(v_high, low)
+
+
+def piece_blocks(q, c):
+    own = [2 * jnp.bitwise_xor(q, r) + c for r in range(4)]
+    other = [2 * jnp.bitwise_xor(q, r) + (1 - c) for r in range(4)]
+    return own + other
+
+
+def assemble(pieces, blocks, n, width, extent, whole):
+    tiles = width // LANES
+    for piece, b in zip(pieces, blocks):
+        parts = [piece[n * t:n * (t + 1), :] for t in range(tiles)]
+        parts += [jnp.zeros((n, LANES), F32)] * (extent // LANES - tiles)
+        turned = rolled(jnp.concatenate(parts, axis=1), n * b)
+        whole[pl.ds(pl.multiple_of(n * b, 8), n), :] = turned
+    windows = whole[...]
+
+    def block_of(axis):
+        shape = (extent, 1) if axis == 0 else (1, extent)
+        index = lax.broadcasted_iota(jnp.int32, shape, axis)
+        return sum([(index >= n * step).astype(jnp.int32) for step in range(1, 8)])
+
+    apart = jnp.bitwise_and(block_of(1) - block_of(0), 7)
+    matrix = jnp.where(apart <= 4, windows, windows.T)
+    return matrix
+
+
+def own_rows(ref, q, c, n):
+    return ref[pl.ds(pl.multiple_of(n * (2 * q + c), 8), n), :]
+
+
+def left_rows(c, rows, start, high, low):
+    first = jnp.where(identity_rows(rows.shape[0], rows.shape[1], start), 2.0, 0.0) - rows
+    second = times(first, high, low)
+    third = 2.0 * second - times(second, high, low)
+    return c * (2.0 * first - third)
+
+
+def right_product(values, c, high, low):
+    first = 2.0 * values - times(values, high, low)
+    second = times(first, high, low)
+    third = 2.0 * second - times(second, high, low)
+    return c * (2.0 * first - third)
+
+
+def left_kernel(n, width, pos, *refs):
+    pieces, (new_ref, x_ref, whole, high_ref, low_ref) = refs[:8], refs[8:]
+    q, c = pos[0], pos[1]
+    extent = whole.shape[0]
+    matrix = assemble(pieces, piece_blocks(q, c), n, width, extent, whole)
+    whole[...] = matrix
+    new_ref[...] = own_rows(whole, q, c, n)
+    factor, scaled = scaled_inverse_terms(matrix)
+    whole[...] = scaled
+    high_ref[...], low_ref[...] = halves(scaled)
+    x_ref[...] = left_rows(
+        factor, own_rows(whole, q, c, n), n * (2 * q + c), high_ref[...], low_ref[...]
+    )
+
+
+def middle_kernel(n, pos, x_ref, *refs):
+    pieces, (t_ref, high_ref, low_ref) = refs[:8], refs[8:]
+    q, c = pos[0], pos[1]
+    tiles = high_ref.shape[1] // LANES
+    for piece, b in zip(pieces, piece_blocks(q, c)):
+        rows = jnp.concatenate([piece[n * t:n * (t + 1), :] for t in range(tiles)], axis=1)
+        at = pl.ds(pl.multiple_of(n * b, 32), n)
+        high_ref[at, :], low_ref[at, :] = halves(rows)
+    t_ref[...] = times(x_ref[...], high_ref[...], low_ref[...])
+
+
+def right_kernel(n, width, pos, t_ref, s_own, *refs):
+    pieces, (new_ref, step_ref, fit_ref, whole, high_ref, low_ref) = refs[:8], refs[8:]
+    q, c = pos[0], pos[1]
+    extent = whole.shape[0]
+    matrix = assemble(pieces, piece_blocks(q, c), n, width, extent, whole)
+    whole[...] = matrix
+    new_ref[...] = own_rows(whole, q, c, n)
+    factor, scaled = scaled_inverse_terms(matrix)
+    high_ref[...], low_ref[...] = halves(scaled)
+    step = right_product(t_ref[...], factor, high_ref[...], low_ref[...])
+    step_ref[...] = step
+    tiles = extent // LANES
+    gradient = jnp.concatenate([s_own[n * t:n * (t + 1), :] for t in range(tiles)], axis=1)
+    fit_ref[...] = jnp.broadcast_to(jnp.sum(step * gradient), fit_ref.shape)
+
+
+def keyval_kernel(n, k, width, pos, *refs):
+    pieces = refs[:8]
+    new_left, new_right, step_ref, fit_ref = refs[8:12]
+    whole, high_ref, low_ref, grad_ref, g_ref = refs[12:]
+    q, c = pos[0], pos[1]
+    extent = whole.shape[0]
+    blocks = piece_blocks(q, c)
+    base = n * (width // LANES)
+    for piece, b in zip(pieces, blocks):
+        grad_ref[pl.ds(pl.multiple_of(n * b, 8), n), :] = piece[base:base + n, :]
+        g_ref[pl.ds(pl.multiple_of(k * b, 8), k), :] = piece[base + n:base + n + k, :]
+    matrix = assemble(pieces, blocks, n, width, extent, whole)
+    whole[...] = matrix
+    new_left[...] = own_rows(whole, q, c, n)
+    new_right[...] = own_rows(g_ref, q, c, k)
+    factor, scaled = scaled_inverse_terms(matrix)
+    whole[...] = scaled
+    high_ref[...], low_ref[...] = halves(scaled)
+    x_rows = left_rows(
+        factor, own_rows(whole, q, c, n), n * (2 * q + c), high_ref[...], low_ref[...]
+    )
+    t_rows = times(x_rows, *halves(grad_ref[...]))
+    factor, scaled = scaled_inverse_terms(g_ref[...])
+    step = right_product(t_rows, factor, *halves(scaled))
+    step_ref[...] = step
+    fit_ref[...] = jnp.broadcast_to(jnp.sum(step * own_rows(grad_ref, q, c, n)), fit_ref.shape)
+
+
+def call(kernel, outs, scratch, count, flops=0):
+    vmem = pl.BlockSpec(memory_space=pltpu.VMEM)
+    smem = pl.BlockSpec(memory_space=pltpu.SMEM)
+    return pl.pallas_call(
+        kernel,
+        out_shape=[jax.ShapeDtypeStruct(shape, F32) for shape in outs],
+        in_specs=[smem] + [vmem] * (count - 1),
+        out_specs=[vmem] * len(outs),
+        scratch_shapes=[pltpu.VMEM(shape, kind) for shape, kind in scratch],
+        compiler_params=pltpu.CompilerParams(vmem_limit_bytes=VMEM_LIMIT),
+        cost_estimate=pl.CostEstimate(flops=flops, bytes_accessed=4_000_000, transcendentals=0),
+    )
+
+
+def flip(value, bit, axis="dp", size=8):
+    return lax.ppermute(value, axis, [(i, i ^ bit) for i in range(size)])
+
+
+def reduce_piece(send, keep, first, second):
+    came = flip(send, first)
+    partial = keep[1] + came[1]
+    return (keep[0] + came[0]) + flip(partial, second)
+
+
+def reduce_planes(piece, first, second):
+    piece = piece + flip(piece, first, "group", 4)
+    return piece + flip(piece, second, "group", 4)
+
+
+def spread(piece, x_bit, first, second):
+    near = flip(piece, first)
+    across = flip(piece, second)
+    far = flip(across, first)
+    own = {0: piece, first: near, second: across, first | second: far}
+    ordered = [own[r << 1] for r in range(4)]
+    return ordered + [flip(value, 1) for value in ordered]
+
+
+def fast_shards(
+    act_query, grad_query, act_keyval, grad_keyval, sample_rows,
+    state_aq, state_gq, state_akv, state_gkv,
+    weight_query, weight_keyval, moment_query, moment_keyval,
+):
+    D, KV = act_query.shape[1], grad_keyval.shape[1]
+    n, k = state_aq.shape[0], state_gkv.shape[0]
+    tokens, samples = act_query.shape[0], sample_rows.shape[0]
+    width = -(-5 * n // LANES) * LANES
+    d = lax.axis_index("dp")
+    pos = jnp.stack([d // 2, d % 2]).astype(jnp.int32)
+    scale = (1.0 - BLEND_RATE) / (samples * 32)
+
+    mine = jnp.concatenate([act_query, grad_query, act_keyval, grad_keyval], axis=1).astype(F32)
+    other = flip(mine, 1)
+    rows_own = sample_rows.reshape(1, samples)
+    rows_other = flip(rows_own, 1)
+
+    r_f, r_s = n * (width // LANES), n * (D // LANES)
+    r_k = r_f + n * (KV // LANES) + k
+    outs = []
+    for rows in (r_f, r_f, r_s, r_k):
+        outs += [(2, rows, LANES)] * 2
+    grams = call(
+        functools.partial(gram_kernel, n, k, width, scale),
+        outs,
+        [
+            ((D, 2 * tokens), BF16), ((D, 2 * tokens), BF16),
+            ((D, 2 * samples), BF16), ((D, 2 * samples), BF16), ((D, 2 * samples), BF16),
+            ((KV, 2 * samples), BF16), ((KV, KV), F32),
+        ],
+        12,
+        2_000_000_000,
+    )(
+        pos, rows_own, rows_other, act_query, grad_query, act_keyval, grad_keyval, other,
+        state_aq, state_gq, state_akv, state_gkv,
+    )
+    X, Y = 2, 4
+    own_a = reduce_piece(grams[0], grams[1], X, Y)
+    own_b = reduce_piece(grams[2], grams[3], Y, X)
+    own_s = reduce_piece(grams[4], grams[5], X, Y)
+    own_k = reduce_piece(grams[6], grams[7], Y, X)
+    own_a = reduce_planes(own_a, 1, 2)
+    own_b = reduce_planes(own_b, 2, 1)
+    own_s = reduce_planes(own_s, 1, 2)
+    own_k = reduce_planes(own_k, 2, 1)
+    all_a = spread(own_a, X, X, Y)
+    all_b = spread(own_b, X, Y, X)
+    all_s = spread(own_s, X, X, Y)
+    all_k = spread(own_k, X, Y, X)
+
+    square = [((D, D), F32), ((D, D), BF16), ((D, D), BF16)]
+    fit = (8, LANES)
+    new_aq, x_rows = call(
+        functools.partial(left_kernel, n, width), [(n, D)] * 2, square, 9, 700_000_000
+    )(pos, *all_a)
+    (t_rows,) = call(
+        functools.partial(middle_kernel, n), [(n, D)], square[1:], 10, 350_000_000
+    )(pos, x_rows, *all_s)
+    new_gq, step_q, fit_q = call(
+        functools.partial(right_kernel, n, width), [(n, D), (n, D), fit], square, 11, 1_000_000_000
+    )(pos, t_rows, own_s, *all_b)
+    new_akv, new_gkv, step_kv, fit_kv = call(
+        functools.partial(keyval_kernel, n, k, width),
+        [(n, D), (k, KV), (n, KV), fit],
+        square + [((D, KV), F32), ((KV, KV), F32)],
+        9,
+        1_000_000_000,
+    )(pos, *all_k)
+
+    total = fit_q + fit_kv
+    for bit in (1, 2, 4):
+        total = total + flip(total, bit)
+    fitness = total[0, 0]
+    scale = jnp.sqrt(TRUST_BOUND / (LEARNING_RATE * LEARNING_RATE * fitness))
+    moment_q = MOMENTUM * moment_query + scale * step_q
+    moment_kv = MOMENTUM * moment_keyval + scale * step_kv
+    weight_q = weight_query - LEARNING_RATE * moment_q
+    weight_kv = weight_keyval - LEARNING_RATE * moment_kv
+    return (new_aq, new_gq, new_akv, new_gkv, weight_q, weight_kv, moment_q, moment_kv)
 
 
 def from_root(value, axis, source):
@@ -151,8 +528,9 @@
         P("dp", None),
         P("dp", None),
     )
+    plane = mesh.shape["dp"] == 8 and mesh.shape["group"] == 4
     return jax.shard_map(
-        shards,
+        fast_shards if plane else shards,
         mesh=mesh,
         in_specs=placed,
         out_specs=(

time: 636 us -> 149 us (0.23)
  waiting for transfers between devices: 489 us -> 88.9 us
  matrix products: 50.5 us -> 0 us
  blocking collectives: 39.1 us -> 0 us
  starting transfers between devices: 0.49 us -> 34.5 us
  other arithmetic: 25.8 us -> 5.1 us
  Pallas kernels: 0 us -> 18.4 us
  between operations: 16 us -> 1.81 us
    reduce_scatter x6 -> x0, waiting for transfers between devices: 244 us -> none  [the longest x1 46.2 us: shards(): lax.psum_scatter(local_terms[0], 'dp', scatter_dimension=0, tiled=True)]
    psum x2 -> x0, waiting for transfers between devices: 189 us -> none  [the longest x1 133 us: from_root(): return lax.psum(kept, axis)]
    ppermute x0 -> x49, waiting for transfers between devices: none -> 88.9 us  [flip(): return lax.ppermute(value, axis, [(i, i ^ bit) for i in range(size)])]
    all_gather x4 -> x0, waiting for transfers between devices: 55.2 us -> none  [the longest x1 30.9 us: shards(): lax.all_gather(rows_q, 'dp', axis=0, tiled=True)]
    dot_general x12 -> x0, matrix products: 50.5 us -> none  [the longest x2 14.7 us: newton(): product = jnp.dot(damped, iterate, precision=PRECISE)]
    ppermute x0 -> x49, starting transfers between devices: none -> 34.5 us  [flip(): return lax.ppermute(value, axis, [(i, i ^ bit) for i in range(size)])]
    psum x1 -> x0, blocking collectives: 20.2 us -> none  [shards(): lax.psum((shares[0], shares[1], shares[2], shares[3], shares[4], shares[5...]
    all_gather x2 -> x0, blocking collectives: 18.9 us -> none  [the longest x1 10.3 us: shards(): lax.all_gather(new_gkv, 'dp', axis=0, tiled=True)]
  transfers between devices with their start and end apart: 12 -> 49, of which waited for: 10 -> 21; matrix products, arithmetic and copies ran while one was open for 11% -> 0% of each run, Pallas kernels for 0% -> 7%
where the time goes in v1:
time: 149 us
  waiting for transfers between devices  88.9 us (60%)
  starting transfers between devices  34.5 us (23%)
  Pallas kernels  18.4 us (12%)
  other arithmetic  5.1 us (3%)
  between operations  1.81 us (1%)
    ppermute x49, waiting for transfers between devices, flip(): return lax.ppermute(value, axis, [(i, i ^ bit) for i in range(size)])  88.9 us
    ppermute x49, starting transfers between devices, flip(): return lax.ppermute(value, axis, [(i, i ^ bit) for i in range(size)])  34.5 us
    pallas_call x1, Pallas kernels, fast_shards(): call(functools.partial(keyval_kernel, n, k, width), [(n, D), (k, KV), (n,...  5.17 us
    pallas_call x1, Pallas kernels, fast_shards(): call(functools.partial(right_kernel, n, width), [(n, D), (n, D), fit], sq...  4.2 us
    pallas_call x1, Pallas kernels, fast_shards(): call(functools.partial(gram_kernel, n, k, width, scale), outs, [((D, 2 *...  3.85 us
    pallas_call x1, Pallas kernels, fast_shards(): call(functools.partial(left_kernel, n, width), [(n, D)] * 2, square, 9, 7...  3.61 us
    convert_element_type x1, other arithmetic, fast_shards(): jnp.concatenate([act_query, grad_query, act_keyval, grad_keyval], axis=1)  2.99 us
  transfers between devices with their start and end apart: 49, of which 21 were waited for; matrix products, arithmetic and copies ran while one was open for 0% of the time, Pallas kernels for 7%

profile of v1, /device:TPU:0, one launch (start us, length us, event | category | flops | bytes accessed | tf_op | source)
XLA Modules:
  0.0 149.3 jit_solution(13205294995891713930)
XLA Ops:
  0.7 3.0 %maximum_convert_fusion = f32[256,2432]{1,0:T(8,128)} fusion(bf16[256,128]{1,0:T(8,128)(2,1)} %gkv.1, bf16[256,768]{1,0:T(8,128)(2,1)} %akv.1, bf16[256,768]{1,0:T(8,128)(2,1)} %gq.1, bf16[256,768]{1,0:T(8,128)(2,1)} %aq.1), kind=kLoop, calls=%fused_computation | loop fusion | flops 4980736 | bytes 3735552 | tf_op jit(solution)/shard_map/convert_element_type | solution.py:322
  4.3 4.1 %collective-permute-done.rows_other = s32[1,128]{1,0:T(1,128)S(1)} collective-permute-done((s32[1,128]{1,0:T(1,128)S(1)}, s32[1,128]{1,0:T(1,128)S(1)}, u32[]{:S(2)}, u32[]{:S(2)}) %collective-permute-start) | collective-permute-done | bytes 544 | tf_op jit(solution)/shard_map/ppermute | solution.py:286
  8.9 3.9 %shard_map.188 = (f32[2,384,128]{2,1,0:T(8,128)S(1)}, f32[2,384,128]{2,1,0:T(8,128)S(1)}, f32[2,384,128]{2,1,0:T(8,128)S(1)}, f32[2,384,128]{2,1,0:T(8,128)S(1)}...) custom-call(s32[2]{0:T(128)S(1)} %pad_add_fusion.pos, ...), custom_call_target="tpu_custom_call" | custom-call | flops 2000000000 | bytes 4000000 | tf_op jit(solution)/shard_map/pallas_call | solution.py:332
  12.8 2.9 %collective-permute-start.2 = (f32[2,384,128]{2,1,0:T(8,128)S(1)}, f32[2,384,128]{2,1,0:T(8,128)S(1)}, u32[]{:S(2)}, u32[]{:S(2)}) collective-permute-start(f32[2,384,128]{2,1,0:T(8,128)S(1)} %get-tuple-element.26), channel_id=1, source_target_pairs={{0,8},{4,12},{8,0},{12,4},{16,24},{20,28},{24,16},{28,20},{1,9},{5... | collective-permute-start | bytes 1179656 | tf_op jit(solution)/shard_map/ppermute | solution.py:286
  17.8 7.8 %collective-permute-done.2 = f32[2,384,128]{2,1,0:T(8,128)S(1)} collective-permute-done((f32[2,384,128]{2,1,0:T(8,128)S(1)}, f32[2,384,128]{2,1,0:T(8,128)S(1)}, u32[]{:S(2)}, u32[]{:S(2)}) %collective-permute-start.2) | collective-permute-done | bytes 393248 | tf_op jit(solution)/shard_map/ppermute | solution.py:286
  29.4 9.2 %collective-permute-done.35 = f32[2,496,128]{2,1,0:T(8,128)S(1)} collective-permute-done((f32[2,496,128]{2,1,0:T(8,128)S(1)}, f32[2,496,128]{2,1,0:T(8,128)S(1)}, u32[]{:S(2)}, u32[]{:S(2)}) %collective-permute-start.35) | collective-permute-done | bytes 507936 | tf_op jit(solution)/shard_map/ppermute | solution.py:286
  38.7 2.9 %collective-permute-done.3 = f32[384,128]{1,0:T(8,128)S(1)} collective-permute-done((f32[384,128]{1,0:T(8,128)S(1)}, f32[384,128]{1,0:T(8,128)S(1)}, u32[]{:S(2)}, u32[]{:S(2)}) %collective-permute-start.3) | collective-permute-done | bytes 196640 | tf_op jit(solution)/shard_map/ppermute | solution.py:286
  45.0 2.6 %collective-permute-start.26 = (f32[384,128]{1,0:T(8,128)S(1)}, f32[384,128]{1,0:T(8,128)S(1)}, u32[]{:S(2)}, u32[]{:S(2)}) collective-permute-start(f32[384,128]{1,0:T(8,128)S(1)} %fusion.8), channel_id=1, source_target_pairs={{0,2},{1,3},{2,0},{3,1},{4,6},{5,7},{6,4},{7,5},{8,10},{9,11},{10,... | collective-permute-start | bytes 589832 | tf_op jit(solution)/shard_map/ppermute | solution.py:286
  47.7 2.6 %collective-permute-start.37 = (f32[496,128]{1,0:T(8,128)S(1)}, f32[496,128]{1,0:T(8,128)S(1)}, u32[]{:S(2)}, u32[]{:S(2)}) collective-permute-start(f32[496,128]{1,0:T(8,128)S(1)} %fusion.5), channel_id=1, source_target_pairs={{0,2},{1,3},{2,0},{3,1},{4,6},{5,7},{6,4},{7,5},{8,10},{9,11},{10,... | collective-permute-start | bytes 761864 | tf_op jit(solution)/shard_map/ppermute | solution.py:286
  52.3 14.5 %collective-permute-done.26 = f32[384,128]{1,0:T(8,128)S(1)} collective-permute-done((f32[384,128]{1,0:T(8,128)S(1)}, f32[384,128]{1,0:T(8,128)S(1)}, u32[]{:S(2)}, u32[]{:S(2)}) %collective-permute-start.26) | collective-permute-done | bytes 196640 | tf_op jit(solution)/shard_map/ppermute | solution.py:286
  69.0 5.8 %collective-permute-done.5 = f32[384,128]{1,0:T(8,128)S(1)} collective-permute-done((f32[384,128]{1,0:T(8,128)S(1)}, f32[384,128]{1,0:T(8,128)S(1)}, u32[]{:S(2)}, u32[]{:S(2)}) %collective-permute-start.5) | collective-permute-done | bytes 196640 | tf_op jit(solution)/shard_map/ppermute | solution.py:286
  75.6 3.5 %collective-permute-done.27 = f32[384,128]{1,0:T(8,128)S(1)} collective-permute-done((f32[384,128]{1,0:T(8,128)S(1)}, f32[384,128]{1,0:T(8,128)S(1)}, u32[]{:S(2)}, u32[]{:S(2)}) %collective-permute-start.27) | collective-permute-done | bytes 196640 | tf_op jit(solution)/shard_map/ppermute | solution.py:286
  80.4 4.9 %collective-permute-done.15 = f32[576,128]{1,0:T(8,128)S(1)} collective-permute-done((f32[576,128]{1,0:T(8,128)S(1)}, f32[576,128]{1,0:T(8,128)S(1)}, u32[]{:S(2)}, u32[]{:S(2)}) %collective-permute-start.15) | collective-permute-done | bytes 294944 | tf_op jit(solution)/shard_map/ppermute | solution.py:286
  88.2 5.0 %collective-permute-done.28.refs_1_ = f32[384,128]{1,0:T(8,128)S(1)} collective-permute-done((f32[384,128]{1,0:T(8,128)S(1)}, f32[384,128]{1,0:T(8,128)S(1)}, u32[]{:S(2)}, u32[]{:S(2)}) %collective-permute-start.28) | collective-permute-done | bytes 196640 | tf_op jit(solution)/shard_map/ppermute | solution.py:286
  93.8 2.5 %collective-permute-done.8.refs_3_ = f32[384,128]{1,0:T(8,128)S(1)} collective-permute-done((f32[384,128]{1,0:T(8,128)S(1)}, f32[384,128]{1,0:T(8,128)S(1)}, u32[]{:S(2)}, u32[]{:S(2)}) %collective-permute-start.8) | collective-permute-done | bytes 196640 | tf_op jit(solution)/shard_map/ppermute | solution.py:286
  96.3 5.5 %collective-permute-done.16 = f32[576,128]{1,0:T(8,128)S(1)} collective-permute-done((f32[576,128]{1,0:T(8,128)S(1)}, f32[576,128]{1,0:T(8,128)S(1)}, u32[]{:S(2)}, u32[]{:S(2)}) %collective-permute-start.16) | collective-permute-done | bytes 294944 | tf_op jit(solution)/shard_map/ppermute | solution.py:286
  103.9 2.3 %collective-permute-done.40.refs_2_ = f32[496,128]{1,0:T(8,128)S(1)} collective-permute-done((f32[496,128]{1,0:T(8,128)S(1)}, f32[496,128]{1,0:T(8,128)S(1)}, u32[]{:S(2)}, u32[]{:S(2)}) %collective-permute-start.40) | collective-permute-done | bytes 253984 | tf_op jit(solution)/shard_map/ppermute | solution.py:286
  106.8 3.8 %collective-permute-done.39.refs_1_ = f32[496,128]{1,0:T(8,128)S(1)} collective-permute-done((f32[496,128]{1,0:T(8,128)S(1)}, f32[496,128]{1,0:T(8,128)S(1)}, u32[]{:S(2)}, u32[]{:S(2)}) %collective-permute-start.39) | collective-permute-done | bytes 253984 | tf_op jit(solution)/shard_map/ppermute | solution.py:286
  112.8 4.2 %collective-permute-done.17.refs_1_ = f32[576,128]{1,0:T(8,128)S(1)} collective-permute-done((f32[576,128]{1,0:T(8,128)S(1)}, f32[576,128]{1,0:T(8,128)S(1)}, u32[]{:S(2)}, u32[]{:S(2)}) %collective-permute-start.17) | collective-permute-done | bytes 294944 | tf_op jit(solution)/shard_map/ppermute | solution.py:286
  119.2 2.9 %collective-permute-done.19.refs_3_ = f32[576,128]{1,0:T(8,128)S(1)} collective-permute-done((f32[576,128]{1,0:T(8,128)S(1)}, f32[576,128]{1,0:T(8,128)S(1)}, u32[]{:S(2)}, u32[]{:S(2)}) %collective-permute-start.19) | collective-permute-done | bytes 294944 | tf_op jit(solution)/shard_map/ppermute | solution.py:286
  123.2 3.6 %shard_map.189 = (f32[96,768]{1,0:T(8,128)}, f32[96,768]{1,0:T(8,128)S(1)}) custom-call(s32[2]{0:T(128)S(1)} %pad_add_fusion.pos, f32[384,128]{1,0:T(8,128)S(1)} %add.114.refs_0_, f32[384,128]{1,0:T(8,128)S(1)} %collective-permute-done.6.refs_1_, f32[384,128]{1,0:T(8,128)S(1)} %collective-permute-done.7.refs_2_, ...), custom_call_target="tpu_custom_call" | custom-call | flops 700000000 | bytes 4000000 | tf_op jit(solution)/shard_map/pallas_call | solution.py:362
  126.8 5.2 %shard_map.192 = (f32[96,768]{1,0:T(8,128)}, f32[16,128]{1,0:T(8,128)}, f32[96,128]{1,0:T(8,128)S(1)}, f32[8,128]{1,0:T(8,128)S(1)}) custom-call(s32[2]{0:T(128)S(1)} %pad_add_fusion.pos, f32[496,128]{1,0:T(8,128)S(1)} %add.135.refs_0_, f32[496,128]{1,0:T(8,128)S(1)} %collective-permute-done.39.refs_1_, f32[496,128]{1,0:T(8,128)S(1)} %collective-permute-done.40.refs_2_, ...), custom_call_target="tpu_custom_call" | custom-call | flops 1000000000 | bytes 4000000 | tf_op jit(solution)/shard_map/pallas_call | solution.py:371
  133.7 4.2 %shard_map.191 = (f32[96,768]{1,0:T(8,128)}, f32[96,768]{1,0:T(8,128)S(1)}, f32[8,128]{1,0:T(8,128)S(1)}) custom-call(s32[2]{0:T(128)S(1)} %pad_add_fusion.pos, f32[96,768]{1,0:T(8,128)S(1)} %shard_map.190.t_ref, f32[576,128]{1,0:T(8,128)S(1)} %add.121.refs_0_.s_own, f32[384,128]{1,0:T(8,128)S(1)} %add.128.refs_0_, ...), custom_call_target="tpu_custom_call" | custom-call | flops 1000000000 | bytes 4000000 | tf_op jit(solution)/shard_map/pallas_call | solution.py:368
  143.0 3.4 %collective-permute-done.48 = f32[8,128]{1,0:T(8,128)S(1)} collective-permute-done((f32[8,128]{1,0:T(8,128)S(1)}, f32[8,128]{1,0:T(8,128)S(1)}, u32[]{:S(2)}, u32[]{:S(2)}) %collective-permute-start.48) | collective-permute-done | bytes 4128 | tf_op jit(solution)/shard_map/ppermute | solution.py:286
  (130 shorter events, 37.0 us)
Async XLA Ops:
  12.8 12.8 %collective-permute-start.2 = (f32[2,384,128]{2,1,0:T(8,128)S(1)}, f32[2,384,128]{2,1,0:T(8,128)S(1)}, u32[]{:S(2)}, u32[]{:S(2)}) collective-permute-start(f32[2,384,128]{2,1,0:T(8,128)S(1)} %get-tuple-element.26), channel_id=1, source_target_pairs={{0,8},{4,12},{8,0},{12,4},{16,24},{20,28},{24,16},{28,20},{1,9},{5... | collective-permute-start | bytes 1179656 | tf_op jit(solution)/shard_map/ppermute | solution.py:286
  15.7 12.1 %collective-permute-start.24 = (f32[2,384,128]{2,1,0:T(8,128)S(1)}, f32[2,384,128]{2,1,0:T(8,128)S(1)}, u32[]{:S(2)}, u32[]{:S(2)}) collective-permute-start(f32[2,384,128]{2,1,0:T(8,128)S(1)} %get-tuple-element.32), channel_id=1, source_target_pairs={{0,16},{4,20},{8,24},{12,28},{16,0},{20,4},{24,8},{28,12},{1,17},{... | collective-permute-start | bytes 1179656 | tf_op jit(solution)/shard_map/ppermute | solution.py:286
  17.2 21.4 %collective-permute-start.35 = (f32[2,496,128]{2,1,0:T(8,128)S(1)}, f32[2,496,128]{2,1,0:T(8,128)S(1)}, u32[]{:S(2)}, u32[]{:S(2)}) collective-permute-start(f32[2,496,128]{2,1,0:T(8,128)S(1)} %get-tuple-element.35), channel_id=1, source_target_pairs={{0,16},{4,20},{8,24},{12,28},{16,0},{20,4},{24,8},{28,12},{1,17},{... | collective-permute-start | bytes 1523720 | tf_op jit(solution)/shard_map/ppermute | solution.py:286
  17.7 25.6 %collective-permute-start.13 = (f32[2,576,128]{2,1,0:T(8,128)S(1)}, f32[2,576,128]{2,1,0:T(8,128)S(1)}, u32[]{:S(2)}, u32[]{:S(2)}) collective-permute-start(f32[2,576,128]{2,1,0:T(8,128)S(1)} %get-tuple-element.30), channel_id=1, source_target_pairs={{0,8},{4,12},{8,0},{12,4},{16,24},{20,28},{24,16},{28,20},{1,9},{5... | collective-permute-start | bytes 1769480 | tf_op jit(solution)/shard_map/ppermute | solution.py:286
  25.6 16.0 %collective-permute-start.3 = (f32[384,128]{1,0:T(8,128)S(1)}, f32[384,128]{1,0:T(8,128)S(1)}, u32[]{:S(2)}, u32[]{:S(2)}) collective-permute-start(f32[384,128]{1,0:T(8,128)S(1)} %fusion.9), channel_id=1, source_target_pairs={{0,16},{4,20},{8,24},{12,28},{16,0},{20,4},{24,8},{28,12},{1,17},{... | collective-permute-start | bytes 589832 | tf_op jit(solution)/shard_map/ppermute | solution.py:286
  27.8 17.2 %collective-permute-start.25 = (f32[384,128]{1,0:T(8,128)S(1)}, f32[384,128]{1,0:T(8,128)S(1)}, u32[]{:S(2)}, u32[]{:S(2)}) collective-permute-start(f32[384,128]{1,0:T(8,128)S(1)} %fusion.6), channel_id=1, source_target_pairs={{0,8},{4,12},{8,0},{12,4},{16,24},{20,28},{24,16},{28,20},{1,9},{5... | collective-permute-start | bytes 589832 | tf_op jit(solution)/shard_map/ppermute | solution.py:286
  43.4 23.5 %collective-permute-start.14 = (f32[576,128]{1,0:T(8,128)S(1)}, f32[576,128]{1,0:T(8,128)S(1)}, u32[]{:S(2)}, u32[]{:S(2)}) collective-permute-start(f32[576,128]{1,0:T(8,128)S(1)} %fusion), channel_id=1, source_target_pairs={{0,16},{4,20},{8,24},{12,28},{16,0},{20,4},{24,8},{28,12},{1,17},{... | collective-permute-start | bytes 884744 | tf_op jit(solution)/shard_map/ppermute | solution.py:286
  45.0 21.7 %collective-permute-start.26 = (f32[384,128]{1,0:T(8,128)S(1)}, f32[384,128]{1,0:T(8,128)S(1)}, u32[]{:S(2)}, u32[]{:S(2)}) collective-permute-start(f32[384,128]{1,0:T(8,128)S(1)} %fusion.8), channel_id=1, source_target_pairs={{0,2},{1,3},{2,0},{3,1},{4,6},{5,7},{6,4},{7,5},{8,10},{9,11},{10,... | collective-permute-start | bytes 589832 | tf_op jit(solution)/shard_map/ppermute | solution.py:286
  47.7 31.9 %collective-permute-start.37 = (f32[496,128]{1,0:T(8,128)S(1)}, f32[496,128]{1,0:T(8,128)S(1)}, u32[]{:S(2)}, u32[]{:S(2)}) collective-permute-start(f32[496,128]{1,0:T(8,128)S(1)} %fusion.5), channel_id=1, source_target_pairs={{0,2},{1,3},{2,0},{3,1},{4,6},{5,7},{6,4},{7,5},{8,10},{9,11},{10,... | collective-permute-start | bytes 761864 | tf_op jit(solution)/shard_map/ppermute | solution.py:286
  50.4 24.5 %collective-permute-start.5 = (f32[384,128]{1,0:T(8,128)S(1)}, f32[384,128]{1,0:T(8,128)S(1)}, u32[]{:S(2)}, u32[]{:S(2)}) collective-permute-start(f32[384,128]{1,0:T(8,128)S(1)} %add.113), channel_id=1, source_target_pairs={{0,2},{1,3},{2,0},{3,1},{4,6},{5,7},{6,4},{7,5},{8,10},{9,11},{10,... | collective-permute-start | bytes 589832 | tf_op jit(solution)/shard_map/ppermute | solution.py:286
  66.8 12.2 %collective-permute-start.27 = (f32[384,128]{1,0:T(8,128)S(1)}, f32[384,128]{1,0:T(8,128)S(1)}, u32[]{:S(2)}, u32[]{:S(2)}) collective-permute-start(f32[384,128]{1,0:T(8,128)S(1)} %add.127), channel_id=1, source_target_pairs={{0,1},{1,0},{2,3},{3,2},{4,5},{5,4},{6,7},{7,6},{8,9},{9,8},{10,11... | collective-permute-start | bytes 589832 | tf_op jit(solution)/shard_map/ppermute | solution.py:286
  66.9 18.4 %collective-permute-start.15 = (f32[576,128]{1,0:T(8,128)S(1)}, f32[576,128]{1,0:T(8,128)S(1)}, u32[]{:S(2)}, u32[]{:S(2)}) collective-permute-start(f32[576,128]{1,0:T(8,128)S(1)} %fusion.2), channel_id=1, source_target_pairs={{0,1},{1,0},{2,3},{3,2},{4,5},{5,4},{6,7},{7,6},{8,9},{9,8},{10,11... | collective-permute-start | bytes 884744 | tf_op jit(solution)/shard_map/ppermute | solution.py:286
  74.9 11.0 %collective-permute-start.7 = (f32[384,128]{1,0:T(8,128)S(1)}, f32[384,128]{1,0:T(8,128)S(1)}, u32[]{:S(2)}, u32[]{:S(2)}) collective-permute-start(f32[384,128]{1,0:T(8,128)S(1)} %add.114.refs_0_), channel_id=1, source_target_pairs={{0,16},{4,20},{8,24},{12,28},{16,0},{20,4},{24,8},{28,12},{1,17},{... | collective-permute-start | bytes 589832 | tf_op jit(solution)/shard_map/ppermute | solution.py:286
  80.4 12.8 %collective-permute-start.38 = (f32[496,128]{1,0:T(8,128)S(1)}, f32[496,128]{1,0:T(8,128)S(1)}, u32[]{:S(2)}, u32[]{:S(2)}) collective-permute-start(f32[496,128]{1,0:T(8,128)S(1)} %add.134), channel_id=1, source_target_pairs={{0,1},{1,0},{2,3},{3,2},{4,5},{5,4},{6,7},{7,6},{8,9},{9,8},{10,11... | collective-permute-start | bytes 761864 | tf_op jit(solution)/shard_map/ppermute | solution.py:286
  85.9 15.8 %collective-permute-start.16 = (f32[576,128]{1,0:T(8,128)S(1)}, f32[576,128]{1,0:T(8,128)S(1)}, u32[]{:S(2)}, u32[]{:S(2)}) collective-permute-start(f32[576,128]{1,0:T(8,128)S(1)} %add.120), channel_id=1, source_target_pairs={{0,2},{1,3},{2,0},{3,1},{4,6},{5,7},{6,4},{7,5},{8,10},{9,11},{10,... | collective-permute-start | bytes 884744 | tf_op jit(solution)/shard_map/ppermute | solution.py:286
  93.1 10.1 %collective-permute-start.10 = (f32[384,128]{1,0:T(8,128)S(1)}, f32[384,128]{1,0:T(8,128)S(1)}, u32[]{:S(2)}, u32[]{:S(2)}) collective-permute-start(f32[384,128]{1,0:T(8,128)S(1)} %collective-permute-done.6.refs_1_), channel_id=1, source_target_pairs={{0,4},{4,0},{8,12},{12,8},{16,20},{20,16},{24,28},{28,24},{1,5},{5... | collective-permute-start | bytes 589832 | tf_op jit(solution)/shard_map/ppermute | solution.py:286
  93.2 10.1 %collective-permute-start.30 = (f32[384,128]{1,0:T(8,128)S(1)}, f32[384,128]{1,0:T(8,128)S(1)}, u32[]{:S(2)}, u32[]{:S(2)}) collective-permute-start(f32[384,128]{1,0:T(8,128)S(1)} %collective-permute-done.28.refs_1_), channel_id=1, source_target_pairs={{0,16},{4,20},{8,24},{12,28},{16,0},{20,4},{24,8},{28,12},{1,17},{... | collective-permute-start | bytes 589832 | tf_op jit(solution)/shard_map/ppermute | solution.py:286
  93.2 10.2 %collective-permute-start.42 = (f32[496,128]{1,0:T(8,128)S(1)}, f32[496,128]{1,0:T(8,128)S(1)}, u32[]{:S(2)}, u32[]{:S(2)}) collective-permute-start(f32[496,128]{1,0:T(8,128)S(1)} %add.135.refs_0_), channel_id=1, source_target_pairs={{0,4},{4,0},{8,12},{12,8},{16,20},{20,16},{24,28},{28,24},{1,5},{5... | collective-permute-start | bytes 761864 | tf_op jit(solution)/shard_map/ppermute | solution.py:286
  106.1 10.8 %collective-permute-start.17 = (f32[576,128]{1,0:T(8,128)S(1)}, f32[576,128]{1,0:T(8,128)S(1)}, u32[]{:S(2)}, u32[]{:S(2)}) collective-permute-start(f32[576,128]{1,0:T(8,128)S(1)} %add.121.refs_0_.s_own), channel_id=1, source_target_pairs={{0,8},{4,12},{8,0},{12,4},{16,24},{20,28},{24,16},{28,20},{1,9},{5... | collective-permute-start | bytes 884744 | tf_op jit(solution)/shard_map/ppermute | solution.py:286
  112.8 9.9 %collective-permute-start.22 = (f32[576,128]{1,0:T(8,128)S(1)}, f32[576,128]{1,0:T(8,128)S(1)}, u32[]{:S(2)}, u32[]{:S(2)}) collective-permute-start(f32[576,128]{1,0:T(8,128)S(1)} %collective-permute-done.18.refs_2_), channel_id=1, source_target_pairs={{0,4},{4,0},{8,12},{12,8},{16,20},{20,16},{24,28},{28,24},{1,5},{5... | collective-permute-start | bytes 884744 | tf_op jit(solution)/shard_map/ppermute | solution.py:286
  122.1 11.5 %collective-permute-start.31 = (f32[384,128]{1,0:T(8,128)S(1)}, f32[384,128]{1,0:T(8,128)S(1)}, u32[]{:S(2)}, u32[]{:S(2)}) collective-permute-start(f32[384,128]{1,0:T(8,128)S(1)} %add.128.refs_0_), channel_id=1, source_target_pairs={{0,4},{4,0},{8,12},{12,8},{16,20},{20,16},{24,28},{28,24},{1,5},{5... | collective-permute-start | bytes 589832 | tf_op jit(solution)/shard_map/ppermute | solution.py:286
  122.6 11.1 %collective-permute-start.32 = (f32[384,128]{1,0:T(8,128)S(1)}, f32[384,128]{1,0:T(8,128)S(1)}, u32[]{:S(2)}, u32[]{:S(2)}) collective-permute-start(f32[384,128]{1,0:T(8,128)S(1)} %collective-permute-done.28.refs_1_), channel_id=1, source_target_pairs={{0,4},{4,0},{8,12},{12,8},{16,20},{20,16},{24,28},{28,24},{1,5},{5... | collective-permute-start | bytes 589832 | tf_op jit(solution)/shard_map/ppermute | solution.py:286
  122.7 11.0 %collective-permute-start.33 = (f32[384,128]{1,0:T(8,128)S(1)}, f32[384,128]{1,0:T(8,128)S(1)}, u32[]{:S(2)}, u32[]{:S(2)}) collective-permute-start(f32[384,128]{1,0:T(8,128)S(1)} %collective-permute-done.29.refs_2_), channel_id=1, source_target_pairs={{0,4},{4,0},{8,12},{12,8},{16,20},{20,16},{24,28},{28,24},{1,5},{5... | collective-permute-start | bytes 589832 | tf_op jit(solution)/shard_map/ppermute | solution.py:286
  123.1 10.5 %collective-permute-start.34 = (f32[384,128]{1,0:T(8,128)S(1)}, f32[384,128]{1,0:T(8,128)S(1)}, u32[]{:S(2)}, u32[]{:S(2)}) collective-permute-start(f32[384,128]{1,0:T(8,128)S(1)} %collective-permute-done.30.refs_3_), channel_id=1, source_target_pairs={{0,4},{4,0},{8,12},{12,8},{16,20},{20,16},{24,28},{28,24},{1,5},{5... | collective-permute-start | bytes 589832 | tf_op jit(solution)/shard_map/ppermute | solution.py:286
  (38 other events, 300.4 us)

commit v2 on v1

--- a/solution.py
+++ b/solution.py
@@ -47,47 +47,54 @@
     )
 
 
+def cast_kernel(aq, gq, akv, gkv, out):
+    at = 0
+    for ref in (aq, gq, akv, gkv):
+        out[:, at:at + ref.shape[1]] = ref[...].astype(F32)
+        at += ref.shape[1]
+
+
+def picker(rows, tokens):
+    token = lax.broadcasted_iota(jnp.int32, (tokens, rows.shape[1]), 0)
+    return (token == rows[...]).astype(F32).T.astype(BF16)
+
+
+def turned(values):
+    return values.astype(F32).T.astype(BF16)
+
+
+def own_kernel(rows, aq, gq, akv, gkv, y_aq, y_gq, y_akv, y_gkv, u_aq, u_gq, u_akv, u_gkv, t_q, t_kv):
+    pick = picker(rows, aq.shape[0])
+    for source, y, u in ((aq, y_aq, u_aq), (gq, y_gq, u_gq), (akv, y_akv, u_akv), (gkv, y_gkv, u_gkv)):
+        chosen = product(pick, source[...])
+        y[...] = chosen.astype(BF16)
+        u[...] = chosen.T.astype(BF16)
+    t_q[...] = turned(aq[...])
+    t_kv[...] = turned(akv[...])
+
+
 def gram_kernel(
     n, k, width, scale,
-    pos, rows_own, rows_other, aq, gq, akv, gkv, other, st_aq, st_gq, st_akv, st_gkv,
-    a_send, a_keep, b_send, b_keep, s_send, s_keep, k_send, k_keep,
-    t_q, t_kv, u_aq, u_gq, u_akv, u_gkv, g_kv,
+    pos, rows_other, other, gq, gkv,
+    oy_aq, oy_gq, oy_akv, oy_gkv, ou_aq, ou_gq, ou_akv, ou_gkv, ot_q, ot_kv,
+    st_aq, st_gq, st_akv, st_gkv,
+    a_send, a_keep, b_send, b_keep, c_send, c_keep, d_send, d_keep,
+    u_aq, u_gq, u_akv, u_gkv, t_q, t_kv, g_kv,
 ):
     q, c = pos[0], pos[1]
-    D = aq.shape[1]
-    tokens = aq.shape[0]
-    samples = rows_own.shape[1]
-
-    def picker(rows):
-        token = lax.broadcasted_iota(jnp.int32, (tokens, samples), 0)
-        return (token == rows[...]).astype(F32).T.astype(BF16)
-
-    pick_own, pick_other = picker(rows_own), picker(rows_other)
-
-    def both(own, lo, hi):
-        return jnp.concatenate([own[...], other[:, lo:hi].astype(BF16)], axis=0)
-
-    def sampled(own, lo, hi):
-        return jnp.concatenate(
-            [product(pick_own, own[...]), product(pick_other, other[:, lo:hi].astype(BF16))],
-            axis=0,
-        )
-
-    def turn(ref, values):
-        ref[...] = values.astype(F32).T.astype(BF16)
-
-    y_aq = sampled(aq, 0, D)
-    y_gq = sampled(gq, D, 2 * D)
-    y_akv = sampled(akv, 2 * D, 3 * D)
-    y_gkv = sampled(gkv, 3 * D, 3 * D + gkv.shape[1])
-    turn(u_aq, y_aq)
-    turn(u_gq, y_gq)
-    turn(u_akv, y_akv)
-    turn(u_gkv, y_gkv)
-    turn(t_q, both(aq, 0, D))
-    turn(t_kv, both(akv, 2 * D, 3 * D))
-    y_aq, y_gq = y_aq.astype(BF16), y_gq.astype(BF16)
-    y_akv, y_gkv = y_akv.astype(BF16), y_gkv.astype(BF16)
+    tokens, D = gq.shape
+    KV = gkv.shape[1]
+    samples = oy_aq.shape[0]
+    pick = picker(rows_other, tokens)
+
+    def theirs(lo, hi):
+        return other[:, lo:hi].astype(BF16)
+
+    def join(u, own_u, own_y, lo, hi):
+        chosen = product(pick, theirs(lo, hi))
+        u[:, :samples] = own_u[...]
+        u[:, samples:] = chosen.T.astype(BF16)
+        return jnp.concatenate([own_y[...], chosen.astype(BF16)], axis=0)
 
     blocks = [2 * jnp.bitwise_xor(q, r) + c for r in range(4)]
 
@@ -100,32 +107,45 @@
 
     share = BLEND_RATE / 4.0
 
-    def window(values, r):
-        return window_tiles(values, n * blocks[r], width)
-
     def place(send, keep, first, tiles, at=0):
-        second = 3 - first
         write_tiles(send, 0, tiles[first], at)
         write_tiles(send, 1, tiles[3], at)
         write_tiles(keep, 0, tiles[0], at)
-        return write_tiles(keep, 1, tiles[second], at)
+        return write_tiles(keep, 1, tiles[3 - first], at)
 
     def factor(ref, y, state):
         parts = four(product(left(ref), y) * scale)
         parts[0] = parts[0] + share * state[...]
-        return [window(parts[r], r) for r in range(4)]
-
-    place(a_send, a_keep, 1, factor(u_aq, y_aq, st_aq))
-    place(b_send, b_keep, 2, factor(u_gq, y_gq, st_gq))
-    sum_q = four(product(left(t_q), both(gq, D, 2 * D)))
-    place(s_send, s_keep, 1, [plain_tiles(part) for part in sum_q])
-    at = place(k_send, k_keep, 2, factor(u_akv, y_akv, st_akv))
-    sum_kv = four(product(left(t_kv), both(gkv, 3 * D, 3 * D + gkv.shape[1])))
-    at = place(k_send, k_keep, 2, [plain_tiles(part) for part in sum_kv], at)
-    g_kv[...] = product(u_gkv[...], y_gkv) * scale
+        return [window_tiles(parts[r], n * blocks[r], width) for r in range(4)]
+
+    y = join(u_aq, ou_aq, oy_aq, 0, D)
+    at_a = place(a_send, a_keep, 1, factor(u_aq, y, st_aq))
+    y = join(u_akv, ou_akv, oy_akv, 2 * D, 3 * D)
+    at_b = place(b_send, b_keep, 2, factor(u_akv, y, st_akv))
+
+    y = join(u_gkv, ou_gkv, oy_gkv, 3 * D, 3 * D + KV)
+    g_kv[...] = product(u_gkv[...], y) * scale
     small = [g_kv[pl.ds(pl.multiple_of(k * b, 8), k), :] for b in blocks]
     small[0] = small[0] + share * st_gkv[...]
-    place(k_send, k_keep, 2, [[part] for part in small], at)
+    t_kv[:, :tokens] = ot_kv[...]
+    t_kv[:, tokens:] = turned(other[:, 2 * D:3 * D])
+    sums = four(product(
+        left(t_kv), jnp.concatenate([gkv[...], theirs(3 * D, 3 * D + KV)], axis=0)
+    ))
+    h, e = n // 2, k // 2
+    at_a = place(a_send, a_keep, 1, [[part[:h]] for part in sums], at_a)
+    place(a_send, a_keep, 1, [[part[:e]] for part in small], at_a)
+    at_b = place(b_send, b_keep, 2, [[part[h:]] for part in sums], at_b)
+    place(b_send, b_keep, 2, [[part[e:]] for part in small], at_b)
+
+    t_q[:, :tokens] = ot_q[...]
+    t_q[:, tokens:] = turned(other[:, :D])
+    sums = four(product(left(t_q), jnp.concatenate([gq[...], theirs(D, 2 * D)], axis=0)))
+    sums = [plain_tiles(part) for part in sums]
+    place(c_send, c_keep, 1, [tiles[:-1] for tiles in sums])
+    y = join(u_gq, ou_gq, oy_gq, D, 2 * D)
+    at_d = place(d_send, d_keep, 2, factor(u_gq, y, st_gq))
+    place(d_send, d_keep, 2, [tiles[-1:] for tiles in sums], at_d)
 
 
 def identity_rows(rows, extent, start):
@@ -213,18 +233,22 @@
     )
 
 
+def gradient_rows(main, rest, n):
+    tiles = main.shape[0] // n
+    parts = [main[n * t:n * (t + 1), :] for t in range(tiles)]
+    return jnp.concatenate(parts + [rest[rest.shape[0] - n:, :]], axis=1)
+
+
 def middle_kernel(n, pos, x_ref, *refs):
-    pieces, (t_ref, high_ref, low_ref) = refs[:8], refs[8:]
+    mains, rests, (t_ref, high_ref, low_ref) = refs[:8], refs[8:16], refs[16:]
     q, c = pos[0], pos[1]
-    tiles = high_ref.shape[1] // LANES
-    for piece, b in zip(pieces, piece_blocks(q, c)):
-        rows = jnp.concatenate([piece[n * t:n * (t + 1), :] for t in range(tiles)], axis=1)
+    for main, rest, b in zip(mains, rests, piece_blocks(q, c)):
         at = pl.ds(pl.multiple_of(n * b, 32), n)
-        high_ref[at, :], low_ref[at, :] = halves(rows)
+        high_ref[at, :], low_ref[at, :] = halves(gradient_rows(main, rest, n))
     t_ref[...] = times(x_ref[...], high_ref[...], low_ref[...])
 
 
-def right_kernel(n, width, pos, t_ref, s_own, *refs):
+def right_kernel(n, width, pos, t_ref, main_own, *refs):
     pieces, (new_ref, step_ref, fit_ref, whole, high_ref, low_ref) = refs[:8], refs[8:]
     q, c = pos[0], pos[1]
     extent = whole.shape[0]
@@ -235,22 +259,25 @@
     high_ref[...], low_ref[...] = halves(scaled)
     step = right_product(t_ref[...], factor, high_ref[...], low_ref[...])
     step_ref[...] = step
-    tiles = extent // LANES
-    gradient = jnp.concatenate([s_own[n * t:n * (t + 1), :] for t in range(tiles)], axis=1)
+    gradient = gradient_rows(main_own, pieces[0], n)
     fit_ref[...] = jnp.broadcast_to(jnp.sum(step * gradient), fit_ref.shape)
 
 
 def keyval_kernel(n, k, width, pos, *refs):
-    pieces = refs[:8]
-    new_left, new_right, step_ref, fit_ref = refs[8:12]
-    whole, high_ref, low_ref, grad_ref, g_ref = refs[12:]
+    mates, pieces = refs[:8], refs[8:16]
+    new_left, new_right, step_ref, fit_ref = refs[16:20]
+    whole, high_ref, low_ref, grad_ref, g_ref = refs[20:]
     q, c = pos[0], pos[1]
     extent = whole.shape[0]
     blocks = piece_blocks(q, c)
     base = n * (width // LANES)
-    for piece, b in zip(pieces, blocks):
-        grad_ref[pl.ds(pl.multiple_of(n * b, 8), n), :] = piece[base:base + n, :]
-        g_ref[pl.ds(pl.multiple_of(k * b, 8), k), :] = piece[base + n:base + n + k, :]
+    h, e = n // 2, k // 2
+    for mate, piece, b in zip(mates, pieces, blocks):
+        for half, ref in ((0, mate), (1, piece)):
+            at = pl.multiple_of(n * b + h * half, 8)
+            grad_ref[pl.ds(at, h), :] = ref[base:base + h, :]
+            at = pl.multiple_of(k * b + e * half, 8)
+            g_ref[pl.ds(at, e), :] = ref[base + h:base + h + e, :]
     matrix = assemble(pieces, blocks, n, width, extent, whole)
     whole[...] = matrix
     new_left[...] = own_rows(whole, q, c, n)
@@ -268,13 +295,30 @@
     fit_ref[...] = jnp.broadcast_to(jnp.sum(step * own_rows(grad_ref, q, c, n)), fit_ref.shape)
 
 
-def call(kernel, outs, scratch, count, flops=0):
+def update_kernel(fit_own, *refs):
+    others, refs = refs[:7], refs[7:]
+    (step_q, step_kv, weight_q, weight_kv, moment_q, moment_kv) = refs[:6]
+    outs = refs[6:]
+    total = fit_own[...]
+    for other in others:
+        total = total + other[...]
+    fitness = total[:1, :1]
+    scale = jnp.sqrt(TRUST_BOUND / (LEARNING_RATE * LEARNING_RATE * fitness))
+    for step, weight, moment, at in (
+        (step_q, weight_q, moment_q, 0), (step_kv, weight_kv, moment_kv, 1)
+    ):
+        fresh = MOMENTUM * moment[...] + scale * step[...]
+        outs[2 + at][...] = fresh
+        outs[at][...] = weight[...] - LEARNING_RATE * fresh
+
+
+def call(kernel, outs, scratch, count, flops=0, scalars=1, kind=F32):
     vmem = pl.BlockSpec(memory_space=pltpu.VMEM)
     smem = pl.BlockSpec(memory_space=pltpu.SMEM)
     return pl.pallas_call(
         kernel,
-        out_shape=[jax.ShapeDtypeStruct(shape, F32) for shape in outs],
-        in_specs=[smem] + [vmem] * (count - 1),
+        out_shape=[jax.ShapeDtypeStruct(shape, kind) for shape in outs],
+        in_specs=[smem] * scalars + [vmem] * (count - scalars),
         out_specs=[vmem] * len(outs),
         scratch_shapes=[pltpu.VMEM(shape, kind) for shape, kind in scratch],
         compiler_params=pltpu.CompilerParams(vmem_limit_bytes=VMEM_LIMIT),
@@ -286,24 +330,60 @@
     return lax.ppermute(value, axis, [(i, i ^ bit) for i in range(size)])
 
 
-def reduce_piece(send, keep, first, second):
-    came = flip(send, first)
-    partial = keep[1] + came[1]
-    return (keep[0] + came[0]) + flip(partial, second)
-
-
-def reduce_planes(piece, first, second):
-    piece = piece + flip(piece, first, "group", 4)
-    return piece + flip(piece, second, "group", 4)
-
-
-def spread(piece, x_bit, first, second):
-    near = flip(piece, first)
-    across = flip(piece, second)
-    far = flip(across, first)
-    own = {0: piece, first: near, second: across, first | second: far}
-    ordered = [own[r << 1] for r in range(4)]
-    return ordered + [flip(value, 1) for value in ordered]
+def flip_plane(value, bit):
+    return flip(value, bit, "group", 4)
+
+
+X, Y = 2, 4
+
+
+def in_order(*values):
+    return lax.optimization_barrier(values)
+
+
+def by_chip(first, own, near, across, far):
+    pieces = {0: own, first: near, X + Y - first: across, X + Y: far}
+    return [pieces[r] for r in (0, X, Y, X + Y)]
+
+
+def reduce_and_spread(a, b, s, g):
+    (a_send, a_keep), (b_send, b_keep), (s_send, s_keep), (g_send, g_keep) = a, b, s, g
+    a_came, b_came = in_order(flip(a_send, X), flip(b_send, Y))
+    a_next, b_next = a_keep[1] + a_came[1], b_keep[1] + b_came[1]
+    a_own, b_own, s_send, g_send = in_order(
+        a_keep[0] + a_came[0] + flip(a_next, Y),
+        b_keep[0] + b_came[0] + flip(b_next, X),
+        s_send, g_send,
+    )
+    a_own, b_own, s_came, g_came = in_order(
+        a_own + flip_plane(a_own, 1), b_own + flip_plane(b_own, 2),
+        flip(s_send, X), flip(g_send, Y),
+    )
+    s_next, g_next = s_keep[1] + s_came[1], g_keep[1] + g_came[1]
+    a_own, b_own, s_own, g_own = in_order(
+        a_own + flip_plane(a_own, 2), b_own + flip_plane(b_own, 1),
+        s_keep[0] + s_came[0] + flip(s_next, Y),
+        g_keep[0] + g_came[0] + flip(g_next, X),
+    )
+    a_near, a_across, b_near, b_across, s_own, g_own = in_order(
+        flip(a_own, X), flip(a_own, Y), flip(b_own, Y), flip(b_own, X),
+        s_own + flip_plane(s_own, 1), g_own + flip_plane(g_own, 2),
+    )
+    a_far, b_far, s_own, g_own = in_order(
+        flip(a_across, X), flip(b_across, Y),
+        s_own + flip_plane(s_own, 2), g_own + flip_plane(g_own, 1),
+    )
+    s_near, s_across, g_near, g_across = in_order(
+        flip(s_own, X), flip(s_own, Y), flip(g_own, Y), flip(g_own, X),
+    )
+    s_far, g_far = flip(s_across, X), flip(g_across, Y)
+    chunks = (
+        by_chip(X, a_own, a_near, a_across, a_far),
+        by_chip(Y, b_own, b_near, b_across, b_far),
+        by_chip(X, s_own, s_near, s_across, s_far),
+        by_chip(Y, g_own, g_near, g_across, g_far),
+    )
+    return [pieces + [flip(piece, 1) for piece in pieces] for pieces in chunks]
 
 
 def fast_shards(
@@ -319,72 +399,64 @@
     pos = jnp.stack([d // 2, d % 2]).astype(jnp.int32)
     scale = (1.0 - BLEND_RATE) / (samples * 32)
 
-    mine = jnp.concatenate([act_query, grad_query, act_keyval, grad_keyval], axis=1).astype(F32)
-    other = flip(mine, 1)
+    (mine,) = call(cast_kernel, [(tokens, 3 * D + KV)], [], 4, scalars=0)(
+        act_query, grad_query, act_keyval, grad_keyval
+    )
     rows_own = sample_rows.reshape(1, samples)
     rows_other = flip(rows_own, 1)
-
-    r_f, r_s = n * (width // LANES), n * (D // LANES)
-    r_k = r_f + n * (KV // LANES) + k
+    other = flip(mine, 1)
+    owns = call(
+        own_kernel,
+        [(samples, D)] * 3 + [(samples, KV)] + [(D, samples)] * 3 + [(KV, samples)]
+        + [(D, tokens)] * 2,
+        [], 5, 300_000_000, scalars=0, kind=BF16,
+    )(rows_own, act_query, grad_query, act_keyval, grad_keyval)
+
+    r_f = n * (width // LANES)
+    r_kv = r_f + n // 2 + k // 2
+    r_s = n * (D // LANES - 1)
     outs = []
-    for rows in (r_f, r_f, r_s, r_k):
+    for rows in (r_kv, r_kv, r_s, r_f + n):
         outs += [(2, rows, LANES)] * 2
     grams = call(
         functools.partial(gram_kernel, n, k, width, scale),
         outs,
-        [
-            ((D, 2 * tokens), BF16), ((D, 2 * tokens), BF16),
-            ((D, 2 * samples), BF16), ((D, 2 * samples), BF16), ((D, 2 * samples), BF16),
-            ((KV, 2 * samples), BF16), ((KV, KV), F32),
-        ],
-        12,
+        [((D, 2 * samples), BF16)] * 3 + [((KV, 2 * samples), BF16)]
+        + [((D, 2 * tokens), BF16)] * 2 + [((KV, KV), F32)],
+        19,
         2_000_000_000,
     )(
-        pos, rows_own, rows_other, act_query, grad_query, act_keyval, grad_keyval, other,
+        pos, rows_other, other, grad_query, grad_keyval, *owns,
         state_aq, state_gq, state_akv, state_gkv,
     )
-    X, Y = 2, 4
-    own_a = reduce_piece(grams[0], grams[1], X, Y)
-    own_b = reduce_piece(grams[2], grams[3], Y, X)
-    own_s = reduce_piece(grams[4], grams[5], X, Y)
-    own_k = reduce_piece(grams[6], grams[7], Y, X)
-    own_a = reduce_planes(own_a, 1, 2)
-    own_b = reduce_planes(own_b, 2, 1)
-    own_s = reduce_planes(own_s, 1, 2)
-    own_k = reduce_planes(own_k, 2, 1)
-    all_a = spread(own_a, X, X, Y)
-    all_b = spread(own_b, X, Y, X)
-    all_s = spread(own_s, X, X, Y)
-    all_k = spread(own_k, X, Y, X)
+    all_a, all_k, all_s, all_g = reduce_and_spread(grams[0:2], grams[2:4], grams[4:6], grams[6:8])
 
     square = [((D, D), F32), ((D, D), BF16), ((D, D), BF16)]
     fit = (8, LANES)
     new_aq, x_rows = call(
         functools.partial(left_kernel, n, width), [(n, D)] * 2, square, 9, 700_000_000
     )(pos, *all_a)
-    (t_rows,) = call(
-        functools.partial(middle_kernel, n), [(n, D)], square[1:], 10, 350_000_000
-    )(pos, x_rows, *all_s)
-    new_gq, step_q, fit_q = call(
-        functools.partial(right_kernel, n, width), [(n, D), (n, D), fit], square, 11, 1_000_000_000
-    )(pos, t_rows, own_s, *all_b)
     new_akv, new_gkv, step_kv, fit_kv = call(
         functools.partial(keyval_kernel, n, k, width),
         [(n, D), (k, KV), (n, KV), fit],
         square + [((D, KV), F32), ((KV, KV), F32)],
-        9,
+        17,
         1_000_000_000,
-    )(pos, *all_k)
-
-    total = fit_q + fit_kv
-    for bit in (1, 2, 4):
-        total = total + flip(total, bit)
-    fitness = total[0, 0]
-    scale = jnp.sqrt(TRUST_BOUND / (LEARNING_RATE * LEARNING_RATE * fitness))
-    moment_q = MOMENTUM * moment_query + scale * step_q
-    moment_kv = MOMENTUM * moment_keyval + scale * step_kv
-    weight_q = weight_query - LEARNING_RATE * moment_q
-    weight_kv = weight_keyval - LEARNING_RATE * moment_kv
+    )(pos, *all_a, *all_k)
+    (t_rows,) = call(
+        functools.partial(middle_kernel, n), [(n, D)], square[1:], 18, 350_000_000
+    )(pos, x_rows, *all_s, *all_g)
+    new_gq, step_q, fit_q = call(
+        functools.partial(right_kernel, n, width), [(n, D), (n, D), fit], square, 11, 1_000_000_000
+    )(pos, t_rows, all_s[0], *all_g)
+
+    part = fit_q + fit_kv
+    weight_q, weight_kv, moment_q, moment_kv = call(
+        update_kernel, [(n, D), (n, KV)] * 2, [], 14, scalars=0
+    )(
+        part, *[flip(part, bit) for bit in range(1, 8)], step_q, step_kv,
+        weight_query, weight_keyval, moment_query, moment_keyval,
+    )
     return (new_aq, new_gq, new_akv, new_gkv, weight_q, weight_kv, moment_q, moment_kv)
 
 

time: 149 us -> 146 us (0.980)
  waiting for transfers between devices: 88.9 us -> 67.9 us
  starting transfers between devices: 34.5 us -> 46.6 us
  local copies, waits for them, and re-layouts: 0.58 us -> 7.75 us
  other arithmetic: 5.1 us -> 0.61 us
  Pallas kernels: 18.4 us -> 22 us
    ppermute x49 -> x53, waiting for transfers between devices: 88.9 us -> 67.9 us  [flip(): return lax.ppermute(value, axis, [(i, i ^ bit) for i in range(size)])]
    ppermute x49 -> x53, starting transfers between devices: 34.5 us -> 46.6 us  [flip(): return lax.ppermute(value, axis, [(i, i ^ bit) for i in range(size)])]
    unnamed x26 -> x38, local copies, waits for them, and re-layouts: 0.06 us -> 7.75 us
    convert_element_type x1 -> x0, other arithmetic: 2.99 us -> none  [fast_shards(): jnp.concatenate([act_query, grad_query, act_keyval, grad_keyval], axis=1)]
    pallas_call x1 -> x4, Pallas kernels: 1.59 us -> 3.26 us  [the longest x1 1.63 us: fast_shards(): call(functools.partial(middle_kernel, n), [(n, D)], square[1:], 18, 35000...]
    sub x2 -> x0, other arithmetic: 1.52 us -> none  [the longest x1 0.87 us: fast_shards(): weight_q = weight_query - LEARNING_RATE * moment_q]
  transfers between devices with their start and end apart: 49 -> 53, of which waited for: 21 -> 24; matrix products, arithmetic and copies ran while one was open for 0% -> 0% of each run, Pallas kernels for 7% -> 6%
where the time goes in v2:
time: 146 us
  waiting for transfers between devices  67.9 us (47%)
  starting transfers between devices  46.6 us (32%)
  Pallas kernels  22 us (15%)
  local copies, waits for them, and re-layouts  7.75 us (5%)
    ppermute x53, waiting for transfers between devices, flip(): return lax.ppermute(value, axis, [(i, i ^ bit) for i in range(size)])  67.9 us
    ppermute x53, starting transfers between devices, flip(): return lax.ppermute(value, axis, [(i, i ^ bit) for i in range(size)])  46.6 us
    unnamed x38, local copies, waits for them, and re-layouts  7.75 us
    pallas_call x1, Pallas kernels, fast_shards(): call(functools.partial(keyval_kernel, n, k, width), [(n, D), (k, KV), (n,...  5.19 us
    pallas_call x1, Pallas kernels, fast_shards(): call(functools.partial(gram_kernel, n, k, width, scale), outs, [((D, 2 *...  5.15 us
    pallas_call x1, Pallas kernels, fast_shards(): call(functools.partial(right_kernel, n, width), [(n, D), (n, D), fit], sq...  4.76 us
    pallas_call x1, Pallas kernels, fast_shards(): call(functools.partial(left_kernel, n, width), [(n, D)] * 2, square, 9, 7...  3.61 us
  transfers between devices with their start and end apart: 53, of which 24 were waited for; matrix products, arithmetic and copies ran while one was open for 0% of the time, Pallas kernels for 6%

profile of v2, /device:TPU:0, one launch (start us, length us, event | category | flops | bytes accessed | tf_op | source)
XLA Modules:
  0.0 145.8 jit_solution(11552780263142301208)
XLA Ops:
  7.2 2.3 %collective-permute-done.rows_other = s32[1,128]{1,0:T(1,128)S(1)} collective-permute-done((s32[1,128]{1,0:T(1,128)S(1)}, s32[1,128]{1,0:T(1,128)S(1)}, u32[]{:S(2)}, u32[]{:S(2)}) %collective-permute-start) | collective-permute-done | bytes 544 | tf_op jit(solution)/shard_map/ppermute | solution.py:330
  12.5 5.1 %shard_map.190 = (f32[2,440,128]{2,1,0:T(8,128)S(1)}, f32[2,440,128]{2,1,0:T(8,128)S(1)}, f32[2,440,128]{2,1,0:T(8,128)S(1)}, f32[2,440,128]{2,1,0:T(8,128)S(1)}...) custom-call(s32[2]{0:T(128)S(1)} %pad_add_fusion.pos, ...), custom_call_target="tpu_custom_call" | custom-call | flops 2000000000 | bytes 4000000 | tf_op jit(solution)/shard_map/pallas_call | solution.py:421
  17.7 2.9 %collective-permute-start.2 = (f32[2,440,128]{2,1,0:T(8,128)S(1)}, f32[2,440,128]{2,1,0:T(8,128)S(1)}, u32[]{:S(2)}, u32[]{:S(2)}) collective-permute-start(f32[2,440,128]{2,1,0:T(8,128)S(1)} %get-tuple-element.78), channel_id=1, source_target_pairs={{0,8},{4,12},{8,0},{12,4},{16,24},{20,28},{24,16},{28,20},{1,9},{5... | collective-permute-start | bytes 1351688 | tf_op jit(solution)/shard_map/ppermute | solution.py:330
  22.1 9.1 %collective-permute-done.2 = f32[2,440,128]{2,1,0:T(8,128)S(1)} collective-permute-done((f32[2,440,128]{2,1,0:T(8,128)S(1)}, f32[2,440,128]{2,1,0:T(8,128)S(1)}, u32[]{:S(2)}, u32[]{:S(2)}) %collective-permute-start.2) | collective-permute-done | bytes 450592 | tf_op jit(solution)/shard_map/ppermute | solution.py:330
  34.9 4.3 %collective-permute-done.5 = f32[440,128]{1,0:T(8,128)S(1)} collective-permute-done((f32[440,128]{1,0:T(8,128)S(1)}, f32[440,128]{1,0:T(8,128)S(1)}, u32[]{:S(2)}, u32[]{:S(2)}) %collective-permute-start.5) | collective-permute-done | bytes 225312 | tf_op jit(solution)/shard_map/ppermute | solution.py:330
  44.2 2.6 %collective-permute-start.7 = (f32[440,128]{1,0:T(8,128)S(1)}, f32[440,128]{1,0:T(8,128)S(1)}, u32[]{:S(2)}, u32[]{:S(2)}) collective-permute-start(f32[440,128]{1,0:T(8,128)S(1)} %bitcast_add_fusion.2), channel_id=1, source_target_pairs={{0,2},{1,3},{2,0},{3,1},{4,6},{5,7},{6,4},{7,5},{8,10},{9,11},{10,... | collective-permute-start | bytes 675848 | tf_op jit(solution)/shard_map/ppermute | solution.py:330
  46.8 5.2 %collective-permute-done.6 = f32[440,128]{1,0:T(8,128)S(1)} collective-permute-done((f32[440,128]{1,0:T(8,128)S(1)}, f32[440,128]{1,0:T(8,128)S(1)}, u32[]{:S(2)}, u32[]{:S(2)}) %collective-permute-start.6) | collective-permute-done | bytes 225312 | tf_op jit(solution)/shard_map/ppermute | solution.py:330
  52.0 4.9 %collective-permute-done.7 = f32[440,128]{1,0:T(8,128)S(1)} collective-permute-done((f32[440,128]{1,0:T(8,128)S(1)}, f32[440,128]{1,0:T(8,128)S(1)}, u32[]{:S(2)}, u32[]{:S(2)}) %collective-permute-start.7) | collective-permute-done | bytes 225312 | tf_op jit(solution)/shard_map/ppermute | solution.py:330
  57.2 4.0 %collective-permute-start.11 = (f32[440,128]{1,0:T(8,128)S(1)}, f32[440,128]{1,0:T(8,128)S(1)}, u32[]{:S(2)}, u32[]{:S(2)}) collective-permute-start(f32[440,128]{1,0:T(8,128)S(1)} %add.104), channel_id=1, source_target_pairs={{0,1},{1,0},{2,3},{3,2},{4,5},{5,4},{6,7},{7,6},{8,9},{9,8},{10,11... | collective-permute-start | bytes 675848 | tf_op jit(solution)/shard_map/ppermute | solution.py:330
  61.2 7.1 %collective-permute-done.10 = f32[440,128]{1,0:T(8,128)S(1)} collective-permute-done((f32[440,128]{1,0:T(8,128)S(1)}, f32[440,128]{1,0:T(8,128)S(1)}, u32[]{:S(2)}, u32[]{:S(2)}) %collective-permute-start.10) | collective-permute-done | bytes 225312 | tf_op jit(solution)/shard_map/ppermute | solution.py:330
  68.4 3.4 %collective-permute-done.11 = f32[440,128]{1,0:T(8,128)S(1)} collective-permute-done((f32[440,128]{1,0:T(8,128)S(1)}, f32[440,128]{1,0:T(8,128)S(1)}, u32[]{:S(2)}, u32[]{:S(2)}) %collective-permute-start.11) | collective-permute-done | bytes 225312 | tf_op jit(solution)/shard_map/ppermute | solution.py:330
  71.9 2.6 %collective-permute-start.19 = (f32[480,128]{1,0:T(8,128)S(1)}, f32[480,128]{1,0:T(8,128)S(1)}, u32[]{:S(2)}, u32[]{:S(2)}) collective-permute-start(f32[480,128]{1,0:T(8,128)S(1)} %bitcast_add_fusion), channel_id=1, source_target_pairs={{0,2},{1,3},{2,0},{3,1},{4,6},{5,7},{6,4},{7,5},{8,10},{9,11},{10,... | collective-permute-start | bytes 737288 | tf_op jit(solution)/shard_map/ppermute | solution.py:330
  76.1 2.0 %collective-permute-start.15 = (f32[440,128]{1,0:T(8,128)S(1)}, f32[440,128]{1,0:T(8,128)S(1)}, u32[]{:S(2)}, u32[]{:S(2)}) collective-permute-start(f32[440,128]{1,0:T(8,128)S(1)} %add.105.refs_0_), channel_id=1, source_target_pairs={{0,16},{4,20},{8,24},{12,28},{16,0},{20,4},{24,8},{28,12},{1,17},{... | collective-permute-start | bytes 675848 | tf_op jit(solution)/shard_map/ppermute | solution.py:330
  79.8 2.7 %collective-permute-start.14 = (f32[440,128]{1,0:T(8,128)S(1)}, f32[440,128]{1,0:T(8,128)S(1)}, u32[]{:S(2)}, u32[]{:S(2)}) collective-permute-start(f32[440,128]{1,0:T(8,128)S(1)} %add.105.refs_0_), channel_id=1, source_target_pairs={{0,8},{4,12},{8,0},{12,4},{16,24},{20,28},{24,16},{28,20},{1,9},{5... | collective-permute-start | bytes 675848 | tf_op jit(solution)/shard_map/ppermute | solution.py:330
  82.6 2.7 %collective-permute-done.19 = f32[480,128]{1,0:T(8,128)S(1)} collective-permute-done((f32[480,128]{1,0:T(8,128)S(1)}, f32[480,128]{1,0:T(8,128)S(1)}, u32[]{:S(2)}, u32[]{:S(2)}) %collective-permute-start.19) | collective-permute-done | bytes 245792 | tf_op jit(solution)/shard_map/ppermute | solution.py:330
  87.3 1.9 %collective-permute-start.23 = (f32[480,128]{1,0:T(8,128)S(1)}, f32[480,128]{1,0:T(8,128)S(1)}, u32[]{:S(2)}, u32[]{:S(2)}) collective-permute-start(f32[480,128]{1,0:T(8,128)S(1)} %add.118), channel_id=1, source_target_pairs={{0,1},{1,0},{2,3},{3,2},{4,5},{5,4},{6,7},{7,6},{8,9},{9,8},{10,11... | collective-permute-start | bytes 737288 | tf_op jit(solution)/shard_map/ppermute | solution.py:330
  90.6 5.7 %collective-permute-done.22 = f32[480,128]{1,0:T(8,128)S(1)} collective-permute-done((f32[480,128]{1,0:T(8,128)S(1)}, f32[480,128]{1,0:T(8,128)S(1)}, u32[]{:S(2)}, u32[]{:S(2)}) %collective-permute-start.22) | collective-permute-done | bytes 245792 | tf_op jit(solution)/shard_map/ppermute | solution.py:330
  102.2 3.1 %collective-permute-done.29.refs_2_ = f32[480,128]{1,0:T(8,128)S(1)} collective-permute-done((f32[480,128]{1,0:T(8,128)S(1)}, f32[480,128]{1,0:T(8,128)S(1)}, u32[]{:S(2)}, u32[]{:S(2)}) %collective-permute-start.29) | collective-permute-done | bytes 245792 | tf_op jit(solution)/shard_map/ppermute | solution.py:330
  106.1 4.1 %collective-permute-done.31.refs_9_.refs_1_ = f32[480,128]{1,0:T(8,128)S(1)} collective-permute-done((f32[480,128]{1,0:T(8,128)S(1)}, f32[480,128]{1,0:T(8,128)S(1)}, u32[]{:S(2)}, u32[]{:S(2)}) %collective-permute-start.31) | collective-permute-done | bytes 245792 | tf_op jit(solution)/shard_map/ppermute | solution.py:330
  115.0 4.7 %collective-permute-done.32.refs_3_ = f32[480,128]{1,0:T(8,128)S(1)} collective-permute-done((f32[480,128]{1,0:T(8,128)S(1)}, f32[480,128]{1,0:T(8,128)S(1)}, u32[]{:S(2)}, u32[]{:S(2)}) %collective-permute-start.32) | collective-permute-done | bytes 245792 | tf_op jit(solution)/shard_map/ppermute | solution.py:330
  120.6 3.6 %shard_map.191 = (f32[96,768]{1,0:T(8,128)}, f32[96,768]{1,0:T(8,128)S(1)}) custom-call(s32[2]{0:T(128)S(1)} %pad_add_fusion.pos, f32[440,128]{1,0:T(8,128)S(1)} %add.105.refs_0_, f32[440,128]{1,0:T(8,128)S(1)} %collective-permute-done.14.refs_1_, f32[440,128]{1,0:T(8,128)S(1)} %collective-permute-done.15.refs_2_, ...), custom_call_target="tpu_custom_call" | custom-call | flops 700000000 | bytes 4000000 | tf_op jit(solution)/shard_map/pallas_call | solution.py:436
  124.2 5.2 %shard_map.194 = (f32[96,768]{1,0:T(8,128)}, f32[16,128]{1,0:T(8,128)}, f32[96,128]{1,0:T(8,128)S(1)}, f32[8,128]{1,0:T(8,128)S(1)}) custom-call(s32[2]{0:T(128)S(1)} %pad_add_fusion.pos, f32[440,128]{1,0:T(8,128)S(1)} %add.105.refs_0_, f32[440,128]{1,0:T(8,128)S(1)} %collective-permute-done.14.refs_1_, f32[440,128]{1,0:T(8,128)S(1)} %collective-permute-done.15.refs_2_, ...), custom_call_target="tpu_custom_call" | custom-call | flops 1000000000 | bytes 4000000 | tf_op jit(solution)/shard_map/pallas_call | solution.py:439
  131.1 4.8 %shard_map.193 = (f32[96,768]{1,0:T(8,128)}, f32[96,768]{1,0:T(8,128)S(1)}, f32[8,128]{1,0:T(8,128)S(1)}) custom-call(s32[2]{0:T(128)S(1)} %pad_add_fusion.pos, f32[96,768]{1,0:T(8,128)S(1)} %shard_map.192.t_ref, f32[480,128]{1,0:T(8,128)S(1)} %add.119.refs_0_.main_own, f32[480,128]{1,0:T(8,128)S(1)} %add.120.refs_8_.refs_0_, ...), custom_call_target="tpu_custom_call" | custom-call | flops 1000000000 | bytes 4000000 | tf_op jit(solution)/shard_map/pallas_call | solution.py:449
  135.9 2.1 %collective-permute-start.52 = (f32[8,128]{1,0:T(8,128)S(1)}, f32[8,128]{1,0:T(8,128)S(1)}, u32[]{:S(2)}, u32[]{:S(2)}) collective-permute-start(f32[8,128]{1,0:T(8,128)S(1)} %add.121.fit_own), channel_id=1, source_target_pairs={{0,28},{4,24},{8,20},{12,16},{16,12},{20,8},{24,4},{28,0},{1,29},{... | collective-permute-start | bytes 12296 | tf_op jit(solution)/shard_map/ppermute | solution.py:330
  (146 shorter events, 48.9 us)
Async XLA Ops:
  17.7 13.5 %collective-permute-start.2 = (f32[2,440,128]{2,1,0:T(8,128)S(1)}, f32[2,440,128]{2,1,0:T(8,128)S(1)}, u32[]{:S(2)}, u32[]{:S(2)}) collective-permute-start(f32[2,440,128]{2,1,0:T(8,128)S(1)} %get-tuple-element.78), channel_id=1, source_target_pairs={{0,8},{4,12},{8,0},{12,4},{16,24},{20,28},{24,16},{28,20},{1,9},{5... | collective-permute-start | bytes 1351688 | tf_op jit(solution)/shard_map/ppermute | solution.py:330
  20.6 12.1 %collective-permute-start.3 = (f32[2,440,128]{2,1,0:T(8,128)S(1)}, f32[2,440,128]{2,1,0:T(8,128)S(1)}, u32[]{:S(2)}, u32[]{:S(2)}) collective-permute-start(f32[2,440,128]{2,1,0:T(8,128)S(1)} %get-tuple-element.79), channel_id=1, source_target_pairs={{0,16},{4,20},{8,24},{12,28},{16,0},{20,4},{24,8},{28,12},{1,17},{... | collective-permute-start | bytes 1351688 | tf_op jit(solution)/shard_map/ppermute | solution.py:330
  39.7 17.2 %collective-permute-start.8 = (f32[2,480,128]{2,1,0:T(8,128)S(1)}, f32[2,480,128]{2,1,0:T(8,128)S(1)}, u32[]{:S(2)}, u32[]{:S(2)}) collective-permute-start(f32[2,480,128]{2,1,0:T(8,128)S(1)} %get-tuple-element.87), channel_id=1, source_target_pairs={{0,8},{4,12},{8,0},{12,4},{16,24},{20,28},{24,16},{28,20},{1,9},{5... | collective-permute-start | bytes 1474568 | tf_op jit(solution)/shard_map/ppermute | solution.py:330
  41.1 15.8 %collective-permute-start.9 = (f32[2,480,128]{2,1,0:T(8,128)S(1)}, f32[2,480,128]{2,1,0:T(8,128)S(1)}, u32[]{:S(2)}, u32[]{:S(2)}) collective-permute-start(f32[2,480,128]{2,1,0:T(8,128)S(1)} %copy-done.18), channel_id=1, source_target_pairs={{0,16},{4,20},{8,24},{12,28},{16,0},{20,4},{24,8},{28,12},{1,17},{... | collective-permute-start | bytes 1474568 | tf_op jit(solution)/shard_map/ppermute | solution.py:330
  42.7 9.3 %collective-permute-start.6 = (f32[440,128]{1,0:T(8,128)S(1)}, f32[440,128]{1,0:T(8,128)S(1)}, u32[]{:S(2)}, u32[]{:S(2)}) collective-permute-start(f32[440,128]{1,0:T(8,128)S(1)} %bitcast_add_fusion.3), channel_id=1, source_target_pairs={{0,1},{1,0},{2,3},{3,2},{4,5},{5,4},{6,7},{7,6},{8,9},{9,8},{10,11... | collective-permute-start | bytes 675848 | tf_op jit(solution)/shard_map/ppermute | solution.py:330
  44.2 12.7 %collective-permute-start.7 = (f32[440,128]{1,0:T(8,128)S(1)}, f32[440,128]{1,0:T(8,128)S(1)}, u32[]{:S(2)}, u32[]{:S(2)}) collective-permute-start(f32[440,128]{1,0:T(8,128)S(1)} %bitcast_add_fusion.2), channel_id=1, source_target_pairs={{0,2},{1,3},{2,0},{3,1},{4,6},{5,7},{6,4},{7,5},{8,10},{9,11},{10,... | collective-permute-start | bytes 675848 | tf_op jit(solution)/shard_map/ppermute | solution.py:330
  57.0 14.7 %collective-permute-start.13 = (f32[480,128]{1,0:T(8,128)S(1)}, f32[480,128]{1,0:T(8,128)S(1)}, u32[]{:S(2)}, u32[]{:S(2)}) collective-permute-start(f32[480,128]{1,0:T(8,128)S(1)} %add_bitcast_fusion), channel_id=1, source_target_pairs={{0,8},{4,12},{8,0},{12,4},{16,24},{20,28},{24,16},{28,20},{1,9},{5... | collective-permute-start | bytes 737288 | tf_op jit(solution)/shard_map/ppermute | solution.py:330
  57.1 11.2 %collective-permute-start.10 = (f32[440,128]{1,0:T(8,128)S(1)}, f32[440,128]{1,0:T(8,128)S(1)}, u32[]{:S(2)}, u32[]{:S(2)}) collective-permute-start(f32[440,128]{1,0:T(8,128)S(1)} %add.103), channel_id=1, source_target_pairs={{0,2},{1,3},{2,0},{3,1},{4,6},{5,7},{6,4},{7,5},{8,10},{9,11},{10,... | collective-permute-start | bytes 675848 | tf_op jit(solution)/shard_map/ppermute | solution.py:330
  57.2 14.5 %collective-permute-start.11 = (f32[440,128]{1,0:T(8,128)S(1)}, f32[440,128]{1,0:T(8,128)S(1)}, u32[]{:S(2)}, u32[]{:S(2)}) collective-permute-start(f32[440,128]{1,0:T(8,128)S(1)} %add.104), channel_id=1, source_target_pairs={{0,1},{1,0},{2,3},{3,2},{4,5},{5,4},{6,7},{7,6},{8,9},{9,8},{10,11... | collective-permute-start | bytes 675848 | tf_op jit(solution)/shard_map/ppermute | solution.py:330
  61.2 10.6 %collective-permute-start.12 = (f32[480,128]{1,0:T(8,128)S(1)}, f32[480,128]{1,0:T(8,128)S(1)}, u32[]{:S(2)}, u32[]{:S(2)}) collective-permute-start(f32[480,128]{1,0:T(8,128)S(1)} %add_bitcast_fusion.1), channel_id=1, source_target_pairs={{0,16},{4,20},{8,24},{12,28},{16,0},{20,4},{24,8},{28,12},{1,17},{... | collective-permute-start | bytes 737288 | tf_op jit(solution)/shard_map/ppermute | solution.py:330
  71.9 13.3 %collective-permute-start.19 = (f32[480,128]{1,0:T(8,128)S(1)}, f32[480,128]{1,0:T(8,128)S(1)}, u32[]{:S(2)}, u32[]{:S(2)}) collective-permute-start(f32[480,128]{1,0:T(8,128)S(1)} %bitcast_add_fusion), channel_id=1, source_target_pairs={{0,2},{1,3},{2,0},{3,1},{4,6},{5,7},{6,4},{7,5},{8,10},{9,11},{10,... | collective-permute-start | bytes 737288 | tf_op jit(solution)/shard_map/ppermute | solution.py:330
  74.5 10.8 %collective-permute-start.17 = (f32[440,128]{1,0:T(8,128)S(1)}, f32[440,128]{1,0:T(8,128)S(1)}, u32[]{:S(2)}, u32[]{:S(2)}) collective-permute-start(f32[440,128]{1,0:T(8,128)S(1)} %add.106.refs_8_), channel_id=1, source_target_pairs={{0,8},{4,12},{8,0},{12,4},{16,24},{20,28},{24,16},{28,20},{1,9},{5... | collective-permute-start | bytes 675848 | tf_op jit(solution)/shard_map/ppermute | solution.py:330
  76.1 9.2 %collective-permute-start.16 = (f32[440,128]{1,0:T(8,128)S(1)}, f32[440,128]{1,0:T(8,128)S(1)}, u32[]{:S(2)}, u32[]{:S(2)}) collective-permute-start(f32[440,128]{1,0:T(8,128)S(1)} %add.106.refs_8_), channel_id=1, source_target_pairs={{0,16},{4,20},{8,24},{12,28},{16,0},{20,4},{24,8},{28,12},{1,17},{... | collective-permute-start | bytes 675848 | tf_op jit(solution)/shard_map/ppermute | solution.py:330
  76.1 10.8 %collective-permute-start.15 = (f32[440,128]{1,0:T(8,128)S(1)}, f32[440,128]{1,0:T(8,128)S(1)}, u32[]{:S(2)}, u32[]{:S(2)}) collective-permute-start(f32[440,128]{1,0:T(8,128)S(1)} %add.105.refs_0_), channel_id=1, source_target_pairs={{0,16},{4,20},{8,24},{12,28},{16,0},{20,4},{24,8},{28,12},{1,17},{... | collective-permute-start | bytes 675848 | tf_op jit(solution)/shard_map/ppermute | solution.py:330
  86.9 9.4 %collective-permute-start.22 = (f32[480,128]{1,0:T(8,128)S(1)}, f32[480,128]{1,0:T(8,128)S(1)}, u32[]{:S(2)}, u32[]{:S(2)}) collective-permute-start(f32[480,128]{1,0:T(8,128)S(1)} %add.117), channel_id=1, source_target_pairs={{0,2},{1,3},{2,0},{3,1},{4,6},{5,7},{6,4},{7,5},{8,10},{9,11},{10,... | collective-permute-start | bytes 737288 | tf_op jit(solution)/shard_map/ppermute | solution.py:330
  87.3 9.1 %collective-permute-start.23 = (f32[480,128]{1,0:T(8,128)S(1)}, f32[480,128]{1,0:T(8,128)S(1)}, u32[]{:S(2)}, u32[]{:S(2)}) collective-permute-start(f32[480,128]{1,0:T(8,128)S(1)} %add.118), channel_id=1, source_target_pairs={{0,1},{1,0},{2,3},{3,2},{4,5},{5,4},{6,7},{7,6},{8,9},{9,8},{10,11... | collective-permute-start | bytes 737288 | tf_op jit(solution)/shard_map/ppermute | solution.py:330
  97.2 8.8 %collective-permute-start.28 = (f32[480,128]{1,0:T(8,128)S(1)}, f32[480,128]{1,0:T(8,128)S(1)}, u32[]{:S(2)}, u32[]{:S(2)}) collective-permute-start(f32[480,128]{1,0:T(8,128)S(1)} %add.119.refs_0_.main_own), channel_id=1, source_target_pairs={{0,8},{4,12},{8,0},{12,4},{16,24},{20,28},{24,16},{28,20},{1,9},{5... | collective-permute-start | bytes 737288 | tf_op jit(solution)/shard_map/ppermute | solution.py:330
  98.5 11.7 %collective-permute-start.31 = (f32[480,128]{1,0:T(8,128)S(1)}, f32[480,128]{1,0:T(8,128)S(1)}, u32[]{:S(2)}, u32[]{:S(2)}) collective-permute-start(f32[480,128]{1,0:T(8,128)S(1)} %add.120.refs_8_.refs_0_), channel_id=1, source_target_pairs={{0,8},{4,12},{8,0},{12,4},{16,24},{20,28},{24,16},{28,20},{1,9},{5... | collective-permute-start | bytes 737288 | tf_op jit(solution)/shard_map/ppermute | solution.py:330
  99.3 10.9 %collective-permute-start.30 = (f32[480,128]{1,0:T(8,128)S(1)}, f32[480,128]{1,0:T(8,128)S(1)}, u32[]{:S(2)}, u32[]{:S(2)}) collective-permute-start(f32[480,128]{1,0:T(8,128)S(1)} %add.120.refs_8_.refs_0_), channel_id=1, source_target_pairs={{0,16},{4,20},{8,24},{12,28},{16,0},{20,4},{24,8},{28,12},{1,17},{... | collective-permute-start | bytes 737288 | tf_op jit(solution)/shard_map/ppermute | solution.py:330
  114.4 15.0 %collective-permute-start.35 = (f32[480,128]{1,0:T(8,128)S(1)}, f32[480,128]{1,0:T(8,128)S(1)}, u32[]{:S(2)}, u32[]{:S(2)}) collective-permute-start(f32[480,128]{1,0:T(8,128)S(1)} %collective-permute-done.29.refs_2_), channel_id=1, source_target_pairs={{0,4},{4,0},{8,12},{12,8},{16,20},{20,16},{24,28},{28,24},{1,5},{5... | collective-permute-start | bytes 737288 | tf_op jit(solution)/shard_map/ppermute | solution.py:330
  114.4 15.0 %collective-permute-start.39 = (f32[480,128]{1,0:T(8,128)S(1)}, f32[480,128]{1,0:T(8,128)S(1)}, u32[]{:S(2)}, u32[]{:S(2)}) collective-permute-start(f32[480,128]{1,0:T(8,128)S(1)} %collective-permute-done.31.refs_9_.refs_1_), channel_id=1, source_target_pairs={{0,4},{4,0},{8,12},{12,8},{16,20},{20,16},{24,28},{28,24},{1,5},{5... | collective-permute-start | bytes 737288 | tf_op jit(solution)/shard_map/ppermute | solution.py:330
  114.9 14.5 %collective-permute-start.40 = (f32[480,128]{1,0:T(8,128)S(1)}, f32[480,128]{1,0:T(8,128)S(1)}, u32[]{:S(2)}, u32[]{:S(2)}) collective-permute-start(f32[480,128]{1,0:T(8,128)S(1)} %collective-permute-done.30.refs_10_.refs_2_), channel_id=1, source_target_pairs={{0,4},{4,0},{8,12},{12,8},{16,20},{20,16},{24,28},{28,24},{1,5},{5... | collective-permute-start | bytes 737288 | tf_op jit(solution)/shard_map/ppermute | solution.py:330
  119.7 9.7 %collective-permute-start.36 = (f32[480,128]{1,0:T(8,128)S(1)}, f32[480,128]{1,0:T(8,128)S(1)}, u32[]{:S(2)}, u32[]{:S(2)}) collective-permute-start(f32[480,128]{1,0:T(8,128)S(1)} %collective-permute-done.32.refs_3_), channel_id=1, source_target_pairs={{0,4},{4,0},{8,12},{12,8},{16,20},{20,16},{24,28},{28,24},{1,5},{5... | collective-permute-start | bytes 737288 | tf_op jit(solution)/shard_map/ppermute | solution.py:330
  120.6 8.9 %collective-permute-start.41 = (f32[480,128]{1,0:T(8,128)S(1)}, f32[480,128]{1,0:T(8,128)S(1)}, u32[]{:S(2)}, u32[]{:S(2)}) collective-permute-start(f32[480,128]{1,0:T(8,128)S(1)} %collective-permute-done.37.refs_11_.refs_3_), channel_id=1, source_target_pairs={{0,4},{4,0},{8,12},{12,8},{16,20},{20,16},{24,28},{28,24},{1,5},{5... | collective-permute-start | bytes 737288 | tf_op jit(solution)/shard_map/ppermute | solution.py:330
  (48 other events, 286.1 us)

commit v3 on v0

--- a/solution.py
+++ b/solution.py
@@ -1,6 +1,10 @@
+import functools
+
 import jax
 import jax.numpy as jnp
 from jax import lax
+from jax.experimental import pallas as pl
+from jax.experimental.pallas import tpu as pltpu
 from jax.sharding import PartitionSpec as P
 
 PRECISE = lax.Precision.HIGHEST
@@ -9,6 +13,447 @@
 MOMENTUM = 0.9
 LEARNING_RATE = 0.001
 TRUST_BOUND = 0.5
+LANES = 128
+F32 = jnp.float32
+BF16 = jnp.bfloat16
+VMEM_LIMIT = 28 * 1024 * 1024
+
+
+def rolled(block, shift):
+    return pltpu.roll(block, shift, 1)
+
+
+def window_tiles(block, start, width):
+    extent = block.shape[1]
+    shift = lax.rem(extent - start, extent)
+    turned = rolled(block, shift)
+    return [turned[:, LANES * t:LANES * (t + 1)] for t in range(width // LANES)]
+
+
+def plain_tiles(block):
+    return [block[:, LANES * t:LANES * (t + 1)] for t in range(block.shape[1] // LANES)]
+
+
+def write_tiles(ref, lead, tiles, at=0):
+    for tile in tiles:
+        ref[lead, at:at + tile.shape[0], :] = tile
+        at += tile.shape[0]
+    return at
+
+
+def product(first, second):
+    return lax.dot_general(
+        first, second, (((1,), (0,)), ((), ())), preferred_element_type=F32
+    )
+
+
+def cast_kernel(rows, aq, gq, akv, gkv, out):
+    at, tokens = 0, aq.shape[0]
+    for ref in (aq, gq, akv, gkv):
+        out[:tokens, at:at + ref.shape[1]] = ref[...].astype(F32)
+        at += ref.shape[1]
+    out[tokens:, :] = jnp.zeros((out.shape[0] - tokens, at), F32)
+    out[tokens:tokens + 1, :rows.shape[1]] = rows[...].astype(F32)
+
+
+def picker(all_tokens, tokens, samples):
+    rows = all_tokens[tokens:tokens + 1, :samples].astype(jnp.int32)
+    token = lax.broadcasted_iota(jnp.int32, (tokens, samples), 0)
+    return (token == rows).astype(F32).T.astype(BF16)
+
+
+def turned(values):
+    return values.astype(F32).T.astype(BF16)
+
+
+def own_kernel(tokens, samples, D, mine, y_aq, y_gq, y_akv, y_gkv, u_aq, u_gq, u_akv, u_gkv, t_q, t_kv):
+    pick = picker(mine, tokens, samples)
+    at = 0
+    for y, u in ((y_aq, u_aq), (y_gq, u_gq), (y_akv, u_akv), (y_gkv, u_gkv)):
+        chosen = product(pick, mine[:tokens, at:at + y.shape[1]].astype(BF16))
+        y[...] = chosen.astype(BF16)
+        u[...] = chosen.T.astype(BF16)
+        at += y.shape[1]
+    t_q[...] = turned(mine[:tokens, :D])
+    t_kv[...] = turned(mine[:tokens, 2 * D:3 * D])
+
+
+def roles(q, c):
+    return [2 * chip + c for chip in (q, q ^ (1 + c), q ^ (2 - c), q ^ 3)]
+
+
+def join(u, other, pick, own_u, own_y, lo, hi):
+    samples, tokens = pick.shape
+    chosen = product(pick, other[:tokens, lo:hi].astype(BF16))
+    u[:, :samples] = own_u[...]
+    u[:, samples:] = chosen.T.astype(BF16)
+    return jnp.concatenate([own_y[...], chosen.astype(BF16)], axis=0)
+
+
+def left_blocks(ref, n, blocks):
+    parts = [ref[pl.ds(pl.multiple_of(n * b, 32), n), :] for b in blocks]
+    return jnp.concatenate(parts, axis=0)
+
+
+def four(values, n):
+    return [values[n * r:n * (r + 1)] for r in range(4)]
+
+
+def place(send, keep, tiles, at=0):
+    write_tiles(send, 0, tiles[1], at)
+    write_tiles(send, 1, tiles[3], at)
+    write_tiles(keep, 0, tiles[0], at)
+    return write_tiles(keep, 1, tiles[2], at)
+
+
+def factor_tiles(u, y, state, n, blocks, width, scale):
+    parts = four(product(left_blocks(u, n, blocks), y) * scale, n)
+    parts[0] = parts[0] + (BLEND_RATE / 4.0) * state[...]
+    return [window_tiles(part, n * b, width) for part, b in zip(parts, blocks)]
+
+
+def first_kernel(
+    n, k, width, scale,
+    pos, mine, other, y_aq, y_akv, y_gkv, o_aq, o_akv, o_gkv, o_kv, st_aq, st_akv, st_gkv,
+    send, keep, u_aq, u_akv, u_gkv, t_kv, g_kv,
+):
+    tokens, samples = o_kv.shape[1], o_aq.shape[1]
+    D, KV = y_aq.shape[1], y_gkv.shape[1]
+    blocks = roles(pos[0], pos[1])
+    pick = picker(other, tokens, samples)
+    y = join(u_aq, other, pick, o_aq, y_aq, 0, D)
+    at = place(send, keep, factor_tiles(u_aq, y, st_aq, n, blocks, width, scale))
+    y = join(u_akv, other, pick, o_akv, y_akv, 2 * D, 3 * D)
+    at = place(send, keep, factor_tiles(u_akv, y, st_akv, n, blocks, width, scale), at)
+    t_kv[:, :tokens] = o_kv[...]
+    t_kv[:, tokens:] = turned(other[:tokens, 2 * D:3 * D])
+    ends = [ref[:tokens, 3 * D:].astype(BF16) for ref in (mine, other)]
+    sums = product(left_blocks(t_kv, n, blocks), jnp.concatenate(ends, axis=0))
+    at = place(send, keep, [[part] for part in four(sums, n)], at)
+    y = join(u_gkv, other, pick, o_gkv, y_gkv, 3 * D, 3 * D + KV)
+    g_kv[...] = product(u_gkv[...], y) * scale
+    small = [g_kv[pl.ds(pl.multiple_of(k * b, 8), k), :] for b in blocks]
+    small[0] = small[0] + (BLEND_RATE / 4.0) * st_gkv[...]
+    place(send, keep, [[part] for part in small], at)
+
+
+def second_kernel(
+    n, width, scale,
+    pos, mine, other, y_gq, o_gq, o_q, st_gq, send, keep, u_gq, t_q,
+):
+    tokens, samples = o_q.shape[1], o_gq.shape[1]
+    D = y_gq.shape[1]
+    blocks = roles(pos[0], pos[1])
+    pick = picker(other, tokens, samples)
+    t_q[:, :tokens] = o_q[...]
+    t_q[:, tokens:] = turned(other[:tokens, :D])
+    ends = [ref[:tokens, D:2 * D].astype(BF16) for ref in (mine, other)]
+    sums = four(product(left_blocks(t_q, n, blocks), jnp.concatenate(ends, axis=0)), n)
+    at = place(send, keep, [plain_tiles(part) for part in sums])
+    y = join(u_gq, other, pick, o_gq, y_gq, D, 2 * D)
+    place(send, keep, factor_tiles(u_gq, y, st_gq, n, blocks, width, scale), at)
+
+
+def identity_rows(rows, extent, start):
+    row = lax.broadcasted_iota(jnp.int32, (rows, extent), 0) + start
+    column = lax.broadcasted_iota(jnp.int32, (rows, extent), 1)
+    return row == column
+
+
+def scaled_inverse_terms(matrix):
+    extent = matrix.shape[0]
+    on_diagonal = identity_rows(extent, extent, 0)
+    trace = jnp.sum(jnp.where(on_diagonal, matrix, 0.0))
+    damped = matrix + jnp.where(on_diagonal, DAMPING * trace / extent, 0.0)
+    c = 1.0 / jnp.max(jnp.sum(jnp.abs(damped), axis=1))
+    return c, c * damped
+
+
+def halves(values):
+    high = values.astype(BF16)
+    return high, (values - high.astype(F32)).astype(BF16)
+
+
+def times(values, high, low):
+    v_high, v_low = halves(values)
+    rows = values.shape[0]
+    stacked = product(jnp.concatenate([v_high, v_low], axis=0), high)
+    return stacked[:rows] + stacked[rows:] + product(v_high, low)
+
+
+def pieces_of(stacks, q, c):
+    near, far = (roles(q, parity) for parity in (c, 1 - c))
+    order = [(0, 0, 0), (0, 1, 2), (1, 0, 1), (1, 1, 3)]
+    found = []
+    for stack, blocks in ((stacks[:2], near), (stacks[2:], far)):
+        found += [(stack[which].at[lead], blocks[role]) for which, lead, role in order]
+    return found
+
+
+def assemble(pieces, at, n, width, extent, whole):
+    tiles = width // LANES
+    for piece, b in pieces:
+        parts = [piece[at + n * t:at + n * (t + 1), :] for t in range(tiles)]
+        parts += [jnp.zeros((n, LANES), F32)] * (extent // LANES - tiles)
+        turned = rolled(jnp.concatenate(parts, axis=1), n * b)
+        whole[pl.ds(pl.multiple_of(n * b, 8), n), :] = turned
+    windows = whole[...]
+
+    def block_of(axis):
+        shape = (extent, 1) if axis == 0 else (1, extent)
+        index = lax.broadcasted_iota(jnp.int32, shape, axis)
+        return sum([(index >= n * step).astype(jnp.int32) for step in range(1, 8)])
+
+    apart = jnp.bitwise_and(block_of(1) - block_of(0), 7)
+    matrix = jnp.where(apart <= 4, windows, windows.T)
+    return matrix
+
+
+def own_rows(ref, q, c, n):
+    return ref[pl.ds(pl.multiple_of(n * (2 * q + c), 8), n), :]
+
+
+def parity_rows(ref, c, n):
+    parts = [ref[pl.ds(pl.multiple_of(n * (2 * j + c), 8), n), :] for j in range(4)]
+    return jnp.concatenate(parts, axis=0)
+
+
+def identity_parity(extent, c, n):
+    parts = [identity_rows(n, extent, n * (2 * j + c)) for j in range(4)]
+    return jnp.concatenate(parts, axis=0)
+
+
+def left_rows(c, rows, identity, high, low):
+    first = jnp.where(identity, 2.0, 0.0) - rows
+    second = times(first, high, low)
+    third = 2.0 * second - times(second, high, low)
+    return c * (2.0 * first - third)
+
+
+def right_product(values, c, high, low):
+    first = 2.0 * values - times(values, high, low)
+    second = times(first, high, low)
+    third = 2.0 * second - times(second, high, low)
+    return c * (2.0 * first - third)
+
+
+def left_inverse(matrix, c, n, whole, high_ref, low_ref):
+    factor, scaled = scaled_inverse_terms(matrix)
+    whole[...] = scaled
+    high_ref[...], low_ref[...] = halves(scaled)
+    return left_rows(
+        factor, parity_rows(whole, c, n), identity_parity(whole.shape[0], c, n),
+        high_ref[...], low_ref[...],
+    )
+
+
+def left_kernel(n, width, pos, *refs):
+    stacks, (new_ref, x_ref, whole, high_ref, low_ref) = refs[:4], refs[4:]
+    q, c = pos[0], pos[1]
+    matrix = assemble(pieces_of(stacks, q, c), 0, n, width, whole.shape[0], whole)
+    whole[...] = matrix
+    new_ref[...] = own_rows(whole, q, c, n)
+    x_ref[...] = left_inverse(matrix, c, n, whole, high_ref, low_ref)
+
+
+def query_kernel(n, width, pos, x_ref, *refs):
+    stacks, (new_ref, step_ref, fit_ref) = refs[:4], refs[4:7]
+    whole, high_ref, low_ref, s_ref, s_high, s_low, t_ref = refs[7:]
+    q, c = pos[0], pos[1]
+    extent = whole.shape[0]
+    tiles = extent // LANES
+    pieces = pieces_of(stacks, q, c)
+    for piece, b in pieces:
+        rows = jnp.concatenate([piece[n * t:n * (t + 1), :] for t in range(tiles)], axis=1)
+        at = pl.ds(pl.multiple_of(n * b, 32), n)
+        s_ref[at, :] = rows
+        s_high[at, :], s_low[at, :] = halves(rows)
+    t_ref[...] = times(x_ref[...], s_high[...], s_low[...])
+    matrix = assemble(pieces, n * tiles, n, width, extent, whole)
+    whole[...] = matrix
+    new_ref[...] = own_rows(whole, q, c, n)
+    factor, scaled = scaled_inverse_terms(matrix)
+    high_ref[...], low_ref[...] = halves(scaled)
+    step = right_product(t_ref[...], factor, high_ref[...], low_ref[...])
+    t_ref[...] = step
+    step_ref[...] = t_ref[pl.ds(pl.multiple_of(n * q, 8), n), :]
+    fit_ref[...] = jnp.broadcast_to(jnp.sum(step * parity_rows(s_ref, c, n)), fit_ref.shape)
+
+
+def keyval_kernel(n, k, width, pos, *refs):
+    stacks, (new_left, new_right, step_ref, fit_ref) = refs[:4], refs[4:8]
+    whole, high_ref, low_ref, grad_ref, g_ref, t_ref = refs[8:]
+    q, c = pos[0], pos[1]
+    pieces = pieces_of(stacks, q, c)
+    size = n * (width // LANES)
+    for piece, b in pieces:
+        at = 2 * size
+        grad_ref[pl.ds(pl.multiple_of(n * b, 8), n), :] = piece[at:at + n, :]
+        g_ref[pl.ds(pl.multiple_of(k * b, 8), k), :] = piece[at + n:at + n + k, :]
+    matrix = assemble(pieces, size, n, width, whole.shape[0], whole)
+    whole[...] = matrix
+    new_left[...] = own_rows(whole, q, c, n)
+    new_right[...] = own_rows(g_ref, q, c, k)
+    x_rows = left_inverse(matrix, c, n, whole, high_ref, low_ref)
+    t_rows = times(x_rows, *halves(grad_ref[...]))
+    factor, scaled = scaled_inverse_terms(g_ref[...])
+    step = right_product(t_rows, factor, *halves(scaled))
+    t_ref[...] = step
+    step_ref[...] = t_ref[pl.ds(pl.multiple_of(n * q, 8), n), :]
+    fit_ref[...] = jnp.broadcast_to(jnp.sum(step * parity_rows(grad_ref, c, n)), fit_ref.shape)
+
+
+def update_kernel(fit_own, fit_other, *refs):
+    (step_q, step_kv, weight_q, weight_kv, moment_q, moment_kv) = refs[:6]
+    outs = refs[6:]
+    fitness = (fit_own[...] + fit_other[...])[:1, :1]
+    scale = jnp.sqrt(TRUST_BOUND / (LEARNING_RATE * LEARNING_RATE * fitness))
+    for step, weight, moment, at in (
+        (step_q, weight_q, moment_q, 0), (step_kv, weight_kv, moment_kv, 1)
+    ):
+        fresh = MOMENTUM * moment[...] + scale * step[...]
+        outs[2 + at][...] = fresh
+        outs[at][...] = weight[...] - LEARNING_RATE * fresh
+
+
+def call(kernel, outs, scratch, count, flops=0, scalars=1, kind=F32):
+    vmem = pl.BlockSpec(memory_space=pltpu.VMEM)
+    smem = pl.BlockSpec(memory_space=pltpu.SMEM)
+    return pl.pallas_call(
+        kernel,
+        out_shape=[jax.ShapeDtypeStruct(shape, kind) for shape in outs],
+        in_specs=[smem] * scalars + [vmem] * (count - scalars),
+        out_specs=[vmem] * len(outs),
+        scratch_shapes=[pltpu.VMEM(shape, kind) for shape, kind in scratch],
+        compiler_params=pltpu.CompilerParams(vmem_limit_bytes=VMEM_LIMIT),
+        cost_estimate=pl.CostEstimate(flops=flops, bytes_accessed=4_000_000, transcendentals=0),
+    )
+
+
+def core_flip(value):
+    return lax.ppermute(value, "dp", [(i, i ^ 1) for i in range(8)])
+
+
+def first_hop(value):
+    return lax.ppermute(value, "dp", [(i, i ^ (4 if i & 1 else 2)) for i in range(8)])
+
+
+def second_hop(value):
+    return lax.ppermute(value, "dp", [(i, i ^ (2 if i & 1 else 4)) for i in range(8)])
+
+
+def plane_flip(value, bit):
+    return lax.ppermute(value, "group", [(i, i ^ bit) for i in range(4)])
+
+
+def after(value, *others):
+    return lax.optimization_barrier((value,) + others)[0]
+
+
+def plane_halves(piece):
+    half = piece.shape[0] // 2
+    even = lax.axis_index("group") % 2 == 0
+    low, high = piece[:half], piece[half:]
+    return jnp.where(even, low, high), jnp.where(even, high, low)
+
+
+def plane_whole(mine, theirs):
+    even = lax.axis_index("group") % 2 == 0
+    return jnp.concatenate(
+        [jnp.where(even, mine, theirs), jnp.where(even, theirs, mine)], axis=0
+    )
+
+
+def fast_shards(
+    act_query, grad_query, act_keyval, grad_keyval, sample_rows,
+    state_aq, state_gq, state_akv, state_gkv,
+    weight_query, weight_keyval, moment_query, moment_keyval,
+):
+    D, KV = act_query.shape[1], grad_keyval.shape[1]
+    n, k = state_aq.shape[0], state_gkv.shape[0]
+    tokens, samples = act_query.shape[0], sample_rows.shape[0]
+    width = -(-5 * n // LANES) * LANES
+    d = lax.axis_index("dp")
+    pos = jnp.stack([d // 2, d % 2]).astype(jnp.int32)
+    scale = (1.0 - BLEND_RATE) / (samples * 32)
+
+    (mine,) = call(cast_kernel, [(tokens + 8, 3 * D + KV)], [], 5, scalars=0)(
+        sample_rows.reshape(1, samples), act_query, grad_query, act_keyval, grad_keyval
+    )
+    other = core_flip(mine)
+    y_aq, y_gq, y_akv, y_gkv, u_aq, u_gq, u_akv, u_gkv, t_q, t_kv = call(
+        functools.partial(own_kernel, tokens, samples, D),
+        [(samples, D)] * 3 + [(samples, KV)] + [(D, samples)] * 3 + [(KV, samples)]
+        + [(D, tokens)] * 2,
+        [], 1, 300_000_000, scalars=0, kind=BF16,
+    )(mine)
+
+    r_f = n * (width // LANES)
+    r_a, r_b = 2 * r_f + n + k, n * (D // LANES) + r_f
+    both = (D, 2 * samples)
+    a_send, a_keep = call(
+        functools.partial(first_kernel, n, k, width, scale), [(2, r_a, LANES)] * 2,
+        [(both, BF16)] * 2 + [((KV, 2 * samples), BF16), ((D, 2 * tokens), BF16), ((KV, KV), F32)],
+        13, 700_000_000,
+    )(
+        pos, mine, other, y_aq, y_akv, y_gkv, u_aq, u_akv, u_gkv, t_kv,
+        state_aq, state_akv, state_gkv,
+    )
+    b_send, b_keep = call(
+        functools.partial(second_kernel, n, width, scale), [(2, r_b, LANES)] * 2,
+        [(both, BF16), ((D, 2 * tokens), BF16)], 7, 700_000_000,
+    )(pos, mine, other, y_gq, u_gq, t_q, state_gq)
+
+    a_came = first_hop(a_send)
+    a_own = a_keep[0] + a_came[0] + second_hop(a_keep[1] + a_came[1])
+    b_came = first_hop(after(b_send, a_own))
+    a_mine, a_theirs = plane_halves(a_own)
+    a_mine = a_mine + plane_flip(a_theirs, 1)
+    a_mine = a_mine + plane_flip(a_mine, 2)
+    b_own = b_keep[0] + b_came[0] + second_hop(b_keep[1] + b_came[1])
+    a_own = plane_whole(a_mine, plane_flip(a_mine, 1))
+    b_mine, b_theirs = plane_halves(b_own)
+    a_across = second_hop(after(a_own, b_own))
+    b_mine = b_mine + plane_flip(b_theirs, 1)
+    b_came = plane_flip(b_mine, 2)
+    a_near = jnp.stack([a_own, a_across])
+    a_far = first_hop(a_near)
+    b_mine = b_mine + b_came
+    b_own = plane_whole(b_mine, plane_flip(b_mine, 1))
+    all_a = (a_near, a_far, core_flip(a_near), core_flip(a_far))
+    b_own = after(b_own, *all_a)
+    b_across = second_hop(b_own)
+
+    half = (4 * n, D)
+    square = [((D, D), F32), ((D, D), BF16), ((D, D), BF16)]
+    fit = (8, LANES)
+    new_aq, x_rows = call(
+        functools.partial(left_kernel, n, width), [(n, D), half], square, 5, 2_000_000_000
+    )(pos, *all_a)
+    b_near = after(jnp.stack([b_own, b_across]), x_rows)
+    b_far = first_hop(b_near)
+    b_near_other = core_flip(b_near)
+    new_akv, new_gkv, step_kv, fit_kv = call(
+        functools.partial(keyval_kernel, n, k, width),
+        [(n, D), (k, KV), (n, KV), fit],
+        square + [((D, KV), F32), ((KV, KV), F32), ((4 * n, KV), F32)],
+        5,
+        3_000_000_000,
+    )(pos, *all_a)
+    b_far_other = core_flip(after(b_far, fit_kv))
+    new_gq, step_q, fit_q = call(
+        functools.partial(query_kernel, n, width), [(n, D), (n, D), fit],
+        square + [((D, D), F32), ((D, D), BF16), ((D, D), BF16), (half, F32)], 6, 5_000_000_000,
+    )(pos, x_rows, b_near, b_far, b_near_other, b_far_other)
+
+    part = fit_q + fit_kv
+    weight_q, weight_kv, moment_q, moment_kv = call(
+        update_kernel, [(n, D), (n, KV)] * 2, [], 8, scalars=0
+    )(
+        part, core_flip(part), step_q, step_kv,
+        weight_query, weight_keyval, moment_query, moment_keyval,
+    )
+    return (new_aq, new_gq, new_akv, new_gkv, weight_q, weight_kv, moment_q, moment_kv)
 
 
 def from_root(value, axis, source):
@@ -151,8 +596,9 @@
         P("dp", None),
         P("dp", None),
     )
+    plane = mesh.shape["dp"] == 8 and mesh.shape["group"] == 4
     return jax.shard_map(
-        shards,
+        fast_shards if plane else shards,
         mesh=mesh,
         in_specs=placed,
         out_specs=(

time: 636 us -> 148 us (0.23)
  waiting for transfers between devices: 489 us -> 84.2 us
  matrix products: 50.5 us -> 0 us
  blocking collectives: 39.1 us -> 0 us
  Pallas kernels: 0 us -> 32.4 us
  other arithmetic: 25.8 us -> 0.82 us
  starting transfers between devices: 0.49 us -> 24.8 us
  between operations: 16 us -> 0.82 us
    reduce_scatter x6 -> x0, waiting for transfers between devices: 244 us -> none  [the longest x1 46.2 us: shards(): lax.psum_scatter(local_terms[0], 'dp', scatter_dimension=0, tiled=True)]
    psum x2 -> x0, waiting for transfers between devices: 189 us -> none  [the longest x1 133 us: from_root(): return lax.psum(kept, axis)]
    ppermute x0 -> x20, waiting for transfers between devices: none -> 84.2 us  [the longest x6 36.3 us: plane_flip(): return lax.ppermute(value, 'group', [(i, i ^ bit) for i in range(4)])]
    all_gather x4 -> x0, waiting for transfers between devices: 55.2 us -> none  [the longest x1 30.9 us: shards(): lax.all_gather(rows_q, 'dp', axis=0, tiled=True)]
    dot_general x12 -> x0, matrix products: 50.5 us -> none  [the longest x2 14.7 us: newton(): product = jnp.dot(damped, iterate, precision=PRECISE)]
    pallas_call x0 -> x8, Pallas kernels: none -> 32.4 us  [the longest x1 9.32 us: fast_shards(): call(functools.partial(query_kernel, n, width), [(n, D), (n, D), fit], sq...]
    ppermute x0 -> x20, starting transfers between devices: none -> 24.8 us  [the longest x6 10.4 us: plane_flip(): return lax.ppermute(value, 'group', [(i, i ^ bit) for i in range(4)])]
    psum x1 -> x0, blocking collectives: 20.2 us -> none  [shards(): lax.psum((shares[0], shares[1], shares[2], shares[3], shares[4], shares[5...]
  transfers between devices with their start and end apart: 12 -> 20, of which waited for: 10 -> 15; matrix products, arithmetic and copies ran while one was open for 11% -> 0% of each run, Pallas kernels for 0% -> 13%
where the time goes in v3:
time: 148 us; the launch traced here: 147 us
  waiting for transfers between devices  84.2 us (57%)
  Pallas kernels  32.4 us (22%)
  starting transfers between devices  24.8 us (17%)
  local copies, waits for them, and re-layouts  4.5 us (3%)
    ppermute x6, waiting for transfers between devices, plane_flip(): return lax.ppermute(value, 'group', [(i, i ^ bit) for i in range(4)])  36.3 us
    ppermute x4, waiting for transfers between devices, first_hop(): lax.ppermute(value, 'dp', [(i, i ^ (4 if i & 1 else 2)) for i in range(8)])  24.5 us
    ppermute x4, waiting for transfers between devices, second_hop(): lax.ppermute(value, 'dp', [(i, i ^ (2 if i & 1 else 4)) for i in range(8)])  15.8 us
    ppermute x6, starting transfers between devices, plane_flip(): return lax.ppermute(value, 'group', [(i, i ^ bit) for i in range(4)])  10.4 us
    pallas_call x1, Pallas kernels, fast_shards(): call(functools.partial(query_kernel, n, width), [(n, D), (n, D), fit], sq...  9.32 us
    ppermute x4, starting transfers between devices, first_hop(): lax.ppermute(value, 'dp', [(i, i ^ (4 if i & 1 else 2)) for i in range(8)])  9.13 us
    pallas_call x1, Pallas kernels, fast_shards(): call(functools.partial(keyval_kernel, n, k, width), [(n, D), (k, KV), (n,...  8.11 us
    ppermute x6, waiting for transfers between devices, core_flip(): return lax.ppermute(value, 'dp', [(i, i ^ 1) for i in range(8)])  7.52 us
  transfers between devices with their start and end apart: 20, of which 15 were waited for; matrix products, arithmetic and copies ran while one was open for 0% of the time, Pallas kernels for 13%

profile of v3, /device:TPU:0, one launch (start us, length us, event | category | flops | bytes accessed | tf_op | source)
XLA Modules:
  0.0 147.4 jit_solution(11915534289828315924)
XLA Ops:
  6.5 3.9 %collective-permute-done.other = f32[264,2432]{1,0:T(8,128)} collective-permute-done((f32[264,2432]{1,0:T(8,128)S(1)}, f32[264,2432]{1,0:T(8,128)}, u32[]{:S(2)}, u32[]{:S(2)}) %collective-permute-start) | collective-permute-done | bytes 2568224 | tf_op jit(solution)/shard_map/ppermute | solution.py:334
  10.4 3.3 %shard_map.190 = (f32[2,880,128]{2,1,0:T(8,128)S(1)}, f32[2,880,128]{2,1,0:T(8,128)S(1)}) custom-call(s32[2]{0:T(128)S(1)} %pad_add_fusion.pos, f32[264,2432]{1,0:T(8,128)S(1)} %shard_map.188.mine, f32[264,2432]{1,0:T(8,128)} %collective-permute-done.other, bf16[128,768]{1,0:T(8,128)(2,1)S(1)} %get-tuple-element.40.y_aq, ...), custom_call_target="tpu_custom_call" | custom-call | flops 700000000 | bytes 4000000 | tf_op jit(solution)/shard_map/pallas_call | solution.py:394
  13.8 2.9 %collective-permute-start.1 = (f32[2,880,128]{2,1,0:T(8,128)S(1)}, f32[2,880,128]{2,1,0:T(8,128)S(1)}, u32[]{:S(2)}, u32[]{:S(2)}) collective-permute-start(f32[2,880,128]{2,1,0:T(8,128)S(1)} %get-tuple-element.48), channel_id=1, source_target_pairs={{0,8},{4,20},{8,0},{12,28},{16,24},{20,4},{24,16},{28,12},{1,9},{5... | collective-permute-start | bytes 2703368 | tf_op jit(solution)/shard_map/ppermute | solution.py:338
  16.7 11.2 %collective-permute-done.1 = f32[2,880,128]{2,1,0:T(8,128)S(1)} collective-permute-done((f32[2,880,128]{2,1,0:T(8,128)S(1)}, f32[2,880,128]{2,1,0:T(8,128)S(1)}, u32[]{:S(2)}, u32[]{:S(2)}) %collective-permute-start.1) | collective-permute-done | bytes 901152 | tf_op jit(solution)/shard_map/ppermute | solution.py:338
  28.0 2.1 %collective-permute-start.2 = (f32[880,128]{1,0:T(8,128)S(1)}, f32[880,128]{1,0:T(8,128)S(1)}, u32[]{:S(2)}, u32[]{:S(2)}) collective-permute-start(f32[880,128]{1,0:T(8,128)S(1)} %fusion.3), channel_id=1, source_target_pairs={{0,16},{4,12},{8,24},{12,4},{16,0},{20,28},{24,8},{28,20},{1,17},{... | collective-permute-start | bytes 1351688 | tf_op jit(solution)/shard_map/ppermute | solution.py:342
  30.1 3.9 %shard_map.191 = (f32[2,960,128]{2,1,0:T(8,128)}, f32[2,960,128]{2,1,0:T(8,128)S(1)}) custom-call(s32[2]{0:T(128)S(1)} %pad_add_fusion.pos, f32[264,2432]{1,0:T(8,128)S(1)} %shard_map.188.mine, f32[264,2432]{1,0:T(8,128)} %collective-permute-done.other, bf16[128,768]{1,0:T(8,128)(2,1)S(1)} %get-tuple-element.49.y_gq, ...), custom_call_target="tpu_custom_call" | custom-call | flops 700000000 | bytes 4000000 | tf_op jit(solution)/shard_map/pallas_call | solution.py:402
  34.0 2.4 %collective-permute-done.2 = f32[880,128]{1,0:T(8,128)S(1)} collective-permute-done((f32[880,128]{1,0:T(8,128)S(1)}, f32[880,128]{1,0:T(8,128)S(1)}, u32[]{:S(2)}, u32[]{:S(2)}) %collective-permute-start.2) | collective-permute-done | bytes 450592 | tf_op jit(solution)/shard_map/ppermute | solution.py:342
  40.2 4.4 %collective-permute-done.3 = f32[440,128]{1,0:T(8,128)S(1)} collective-permute-done((f32[440,128]{1,0:T(8,128)S(1)}, f32[440,128]{1,0:T(8,128)S(1)}, u32[]{:S(2)}, u32[]{:S(2)}) %collective-permute-start.3) | collective-permute-done | bytes 225312 | tf_op jit(solution)/shard_map/ppermute | solution.py:346
  44.7 2.7 %collective-permute-start.4 = (f32[440,128]{1,0:T(8,128)S(1)}, f32[440,128]{1,0:T(8,128)S(1)}, u32[]{:S(2)}, u32[]{:S(2)}) collective-permute-start(f32[440,128]{1,0:T(8,128)S(1)} %select_add_fusion.1), channel_id=1, source_target_pairs={{0,2},{1,3},{2,0},{3,1},{4,6},{5,7},{6,4},{7,5},{8,10},{9,11},{10,... | collective-permute-start | bytes 675848 | tf_op jit(solution)/shard_map/ppermute | solution.py:346
  47.4 7.8 %collective-permute-done.4 = f32[440,128]{1,0:T(8,128)S(1)} collective-permute-done((f32[440,128]{1,0:T(8,128)S(1)}, f32[440,128]{1,0:T(8,128)S(1)}, u32[]{:S(2)}, u32[]{:S(2)}) %collective-permute-start.4) | collective-permute-done | bytes 225312 | tf_op jit(solution)/shard_map/ppermute | solution.py:346
  57.1 4.4 %collective-permute-done.5 = f32[440,128]{1,0:T(8,128)S(1)} collective-permute-done((f32[440,128]{1,0:T(8,128)S(1)}, f32[440,128]{1,0:T(8,128)S(1)}, u32[]{:S(2)}, u32[]{:S(2)}) %collective-permute-start.5) | collective-permute-done | bytes 225312 | tf_op jit(solution)/shard_map/ppermute | solution.py:346
  61.7 3.3 %collective-permute-done.7 = f32[960,128]{1,0:T(8,128)S(1)} collective-permute-done((f32[960,128]{1,0:T(8,128)S(1)}, f32[960,128]{1,0:T(8,128)S(1)}, u32[]{:S(2)}, u32[]{:S(2)}) %collective-permute-start.7) | collective-permute-done | bytes 491552 | tf_op jit(solution)/shard_map/ppermute | solution.py:342
  66.1 7.4 %collective-permute-done.8 = f32[880,128]{1,0:T(8,128)S(1)} collective-permute-done((f32[880,128]{1,0:T(8,128)S(1)}, f32[880,128]{1,0:T(8,128)S(1)}, u32[]{:S(2)}, u32[]{:S(2)}) %collective-permute-start.8) | collective-permute-done | bytes 450592 | tf_op jit(solution)/shard_map/ppermute | solution.py:342
  73.5 2.1 %collective-permute-start.9 = (f32[2,880,128]{2,1,0:T(8,128)S(1)}, f32[2,880,128]{2,1,0:T(8,128)S(1)}, u32[]{:S(2)}, u32[]{:S(2)}) collective-permute-start(f32[2,880,128]{2,1,0:T(8,128)S(1)} %pad_maximum_fusion.1.refs_0_), channel_id=1, source_target_pairs={{0,8},{4,20},{8,0},{12,28},{16,24},{20,4},{24,16},{28,12},{1,9},{5... | collective-permute-start | bytes 2703368 | tf_op jit(solution)/shard_map/ppermute | solution.py:338
  77.5 9.3 %collective-permute-done.9.refs_1_ = f32[2,880,128]{2,1,0:T(8,128)S(1)} collective-permute-done((f32[2,880,128]{2,1,0:T(8,128)S(1)}, f32[2,880,128]{2,1,0:T(8,128)S(1)}, u32[]{:S(2)}, u32[]{:S(2)}) %collective-permute-start.9) | collective-permute-done | bytes 901152 | tf_op jit(solution)/shard_map/ppermute | solution.py:338
  86.9 3.4 %collective-permute-start.13 = (f32[480,128]{1,0:T(8,128)S(1)}, f32[480,128]{1,0:T(8,128)S(1)}, u32[]{:S(2)}, u32[]{:S(2)}) collective-permute-start(f32[480,128]{1,0:T(8,128)S(1)} %select_add_fusion), channel_id=1, source_target_pairs={{0,2},{1,3},{2,0},{3,1},{4,6},{5,7},{6,4},{7,5},{8,10},{9,11},{10,... | collective-permute-start | bytes 737288 | tf_op jit(solution)/shard_map/ppermute | solution.py:346
  90.3 11.9 %collective-permute-done.13 = f32[480,128]{1,0:T(8,128)S(1)} collective-permute-done((f32[480,128]{1,0:T(8,128)S(1)}, f32[480,128]{1,0:T(8,128)S(1)}, u32[]{:S(2)}, u32[]{:S(2)}) %collective-permute-start.13) | collective-permute-done | bytes 245792 | tf_op jit(solution)/shard_map/ppermute | solution.py:346
  102.3 7.8 %collective-permute-done.14 = f32[480,128]{1,0:T(8,128)S(1)} collective-permute-done((f32[480,128]{1,0:T(8,128)S(1)}, f32[480,128]{1,0:T(8,128)S(1)}, u32[]{:S(2)}, u32[]{:S(2)}) %collective-permute-start.14) | collective-permute-done | bytes 245792 | tf_op jit(solution)/shard_map/ppermute | solution.py:346
  110.4 6.0 %shard_map.192 = (f32[96,768]{1,0:T(8,128)}, f32[384,768]{1,0:T(8,128)S(1)}) custom-call(s32[2]{0:T(128)S(1)} %pad_add_fusion.pos, f32[2,880,128]{2,1,0:T(8,128)S(1)} %pad_maximum_fusion.1.refs_0_, f32[2,880,128]{2,1,0:T(8,128)S(1)} %collective-permute-done.9.refs_1_, f32[2,880,128]{2,1,0:T(8,128)S(1)} %collective-permute-done.10.refs_2_, ...), custom_call_target="tpu_custom_call" | custom-call | flops 2000000000 | bytes 4000000 | tf_op jit(solution)/shard_map/pallas_call | solution.py:430
  116.3 2.8 %collective-permute-done.15 = f32[960,128]{1,0:T(8,128)S(1)} collective-permute-done((f32[960,128]{1,0:T(8,128)S(1)}, f32[960,128]{1,0:T(8,128)S(1)}, u32[]{:S(2)}, u32[]{:S(2)}) %collective-permute-start.15) | collective-permute-done | bytes 491552 | tf_op jit(solution)/shard_map/ppermute | solution.py:342
  121.2 8.1 %shard_map.193 = (f32[96,768]{1,0:T(8,128)}, f32[16,128]{1,0:T(8,128)}, f32[96,128]{1,0:T(8,128)S(1)}, f32[8,128]{1,0:T(8,128)S(1)}) custom-call(s32[2]{0:T(128)S(1)} %pad_add_fusion.pos, f32[2,880,128]{2,1,0:T(8,128)S(1)} %pad_maximum_fusion.1.refs_0_, f32[2,880,128]{2,1,0:T(8,128)S(1)} %collective-permute-done.9.refs_1_, ...), custom_call_target="tpu_custom_call" | custom-call | flops 3000000000 | bytes 4000000 | tf_op jit(solution)/shard_map/pallas_call | solution.py:436
  129.4 4.0 %collective-permute-done.16.refs_1_ = f32[2,960,128]{2,1,0:T(8,128)S(1)} collective-permute-done((f32[2,960,128]{2,1,0:T(8,128)S(1)}, f32[2,960,128]{2,1,0:T(8,128)S(1)}, u32[]{:S(2)}, u32[]{:S(2)}) %collective-permute-start.16) | collective-permute-done | bytes 983072 | tf_op jit(solution)/shard_map/ppermute | solution.py:338
  133.4 2.5 %collective-permute-done.18.refs_3_ = f32[2,960,128]{2,1,0:T(8,128)S(1)} collective-permute-done((f32[2,960,128]{2,1,0:T(8,128)S(1)}, f32[2,960,128]{2,1,0:T(8,128)S(1)}, u32[]{:S(2)}, u32[]{:S(2)}) %collective-permute-start.18) | collective-permute-done | bytes 983072 | tf_op jit(solution)/shard_map/ppermute | solution.py:334
  136.0 9.3 %shard_map.194 = (f32[96,768]{1,0:T(8,128)}, f32[96,768]{1,0:T(8,128)S(1)}, f32[8,128]{1,0:T(8,128)S(1)}) custom-call(s32[2]{0:T(128)S(1)} %pad_add_fusion.pos, f32[384,768]{1,0:T(8,128)S(1)} %get-tuple-element.57.x_ref, f32[2,960,128]{2,1,0:T(8,128)S(1)} %pad_maximum_fusion.refs_0_, f32[2,960,128]{2,1,0:T(8,128)S(1)} %collective-permute-done.16.refs_1_, ...), custom_call_target="tpu_custom_call" | custom-call | flops 5000000000 | bytes 4000000 | tf_op jit(solution)/shard_map/pallas_call | solution.py:444
  (68 shorter events, 19.5 us)
Async XLA Ops:
  5.3 5.1 %collective-permute-start = (f32[264,2432]{1,0:T(8,128)S(1)}, f32[264,2432]{1,0:T(8,128)}, u32[]{:S(2)}, u32[]{:S(2)}) collective-permute-start(f32[264,2432]{1,0:T(8,128)S(1)} %shard_map.188.mine), channel_id=1, source_target_pairs={{0,4},{4,0},{8,12},{12,8},{16,20},{20,16},{24,28},{28,24},{1,5},{5... | collective-permute-start | bytes 7704584 | tf_op jit(solution)/shard_map/ppermute | solution.py:334
  10.4 19.7 %copy-start.5 = (f32[96,768]{1,0:T(8,128)S(1)}, f32[96,768]{1,0:T(8,128)}, u32[]{:S(2)}) copy-start(f32[96,768]{1,0:T(8,128)} %st_gq.1) | copy-start | bytes 884740
  13.8 14.1 %collective-permute-start.1 = (f32[2,880,128]{2,1,0:T(8,128)S(1)}, f32[2,880,128]{2,1,0:T(8,128)S(1)}, u32[]{:S(2)}, u32[]{:S(2)}) collective-permute-start(f32[2,880,128]{2,1,0:T(8,128)S(1)} %get-tuple-element.48), channel_id=1, source_target_pairs={{0,8},{4,20},{8,0},{12,28},{16,24},{20,4},{24,16},{28,12},{1,9},{5... | collective-permute-start | bytes 2703368 | tf_op jit(solution)/shard_map/ppermute | solution.py:338
  28.0 8.5 %collective-permute-start.2 = (f32[880,128]{1,0:T(8,128)S(1)}, f32[880,128]{1,0:T(8,128)S(1)}, u32[]{:S(2)}, u32[]{:S(2)}) collective-permute-start(f32[880,128]{1,0:T(8,128)S(1)} %fusion.3), channel_id=1, source_target_pairs={{0,16},{4,12},{8,24},{12,4},{16,0},{20,28},{24,8},{28,20},{1,17},{... | collective-permute-start | bytes 1351688 | tf_op jit(solution)/shard_map/ppermute | solution.py:342
  36.5 19.5 %collective-permute-start.6 = (f32[2,960,128]{2,1,0:T(8,128)}, f32[2,960,128]{2,1,0:T(8,128)S(1)}, u32[]{:S(2)}, u32[]{:S(2)}) collective-permute-start(f32[2,960,128]{2,1,0:T(8,128)} %get-tuple-element.54), channel_id=1, source_target_pairs={{0,8},{4,20},{8,0},{12,28},{16,24},{20,4},{24,16},{28,12},{1,9},{5... | collective-permute-start | bytes 2949128 | tf_op jit(solution)/shard_map/ppermute | solution.py:338
  38.6 6.0 %collective-permute-start.3 = (f32[440,128]{1,0:T(8,128)S(1)}, f32[440,128]{1,0:T(8,128)S(1)}, u32[]{:S(2)}, u32[]{:S(2)}) collective-permute-start(f32[440,128]{1,0:T(8,128)S(1)} %slice_select_fusion.1), channel_id=1, source_target_pairs={{0,1},{1,0},{2,3},{3,2},{4,5},{5,4},{6,7},{7,6},{8,9},{9,8},{10,11... | collective-permute-start | bytes 675848 | tf_op jit(solution)/shard_map/ppermute | solution.py:346
  44.7 10.5 %collective-permute-start.4 = (f32[440,128]{1,0:T(8,128)S(1)}, f32[440,128]{1,0:T(8,128)S(1)}, u32[]{:S(2)}, u32[]{:S(2)}) collective-permute-start(f32[440,128]{1,0:T(8,128)S(1)} %select_add_fusion.1), channel_id=1, source_target_pairs={{0,2},{1,3},{2,0},{3,1},{4,6},{5,7},{6,4},{7,5},{8,10},{9,11},{10,... | collective-permute-start | bytes 675848 | tf_op jit(solution)/shard_map/ppermute | solution.py:346
  55.2 6.3 %collective-permute-start.5 = (f32[440,128]{1,0:T(8,128)S(1)}, f32[440,128]{1,0:T(8,128)S(1)}, u32[]{:S(2)}, u32[]{:S(2)}) collective-permute-start(f32[440,128]{1,0:T(8,128)S(1)} %add.64), channel_id=1, source_target_pairs={{0,1},{1,0},{2,3},{3,2},{4,5},{5,4},{6,7},{7,6},{8,9},{9,8},{10,11... | collective-permute-start | bytes 675848 | tf_op jit(solution)/shard_map/ppermute | solution.py:346
  56.0 8.9 %collective-permute-start.7 = (f32[960,128]{1,0:T(8,128)S(1)}, f32[960,128]{1,0:T(8,128)S(1)}, u32[]{:S(2)}, u32[]{:S(2)}) collective-permute-start(f32[960,128]{1,0:T(8,128)S(1)} %fusion), channel_id=1, source_target_pairs={{0,16},{4,12},{8,24},{12,4},{16,0},{20,28},{24,8},{28,20},{1,17},{... | collective-permute-start | bytes 1474568 | tf_op jit(solution)/shard_map/ppermute | solution.py:342
  65.0 8.5 %collective-permute-start.8 = (f32[880,128]{1,0:T(8,128)S(1)}, f32[880,128]{1,0:T(8,128)S(1)}, u32[]{:S(2)}, u32[]{:S(2)}) collective-permute-start(f32[880,128]{1,0:T(8,128)S(1)} %get-tuple-element.55), channel_id=1, source_target_pairs={{0,16},{4,12},{8,24},{12,4},{16,0},{20,28},{24,8},{28,20},{1,17},{... | collective-permute-start | bytes 1351688 | tf_op jit(solution)/shard_map/ppermute | solution.py:342
  73.5 13.3 %collective-permute-start.9 = (f32[2,880,128]{2,1,0:T(8,128)S(1)}, f32[2,880,128]{2,1,0:T(8,128)S(1)}, u32[]{:S(2)}, u32[]{:S(2)}) collective-permute-start(f32[2,880,128]{2,1,0:T(8,128)S(1)} %pad_maximum_fusion.1.refs_0_), channel_id=1, source_target_pairs={{0,8},{4,20},{8,0},{12,28},{16,24},{20,4},{24,16},{28,12},{1,9},{5... | collective-permute-start | bytes 2703368 | tf_op jit(solution)/shard_map/ppermute | solution.py:338
  75.7 11.2 %collective-permute-start.12 = (f32[480,128]{1,0:T(8,128)S(1)}, f32[480,128]{1,0:T(8,128)S(1)}, u32[]{:S(2)}, u32[]{:S(2)}) collective-permute-start(f32[480,128]{1,0:T(8,128)S(1)} %slice_select_fusion), channel_id=1, source_target_pairs={{0,1},{1,0},{2,3},{3,2},{4,5},{5,4},{6,7},{7,6},{8,9},{9,8},{10,11... | collective-permute-start | bytes 737288 | tf_op jit(solution)/shard_map/ppermute | solution.py:346
  77.5 32.7 %collective-permute-start.10 = (f32[2,880,128]{2,1,0:T(8,128)S(1)}, f32[2,880,128]{2,1,0:T(8,128)S(1)}, u32[]{:S(2)}, u32[]{:S(2)}) collective-permute-start(f32[2,880,128]{2,1,0:T(8,128)S(1)} %pad_maximum_fusion.1.refs_0_), channel_id=1, source_target_pairs={{0,4},{4,0},{8,12},{12,8},{16,20},{20,16},{24,28},{28,24},{1,5},{5... | collective-permute-start | bytes 2703368 | tf_op jit(solution)/shard_map/ppermute | solution.py:334
  86.8 23.4 %collective-permute-start.11 = (f32[2,880,128]{2,1,0:T(8,128)S(1)}, f32[2,880,128]{2,1,0:T(8,128)S(1)}, u32[]{:S(2)}, u32[]{:S(2)}) collective-permute-start(f32[2,880,128]{2,1,0:T(8,128)S(1)} %collective-permute-done.9.refs_1_), channel_id=1, source_target_pairs={{0,4},{4,0},{8,12},{12,8},{16,20},{20,16},{24,28},{28,24},{1,5},{5... | collective-permute-start | bytes 2703368 | tf_op jit(solution)/shard_map/ppermute | solution.py:334
  86.9 15.3 %collective-permute-start.13 = (f32[480,128]{1,0:T(8,128)S(1)}, f32[480,128]{1,0:T(8,128)S(1)}, u32[]{:S(2)}, u32[]{:S(2)}) collective-permute-start(f32[480,128]{1,0:T(8,128)S(1)} %select_add_fusion), channel_id=1, source_target_pairs={{0,2},{1,3},{2,0},{3,1},{4,6},{5,7},{6,4},{7,5},{8,10},{9,11},{10,... | collective-permute-start | bytes 737288 | tf_op jit(solution)/shard_map/ppermute | solution.py:346
  102.2 7.9 %collective-permute-start.14 = (f32[480,128]{1,0:T(8,128)S(1)}, f32[480,128]{1,0:T(8,128)S(1)}, u32[]{:S(2)}, u32[]{:S(2)}) collective-permute-start(f32[480,128]{1,0:T(8,128)S(1)} %add.71), channel_id=1, source_target_pairs={{0,1},{1,0},{2,3},{3,2},{4,5},{5,4},{6,7},{7,6},{8,9},{9,8},{10,11... | collective-permute-start | bytes 737288 | tf_op jit(solution)/shard_map/ppermute | solution.py:346
  110.2 8.9 %collective-permute-start.15 = (f32[960,128]{1,0:T(8,128)S(1)}, f32[960,128]{1,0:T(8,128)S(1)}, u32[]{:S(2)}, u32[]{:S(2)}) collective-permute-start(f32[960,128]{1,0:T(8,128)S(1)} %pad_maximum_fusion.2), channel_id=1, source_target_pairs={{0,16},{4,12},{8,24},{12,4},{16,0},{20,28},{24,8},{28,20},{1,17},{... | collective-permute-start | bytes 1474568 | tf_op jit(solution)/shard_map/ppermute | solution.py:342
  119.2 14.2 %collective-permute-start.16 = (f32[2,960,128]{2,1,0:T(8,128)S(1)}, f32[2,960,128]{2,1,0:T(8,128)S(1)}, u32[]{:S(2)}, u32[]{:S(2)}) collective-permute-start(f32[2,960,128]{2,1,0:T(8,128)S(1)} %pad_maximum_fusion.refs_0_), channel_id=1, source_target_pairs={{0,8},{4,20},{8,0},{12,28},{16,24},{20,4},{24,16},{28,12},{1,9},{5... | collective-permute-start | bytes 2949128 | tf_op jit(solution)/shard_map/ppermute | solution.py:338
  129.4 4.1 %collective-permute-start.17 = (f32[2,960,128]{2,1,0:T(8,128)S(1)}, f32[2,960,128]{2,1,0:T(8,128)S(1)}, u32[]{:S(2)}, u32[]{:S(2)}) collective-permute-start(f32[2,960,128]{2,1,0:T(8,128)S(1)} %pad_maximum_fusion.refs_0_), channel_id=1, source_target_pairs={{0,4},{4,0},{8,12},{12,8},{16,20},{20,16},{24,28},{28,24},{1,5},{5... | collective-permute-start | bytes 2949128 | tf_op jit(solution)/shard_map/ppermute | solution.py:334
  133.3 13.1 %copy-start.7 = (f32[96,768]{1,0:T(8,128)S(1)}, f32[96,768]{1,0:T(8,128)}, u32[]{:S(2)}) copy-start(f32[96,768]{1,0:T(8,128)} %refs_4_.1) | copy-start | bytes 884740
  133.3 13.1 %copy-start.9 = (f32[96,128]{1,0:T(8,128)S(1)}, f32[96,128]{1,0:T(8,128)}, u32[]{:S(2)}) copy-start(f32[96,128]{1,0:T(8,128)} %refs_3_.1) | copy-start | bytes 147460
  133.3 13.1 %copy-start.10 = (f32[96,128]{1,0:T(8,128)S(1)}, f32[96,128]{1,0:T(8,128)}, u32[]{:S(2)}) copy-start(f32[96,128]{1,0:T(8,128)} %refs_5_.1) | copy-start | bytes 147460
  133.3 2.6 %collective-permute-start.18 = (f32[2,960,128]{2,1,0:T(8,128)S(1)}, f32[2,960,128]{2,1,0:T(8,128)S(1)}, u32[]{:S(2)}, u32[]{:S(2)}) collective-permute-start(f32[2,960,128]{2,1,0:T(8,128)S(1)} %collective-permute-done.16.refs_1_), channel_id=1, source_target_pairs={{0,4},{4,0},{8,12},{12,8},{16,20},{20,16},{24,28},{28,24},{1,5},{5... | collective-permute-start | bytes 2949128 | tf_op jit(solution)/shard_map/ppermute | solution.py:334
  145.3 1.2 collective-permute-start.19
  (9 other events, 33.5 us)

commit v4 on v3

--- a/solution.py
+++ b/solution.py
@@ -112,19 +112,34 @@
     return [window_tiles(part, n * b, width) for part, b in zip(parts, blocks)]
 
 
-def first_kernel(
+def factor_kernel(n, width, scale, lo, pos, other, y, o, state, send, keep, u):
+    D, samples = y.shape[1], y.shape[0]
+    tokens = other.shape[0] - 8
+    blocks = roles(pos[0], pos[1])
+    chosen = join(u, other, picker(other, tokens, samples), o, y, lo, lo + D)
+    place(send, keep, factor_tiles(u, chosen, state, n, blocks, width, scale))
+
+
+def gradient_kernel(n, pos, mine, other, o_q, send, keep, t_q):
+    D, tokens = o_q.shape
+    t_q[:, :tokens] = o_q[...]
+    t_q[:, tokens:] = turned(other[:tokens, :D])
+    ends = [ref[:tokens, D:2 * D].astype(BF16) for ref in (mine, other)]
+    sums = product(left_blocks(t_q, n, roles(pos[0], pos[1])), jnp.concatenate(ends, axis=0))
+    place(send, keep, [plain_tiles(part) for part in four(sums, n)])
+
+
+def keyval_sums_kernel(
     n, k, width, scale,
-    pos, mine, other, y_aq, y_akv, y_gkv, o_aq, o_akv, o_gkv, o_kv, st_aq, st_akv, st_gkv,
-    send, keep, u_aq, u_akv, u_gkv, t_kv, g_kv,
+    pos, mine, other, y_akv, y_gkv, o_akv, o_gkv, o_kv, st_akv, st_gkv,
+    send, keep, u_akv, u_gkv, t_kv, g_kv,
 ):
-    tokens, samples = o_kv.shape[1], o_aq.shape[1]
-    D, KV = y_aq.shape[1], y_gkv.shape[1]
+    tokens, samples = o_kv.shape[1], o_akv.shape[1]
+    D, KV = y_akv.shape[1], y_gkv.shape[1]
     blocks = roles(pos[0], pos[1])
     pick = picker(other, tokens, samples)
-    y = join(u_aq, other, pick, o_aq, y_aq, 0, D)
-    at = place(send, keep, factor_tiles(u_aq, y, st_aq, n, blocks, width, scale))
     y = join(u_akv, other, pick, o_akv, y_akv, 2 * D, 3 * D)
-    at = place(send, keep, factor_tiles(u_akv, y, st_akv, n, blocks, width, scale), at)
+    at = place(send, keep, factor_tiles(u_akv, y, st_akv, n, blocks, width, scale))
     t_kv[:, :tokens] = o_kv[...]
     t_kv[:, tokens:] = turned(other[:tokens, 2 * D:3 * D])
     ends = [ref[:tokens, 3 * D:].astype(BF16) for ref in (mine, other)]
@@ -137,23 +152,6 @@
     place(send, keep, [[part] for part in small], at)
 
 
-def second_kernel(
-    n, width, scale,
-    pos, mine, other, y_gq, o_gq, o_q, st_gq, send, keep, u_gq, t_q,
-):
-    tokens, samples = o_q.shape[1], o_gq.shape[1]
-    D = y_gq.shape[1]
-    blocks = roles(pos[0], pos[1])
-    pick = picker(other, tokens, samples)
-    t_q[:, :tokens] = o_q[...]
-    t_q[:, tokens:] = turned(other[:tokens, :D])
-    ends = [ref[:tokens, D:2 * D].astype(BF16) for ref in (mine, other)]
-    sums = four(product(left_blocks(t_q, n, blocks), jnp.concatenate(ends, axis=0)), n)
-    at = place(send, keep, [plain_tiles(part) for part in sums])
-    y = join(u_gq, other, pick, o_gq, y_gq, D, 2 * D)
-    place(send, keep, factor_tiles(u_gq, y, st_gq, n, blocks, width, scale), at)
-
-
 def identity_rows(rows, extent, start):
     row = lax.broadcasted_iota(jnp.int32, (rows, extent), 0) + start
     column = lax.broadcasted_iota(jnp.int32, (rows, extent), 1)
@@ -256,28 +254,31 @@
     x_ref[...] = left_inverse(matrix, c, n, whole, high_ref, low_ref)
 
 
-def query_kernel(n, width, pos, x_ref, *refs):
-    stacks, (new_ref, step_ref, fit_ref) = refs[:4], refs[4:7]
-    whole, high_ref, low_ref, s_ref, s_high, s_low, t_ref = refs[7:]
+def middle_kernel(n, pos, x_ref, *refs):
+    stacks, (t_ref, rows_ref, s_ref, s_high, s_low) = refs[:4], refs[4:]
     q, c = pos[0], pos[1]
-    extent = whole.shape[0]
-    tiles = extent // LANES
-    pieces = pieces_of(stacks, q, c)
-    for piece, b in pieces:
+    tiles = s_ref.shape[1] // LANES
+    for piece, b in pieces_of(stacks, q, c):
         rows = jnp.concatenate([piece[n * t:n * (t + 1), :] for t in range(tiles)], axis=1)
         at = pl.ds(pl.multiple_of(n * b, 32), n)
         s_ref[at, :] = rows
         s_high[at, :], s_low[at, :] = halves(rows)
     t_ref[...] = times(x_ref[...], s_high[...], s_low[...])
-    matrix = assemble(pieces, n * tiles, n, width, extent, whole)
+    rows_ref[...] = parity_rows(s_ref, c, n)
+
+
+def right_kernel(n, width, pos, t_ref, rows_ref, *refs):
+    stacks, (new_ref, step_ref, fit_ref, whole, high_ref, low_ref, step_all) = refs[:4], refs[4:]
+    q, c = pos[0], pos[1]
+    matrix = assemble(pieces_of(stacks, q, c), 0, n, width, whole.shape[0], whole)
     whole[...] = matrix
     new_ref[...] = own_rows(whole, q, c, n)
     factor, scaled = scaled_inverse_terms(matrix)
     high_ref[...], low_ref[...] = halves(scaled)
     step = right_product(t_ref[...], factor, high_ref[...], low_ref[...])
-    t_ref[...] = step
-    step_ref[...] = t_ref[pl.ds(pl.multiple_of(n * q, 8), n), :]
-    fit_ref[...] = jnp.broadcast_to(jnp.sum(step * parity_rows(s_ref, c, n)), fit_ref.shape)
+    step_all[...] = step
+    step_ref[...] = step_all[pl.ds(pl.multiple_of(n * q, 8), n), :]
+    fit_ref[...] = jnp.broadcast_to(jnp.sum(step * rows_ref[...]), fit_ref.shape)
 
 
 def keyval_kernel(n, k, width, pos, *refs):
@@ -285,12 +286,11 @@
     whole, high_ref, low_ref, grad_ref, g_ref, t_ref = refs[8:]
     q, c = pos[0], pos[1]
     pieces = pieces_of(stacks, q, c)
-    size = n * (width // LANES)
+    at = n * (width // LANES)
     for piece, b in pieces:
-        at = 2 * size
         grad_ref[pl.ds(pl.multiple_of(n * b, 8), n), :] = piece[at:at + n, :]
         g_ref[pl.ds(pl.multiple_of(k * b, 8), k), :] = piece[at + n:at + n + k, :]
-    matrix = assemble(pieces, size, n, width, whole.shape[0], whole)
+    matrix = assemble(pieces, 0, n, width, whole.shape[0], whole)
     whole[...] = matrix
     new_left[...] = own_rows(whole, q, c, n)
     new_right[...] = own_rows(g_ref, q, c, k)
@@ -362,6 +362,77 @@
     return jnp.concatenate(
         [jnp.where(even, mine, theirs), jnp.where(even, theirs, mine)], axis=0
     )
+
+
+ORDER = (
+    "+Ars1", "+Krs1", "+Srs1", "-Ars1", "+Ars2", "-Krs1", "+Krs2", "-Ars2", "+Az1", "-Srs1",
+    "+Srs2", "+Grs1", "-Krs2", "+Kz1", "-Az1", "+Az2", "-Srs2", "+Sz1", "-Kz1", "+Kz2", "-Grs1",
+    "+Grs2", "-Az2", "+Az3", "-Sz1", "+Sz2", "-Grs2", "+Gz1", "-Az3", "+Aag1", "-Kz2", "+Kz3",
+    "-Gz1", "+Gz2", "-Aag1", "+Acn", "+Aag2", "-Sz2", "+Sz3", "-Kz3", "-Acn", "+Kag1", "-Gz2",
+    "+Gz3", "-Sz3", "+Sag1", "-Aag2", "+Acf", "-Kag1", "+Kcn", "+Kag2", "-Gz3", "-Acf", "+Gag1",
+    "-Kcn", "kA", "-Sag1", "-Gag1", "+Scn", "+Sag2", "-Kag2", "+Kcf", "-Scn", "+Gcn", "+Gag2",
+    "-Kcf", "kK", "-Gcn", "-Sag2", "+Scf", "-Gag2", "+Gcf", "-Scf", "kT", "-Gcf", "kG",
+)
+
+
+class Transfers:
+    def __init__(self, sends, keeps):
+        self.got = {}
+        self.flying = {}
+        self.sends, self.keeps = sends, keeps
+        self.token = None
+
+    def operand(self, chunk, step):
+        got = self.got
+        if step == "rs1":
+            return self.sends[chunk]
+        if step == "rs2":
+            return self.keeps[chunk][1] + got[chunk, "rs1"][1]
+        if step == "z1":
+            own = self.keeps[chunk][0] + got[chunk, "rs1"][0] + got[chunk, "rs2"]
+            got[chunk, "half"], theirs = plane_halves(own)
+            return theirs
+        if step == "z2":
+            got[chunk, "half"] = got[chunk, "half"] + got[chunk, "z1"]
+            return got[chunk, "half"]
+        if step == "z3":
+            got[chunk, "half"] = got[chunk, "half"] + got[chunk, "z2"]
+            return got[chunk, "half"]
+        if step == "ag1":
+            got[chunk, "own"] = plane_whole(got[chunk, "half"], got[chunk, "z3"])
+            return got[chunk, "own"]
+        if step == "ag2":
+            got[chunk, "near"] = jnp.stack([got[chunk, "own"], got[chunk, "ag1"]])
+            return got[chunk, "near"]
+        if step == "cn":
+            if (chunk, "near") not in got:
+                got[chunk, "near"] = jnp.stack([got[chunk, "own"], got[chunk, "ag1"]])
+            return got[chunk, "near"]
+        return got[chunk, "ag2"]
+
+    hops = {
+        "rs1": first_hop, "rs2": second_hop, "ag1": second_hop, "ag2": first_hop,
+        "z1": lambda value: plane_flip(value, 1), "z2": lambda value: plane_flip(value, 2),
+        "z3": lambda value: plane_flip(value, 1), "cn": core_flip, "cf": core_flip,
+    }
+
+    def start(self, chunk, step):
+        value = self.operand(chunk, step)
+        if self.token is not None:
+            value = after(value, self.token)
+        self.flying[chunk, step] = self.hops[step](value)
+
+    def passed(self, value):
+        if self.token is not None:
+            value, _ = lax.optimization_barrier((value, self.token))
+        self.token = value
+        return value
+
+    def wait(self, chunk, step):
+        self.got[chunk, step] = self.passed(self.flying.pop((chunk, step)))
+
+    def stacks(self, chunk):
+        return [self.got[chunk, step] for step in ("near", "ag2", "cn", "cf")]
 
 
 def fast_shards(
@@ -389,62 +460,58 @@
     )(mine)
 
     r_f = n * (width // LANES)
-    r_a, r_b = 2 * r_f + n + k, n * (D // LANES) + r_f
-    both = (D, 2 * samples)
-    a_send, a_keep = call(
-        functools.partial(first_kernel, n, k, width, scale), [(2, r_a, LANES)] * 2,
-        [(both, BF16)] * 2 + [((KV, 2 * samples), BF16), ((D, 2 * tokens), BF16), ((KV, KV), F32)],
-        13, 700_000_000,
-    )(
-        pos, mine, other, y_aq, y_akv, y_gkv, u_aq, u_akv, u_gkv, t_kv,
-        state_aq, state_akv, state_gkv,
-    )
-    b_send, b_keep = call(
-        functools.partial(second_kernel, n, width, scale), [(2, r_b, LANES)] * 2,
-        [(both, BF16), ((D, 2 * tokens), BF16)], 7, 700_000_000,
-    )(pos, mine, other, y_gq, u_gq, t_q, state_gq)
-
-    a_came = first_hop(a_send)
-    a_own = a_keep[0] + a_came[0] + second_hop(a_keep[1] + a_came[1])
-    b_came = first_hop(after(b_send, a_own))
-    a_mine, a_theirs = plane_halves(a_own)
-    a_mine = a_mine + plane_flip(a_theirs, 1)
-    a_mine = a_mine + plane_flip(a_mine, 2)
-    b_own = b_keep[0] + b_came[0] + second_hop(b_keep[1] + b_came[1])
-    a_own = plane_whole(a_mine, plane_flip(a_mine, 1))
-    b_mine, b_theirs = plane_halves(b_own)
-    a_across = second_hop(after(a_own, b_own))
-    b_mine = b_mine + plane_flip(b_theirs, 1)
-    b_came = plane_flip(b_mine, 2)
-    a_near = jnp.stack([a_own, a_across])
-    a_far = first_hop(a_near)
-    b_mine = b_mine + b_came
-    b_own = plane_whole(b_mine, plane_flip(b_mine, 1))
-    all_a = (a_near, a_far, core_flip(a_near), core_flip(a_far))
-    b_own = after(b_own, *all_a)
-    b_across = second_hop(b_own)
-
-    half = (4 * n, D)
+    both, all_tokens = ((D, 2 * samples), BF16), ((D, 2 * tokens), BF16)
+    sends, keeps = {}, {}
+    sends["A"], keeps["A"] = call(
+        functools.partial(factor_kernel, n, width, scale, 0), [(2, r_f, LANES)] * 2,
+        [both], 5, 300_000_000,
+    )(pos, other, y_aq, u_aq, state_aq)
+    sends["K"], keeps["K"] = call(
+        functools.partial(keyval_sums_kernel, n, k, width, scale),
+        [(2, r_f + n + k, LANES)] * 2,
+        [both, ((KV, 2 * samples), BF16), all_tokens, ((KV, KV), F32)], 10, 400_000_000,
+    )(pos, mine, other, y_akv, y_gkv, u_akv, u_gkv, t_kv, state_akv, state_gkv)
+    sends["S"], keeps["S"] = call(
+        functools.partial(gradient_kernel, n), [(2, n * (D // LANES), LANES)] * 2,
+        [all_tokens], 4, 500_000_000,
+    )(pos, mine, other, t_q)
+    sends["G"], keeps["G"] = call(
+        functools.partial(factor_kernel, n, width, scale, D), [(2, r_f, LANES)] * 2,
+        [both], 5, 300_000_000,
+    )(pos, other, y_gq, u_gq, state_gq)
+
+    rows = (4 * n, D)
     square = [((D, D), F32), ((D, D), BF16), ((D, D), BF16)]
     fit = (8, LANES)
-    new_aq, x_rows = call(
-        functools.partial(left_kernel, n, width), [(n, D), half], square, 5, 2_000_000_000
-    )(pos, *all_a)
-    b_near = after(jnp.stack([b_own, b_across]), x_rows)
-    b_far = first_hop(b_near)
-    b_near_other = core_flip(b_near)
-    new_akv, new_gkv, step_kv, fit_kv = call(
-        functools.partial(keyval_kernel, n, k, width),
-        [(n, D), (k, KV), (n, KV), fit],
-        square + [((D, KV), F32), ((KV, KV), F32), ((4 * n, KV), F32)],
-        5,
-        3_000_000_000,
-    )(pos, *all_a)
-    b_far_other = core_flip(after(b_far, fit_kv))
-    new_gq, step_q, fit_q = call(
-        functools.partial(query_kernel, n, width), [(n, D), (n, D), fit],
-        square + [((D, D), F32), ((D, D), BF16), ((D, D), BF16), (half, F32)], 6, 5_000_000_000,
-    )(pos, x_rows, b_near, b_far, b_near_other, b_far_other)
+    moves = Transfers(sends, keeps)
+    for item in ORDER:
+        if item[0] == "+":
+            moves.start(item[1], item[2:])
+        elif item[0] == "-":
+            moves.wait(item[1], item[2:])
+        elif item == "kA":
+            new_aq, x_rows = call(
+                functools.partial(left_kernel, n, width), [(n, D), rows], square, 5, 2_000_000_000
+            )(after(pos, moves.token), *moves.stacks("A"))
+            x_rows = moves.passed(x_rows)
+        elif item == "kK":
+            new_akv, new_gkv, step_kv, fit_kv = call(
+                functools.partial(keyval_kernel, n, k, width),
+                [(n, D), (k, KV), (n, KV), fit],
+                square + [((D, KV), F32), ((KV, KV), F32), ((4 * n, KV), F32)],
+                5, 3_000_000_000,
+            )(after(pos, moves.token), *moves.stacks("K"))
+            fit_kv = moves.passed(fit_kv)
+        elif item == "kT":
+            t_rows, s_rows = call(
+                functools.partial(middle_kernel, n), [rows, rows], square, 6, 1_000_000_000
+            )(after(pos, moves.token), x_rows, *moves.stacks("S"))
+            t_rows = moves.passed(t_rows)
+        else:
+            new_gq, step_q, fit_q = call(
+                functools.partial(right_kernel, n, width), [(n, D), (n, D), fit],
+                square + [(rows, F32)], 7, 3_000_000_000,
+            )(pos, t_rows, s_rows, *moves.stacks("G"))
 
     part = fit_q + fit_kv
     weight_q, weight_kv, moment_q, moment_kv = call(

time: 148 us -> 125 us (0.84)
  waiting for transfers between devices: 84.2 us -> 35.8 us
  starting transfers between devices: 24.8 us -> 38 us
  Pallas kernels: 32.4 us -> 38.3 us
  other arithmetic: 0.82 us -> 4.68 us
  local copies, waits for them, and re-layouts: 4.5 us -> 6.63 us
    ppermute x6 -> x12, waiting for transfers between devices: 36.3 us -> 17.5 us  [plane_flip(): return lax.ppermute(value, 'group', [(i, i ^ bit) for i in range(4)])]
    ppermute x4 -> x8, waiting for transfers between devices: 24.5 us -> 6.63 us  [first_hop(): lax.ppermute(value, 'dp', [(i, i ^ (4 if i & 1 else 2)) for i in range(8)])]
    ppermute x4 -> x8, waiting for transfers between devices: 15.8 us -> 8.31 us  [second_hop(): lax.ppermute(value, 'dp', [(i, i ^ (2 if i & 1 else 4)) for i in range(8)])]
    ppermute x4 -> x8, starting transfers between devices: 4.44 us -> 10.7 us  [second_hop(): lax.ppermute(value, 'dp', [(i, i ^ (2 if i & 1 else 4)) for i in range(8)])]
    pallas_call x4 -> x7, Pallas kernels: 22.6 us -> 28.5 us  [the longest x1 7.72 us: fast_shards(): call(functools.partial(right_kernel, n, width), [(n, D), (n, D), fit], sq...]
    ppermute x6 -> x12, starting transfers between devices: 10.4 us -> 15.9 us  [plane_flip(): return lax.ppermute(value, 'group', [(i, i ^ bit) for i in range(4)])]
    ppermute x6 -> x10, waiting for transfers between devices: 7.52 us -> 3.43 us  [core_flip(): return lax.ppermute(value, 'dp', [(i, i ^ 1) for i in range(8)])]
    add x8 -> x15, other arithmetic: 0.39 us -> 4.19 us  [the longest x4 2.06 us: operand(): own = self.keeps[chunk][0] + got[chunk, 'rs1'][0] + got[chunk, 'rs2']]
  transfers between devices with their start and end apart: 20 -> 38, of which waited for: 15 -> 17; matrix products, arithmetic and copies ran while one was open for 0% -> 4% of each run, Pallas kernels for 13% -> 21%
where the time goes in v4:
time: 125 us
  Pallas kernels  38.3 us (31%)
  starting transfers between devices  38 us (30%)
  waiting for transfers between devices  35.8 us (29%)
  local copies, waits for them, and re-layouts  6.63 us (5%)
  other arithmetic  4.68 us (4%)
    ppermute x12, waiting for transfers between devices, plane_flip(): return lax.ppermute(value, 'group', [(i, i ^ bit) for i in range(4)])  17.5 us
    ppermute x12, starting transfers between devices, plane_flip(): return lax.ppermute(value, 'group', [(i, i ^ bit) for i in range(4)])  15.9 us
    ppermute x8, starting transfers between devices, second_hop(): lax.ppermute(value, 'dp', [(i, i ^ (2 if i & 1 else 4)) for i in range(8)])  10.7 us
    ppermute x8, starting transfers between devices, first_hop(): lax.ppermute(value, 'dp', [(i, i ^ (4 if i & 1 else 2)) for i in range(8)])  9.6 us
    ppermute x8, waiting for transfers between devices, second_hop(): lax.ppermute(value, 'dp', [(i, i ^ (2 if i & 1 else 4)) for i in range(8)])  8.31 us
    pallas_call x1, Pallas kernels, fast_shards(): call(functools.partial(keyval_kernel, n, k, width), [(n, D), (k, KV), (n,...  8.13 us
    pallas_call x1, Pallas kernels, fast_shards(): call(functools.partial(right_kernel, n, width), [(n, D), (n, D), fit], sq...  7.72 us
    unnamed x38, local copies, waits for them, and re-layouts  6.63 us
  transfers between devices with their start and end apart: 38, of which 17 were waited for; matrix products, arithmetic and copies ran while one was open for 4% of the time, Pallas kernels for 21%

profile of v4, /device:TPU:0, one launch (start us, length us, event | category | flops | bytes accessed | tf_op | source)
XLA Modules:
  0.0 124.5 jit_solution(15516274906911911047)
XLA Ops:
  7.8 2.6 %collective-permute-done.other = f32[264,2432]{1,0:T(8,128)} collective-permute-done((f32[264,2432]{1,0:T(8,128)S(1)}, f32[264,2432]{1,0:T(8,128)}, u32[]{:S(2)}, u32[]{:S(2)}) %collective-permute-start) | collective-permute-done | bytes 2568224 | tf_op jit(solution)/shard_map/ppermute | solution.py:334
  10.4 3.4 %shard_map.191 = (f32[2,384,128]{2,1,0:T(8,128)}, f32[2,384,128]{2,1,0:T(8,128)S(1)}) custom-call(s32[2]{0:T(128)S(1)} %pad_add_fusion.pos, f32[264,2432]{1,0:T(8,128)} %collective-permute-done.other, bf16[128,768]{1,0:T(8,128)(2,1)S(1)} %get-tuple-element.118.y, bf16[768,128]{1,0:T(8,128)(2,1)S(1)} %get-tuple-element.119.o, f32[96,768]{1,0:T(8,128)S(1)} %copy-done.6), custom_call_target="tpu_custom_call" | custom-call | flops 300000000 | bytes 4000000 | tf_op jit(solution)/shard_map/pallas_call | solution.py:465
  14.6 2.9 %collective-permute-start.2 = (f32[2,384,128]{2,1,0:T(8,128)}, f32[2,384,128]{2,1,0:T(8,128)}, u32[]{:S(2)}, u32[]{:S(2)}) collective-permute-start(f32[2,384,128]{2,1,0:T(8,128)} %get-tuple-element.120), channel_id=1, source_target_pairs={{0,8},{4,20},{8,0},{12,28},{16,24},{20,4},{24,16},{28,12},{1,9},{5... | collective-permute-start | bytes 1179656 | tf_op jit(solution)/shard_map/ppermute | solution.py:338
  17.5 3.5 %shard_map.190 = (f32[2,496,128]{2,1,0:T(8,128)}, f32[2,496,128]{2,1,0:T(8,128)S(1)}) custom-call(s32[2]{0:T(128)S(1)} %pad_add_fusion.pos, f32[264,2432]{1,0:T(8,128)S(1)} %shard_map.188.mine, f32[264,2432]{1,0:T(8,128)} %collective-permute-done.other, bf16[128,768]{1,0:T(8,128)(2,1)S(1)} %get-tuple-element.111.y_akv, ...), custom_call_target="tpu_custom_call" | custom-call | flops 400000000 | bytes 4000000 | tf_op jit(solution)/shard_map/pallas_call | solution.py:469
  21.0 2.4 %shard_map.192 = (f32[2,576,128]{2,1,0:T(8,128)S(1)}, f32[2,576,128]{2,1,0:T(8,128)S(1)}) custom-call(s32[2]{0:T(128)S(1)} %pad_add_fusion.pos, f32[264,2432]{1,0:T(8,128)S(1)} %shard_map.188.mine, f32[264,2432]{1,0:T(8,128)} %collective-permute-done.other, bf16[768,256]{1,0:T(8,128)(2,1)S(1)} %get-tuple-element.123.o_q), custom_call_target="tpu_custom_call" | custom-call | flops 500000000 | bytes 4000000 | tf_op jit(solution)/shard_map/pallas_call | solution.py:474
  23.4 2.1 %collective-permute-start.4 = (f32[2,576,128]{2,1,0:T(8,128)S(1)}, f32[2,576,128]{2,1,0:T(8,128)S(1)}, u32[]{:S(2)}, u32[]{:S(2)}) collective-permute-start(f32[2,576,128]{2,1,0:T(8,128)S(1)} %get-tuple-element.124), channel_id=1, source_target_pairs={{0,8},{4,20},{8,0},{12,28},{16,24},{20,4},{24,16},{28,12},{1,9},{5... | collective-permute-start | bytes 1769480 | tf_op jit(solution)/shard_map/ppermute | solution.py:338
  25.5 2.7 %shard_map.193 = (f32[2,384,128]{2,1,0:T(8,128)S(1)}, f32[2,384,128]{2,1,0:T(8,128)S(1)}) custom-call(s32[2]{0:T(128)S(1)} %pad_add_fusion.pos, f32[264,2432]{1,0:T(8,128)} %collective-permute-done.other, bf16[128,768]{1,0:T(8,128)(2,1)S(1)} %copy-done.11, bf16[768,128]{1,0:T(8,128)(2,1)S(1)} %copy-done.13, f32[96,768]{1,0:T(8,128)S(1)} %copy-done.7), custom_call_target="tpu_custom_call" | custom-call | flops 300000000 | bytes 4000000 | tf_op jit(solution)/shard_map/pallas_call | solution.py:478
  33.1 4.0 %collective-permute-done.5 = f32[384,128]{1,0:T(8,128)S(1)} collective-permute-done((f32[384,128]{1,0:T(8,128)S(1)}, f32[384,128]{1,0:T(8,128)S(1)}, u32[]{:S(2)}, u32[]{:S(2)}) %collective-permute-start.5) | collective-permute-done | bytes 196640 | tf_op jit(solution)/shard_map/ppermute | solution.py:342
  41.4 2.5 %collective-permute-start.7 = (f32[576,128]{1,0:T(8,128)S(1)}, f32[576,128]{1,0:T(8,128)S(1)}, u32[]{:S(2)}, u32[]{:S(2)}) collective-permute-start(f32[576,128]{1,0:T(8,128)S(1)} %add_bitcast_fusion), channel_id=1, source_target_pairs={{0,16},{4,12},{8,24},{12,4},{16,0},{20,28},{24,8},{28,20},{1,17},{... | collective-permute-start | bytes 884744 | tf_op jit(solution)/shard_map/ppermute | solution.py:342
  45.0 2.7 %collective-permute-start.10 = (f32[192,128]{1,0:T(8,128)S(1)}, f32[192,128]{1,0:T(8,128)S(1)}, u32[]{:S(2)}, u32[]{:S(2)}) collective-permute-start(f32[192,128]{1,0:T(8,128)S(1)} %select_add_fusion.3), channel_id=1, source_target_pairs={{0,2},{1,3},{2,0},{3,1},{4,6},{5,7},{6,4},{7,5},{8,10},{9,11},{10,... | collective-permute-start | bytes 294920 | tf_op jit(solution)/shard_map/ppermute | solution.py:346
  55.4 1.8 %collective-permute-start.12 = (f32[192,128]{1,0:T(8,128)S(1)}, f32[192,128]{1,0:T(8,128)S(1)}, u32[]{:S(2)}, u32[]{:S(2)}) collective-permute-start(f32[192,128]{1,0:T(8,128)S(1)} %add.118), channel_id=1, source_target_pairs={{0,1},{1,0},{2,3},{3,2},{4,5},{5,4},{6,7},{7,6},{8,9},{9,8},{10,11... | collective-permute-start | bytes 294920 | tf_op jit(solution)/shard_map/ppermute | solution.py:346
  57.2 2.9 %collective-permute-done.14 = f32[288,128]{1,0:T(8,128)S(1)} collective-permute-done((f32[288,128]{1,0:T(8,128)S(1)}, f32[288,128]{1,0:T(8,128)S(1)}, u32[]{:S(2)}, u32[]{:S(2)}) %collective-permute-start.14) | collective-permute-done | bytes 147488 | tf_op jit(solution)/shard_map/ppermute | solution.py:346
  61.9 2.9 %collective-permute-done.18 = f32[192,128]{1,0:T(8,128)S(1)} collective-permute-done((f32[192,128]{1,0:T(8,128)S(1)}, f32[192,128]{1,0:T(8,128)S(1)}, u32[]{:S(2)}, u32[]{:S(2)}) %collective-permute-start.18) | collective-permute-done | bytes 98336 | tf_op jit(solution)/shard_map/ppermute | solution.py:346
  68.0 2.7 %collective-permute-done.17 = f32[384,128]{1,0:T(8,128)S(1)} collective-permute-done((f32[384,128]{1,0:T(8,128)S(1)}, f32[384,128]{1,0:T(8,128)S(1)}, u32[]{:S(2)}, u32[]{:S(2)}) %collective-permute-start.17) | collective-permute-done | bytes 196640 | tf_op jit(solution)/shard_map/ppermute | solution.py:342
  72.5 2.2 %collective-permute-start.20 = (f32[496,128]{1,0:T(8,128)S(1)}, f32[496,128]{1,0:T(8,128)S(1)}, u32[]{:S(2)}, u32[]{:S(2)}) collective-permute-start(f32[496,128]{1,0:T(8,128)S(1)} %get-tuple-element.163), channel_id=1, source_target_pairs={{0,16},{4,12},{8,24},{12,4},{16,0},{20,28},{24,8},{28,20},{1,17},{... | collective-permute-start | bytes 761864 | tf_op jit(solution)/shard_map/ppermute | solution.py:342
  75.0 2.0 %collective-permute-start.23 = (f32[192,128]{1,0:T(8,128)S(1)}, f32[192,128]{1,0:T(8,128)S(1)}, u32[]{:S(2)}, u32[]{:S(2)}) collective-permute-start(f32[192,128]{1,0:T(8,128)S(1)} %get-tuple-element.165), channel_id=1, source_target_pairs={{0,2},{1,3},{2,0},{3,1},{4,6},{5,7},{6,4},{7,5},{8,10},{9,11},{10,... | collective-permute-start | bytes 294920 | tf_op jit(solution)/shard_map/ppermute | solution.py:346
  77.0 4.0 %collective-permute-done.23 = f32[192,128]{1,0:T(8,128)S(1)} collective-permute-done((f32[192,128]{1,0:T(8,128)S(1)}, f32[192,128]{1,0:T(8,128)S(1)}, u32[]{:S(2)}, u32[]{:S(2)}) %collective-permute-start.23) | collective-permute-done | bytes 98336 | tf_op jit(solution)/shard_map/ppermute | solution.py:346
  84.3 3.1 %collective-permute-done.26 = f32[192,128]{1,0:T(8,128)S(1)} collective-permute-done((f32[192,128]{1,0:T(8,128)S(1)}, f32[192,128]{1,0:T(8,128)S(1)}, u32[]{:S(2)}, u32[]{:S(2)}) %collective-permute-start.26) | collective-permute-done | bytes 98336 | tf_op jit(solution)/shard_map/ppermute | solution.py:346
  87.7 2.0 %collective-permute-start.31 = (f32[2,496,128]{2,1,0:T(8,128)S(1)}, f32[2,496,128]{2,1,0:T(8,128)S(1)}, u32[]{:S(2)}, u32[]{:S(2)}) collective-permute-start(f32[2,496,128]{2,1,0:T(8,128)S(1)} %pad_maximum_fusion.1.refs_0_), channel_id=1, source_target_pairs={{0,8},{4,20},{8,0},{12,28},{16,24},{20,4},{24,16},{28,12},{1,9},{5... | collective-permute-start | bytes 1523720 | tf_op jit(solution)/shard_map/ppermute | solution.py:338
  89.7 6.0 %shard_map.194 = (f32[96,768]{1,0:T(8,128)}, f32[384,768]{1,0:T(8,128)S(1)}) custom-call(s32[2]{0:T(128)S(1)} %pad_add_fusion.pos, f32[2,384,128]{2,1,0:T(8,128)S(1)} %pad_maximum_fusion.2.refs_0_, f32[2,384,128]{2,1,0:T(8,128)S(1)} %collective-permute-done.21.refs_1_, f32[2,384,128]{2,1,0:T(8,128)S(1)} %collective-permute-done.19.refs_2_, ...), custom_call_target="tpu_custom_call" | custom-call | flops 2000000000 | bytes 4000000 | tf_op jit(solution)/shard_map/pallas_call | solution.py:493
  99.9 8.1 %shard_map.195 = (f32[96,768]{1,0:T(8,128)}, f32[16,128]{1,0:T(8,128)}, f32[96,128]{1,0:T(8,128)S(1)}, f32[8,128]{1,0:T(8,128)S(1)}) custom-call(s32[2]{0:T(128)S(1)} %pad_add_fusion.pos, f32[2,496,128]{2,1,0:T(8,128)S(1)} %pad_maximum_fusion.1.refs_0_, f32[2,496,128]{2,1,0:T(8,128)S(1)} %collective-permute-done.31.refs_1_, ...), custom_call_target="tpu_custom_call" | custom-call | flops 3000000000 | bytes 4000000 | tf_op jit(solution)/shard_map/pallas_call | solution.py:498
  108.2 3.4 %collective-permute-done.35.refs_1_ = f32[2,384,128]{2,1,0:T(8,128)S(1)} collective-permute-done((f32[2,384,128]{2,1,0:T(8,128)S(1)}, f32[2,384,128]{2,1,0:T(8,128)S(1)}, u32[]{:S(2)}, u32[]{:S(2)}) %collective-permute-start.35) | collective-permute-done | bytes 393248 | tf_op jit(solution)/shard_map/ppermute | solution.py:338
  111.6 2.7 %shard_map.196 = (f32[384,768]{1,0:T(8,128)S(1)}, f32[384,768]{1,0:T(8,128)S(1)}) custom-call(s32[2]{0:T(128)S(1)} %pad_add_fusion.pos, f32[384,768]{1,0:T(8,128)S(1)} %get-tuple-element.180.x_ref, f32[2,576,128]{2,1,0:T(8,128)S(1)} %pad_maximum_fusion.refs_0_, f32[2,576,128]{2,1,0:T(8,128)S(1)} %collective-permute-done.29.refs_1_, ...), custom_call_target="tpu_custom_call" | custom-call | flops 1000000000 | bytes 4000000 | tf_op jit(solution)/shard_map/pallas_call | solution.py:506
  114.4 7.7 %shard_map.197 = (f32[96,768]{1,0:T(8,128)}, f32[96,768]{1,0:T(8,128)S(1)}, f32[8,128]{1,0:T(8,128)S(1)}) custom-call(s32[2]{0:T(128)S(1)} %pad_add_fusion.pos, f32[384,768]{1,0:T(8,128)S(1)} %get-tuple-element.200.t_ref, f32[384,768]{1,0:T(8,128)S(1)} %get-tuple-element.201.rows_ref, f32[2,384,128]{2,1,0:T(8,128)S(1)} %pad_maximum_fusion.3.refs_0_, ...), custom_call_target="tpu_custom_call" | custom-call | flops 3000000000 | bytes 4000000 | tf_op jit(solution)/shard_map/pallas_call | solution.py:511
  (134 shorter events, 43.3 us)
Async XLA Ops:
  14.6 13.6 %collective-permute-start.2 = (f32[2,384,128]{2,1,0:T(8,128)}, f32[2,384,128]{2,1,0:T(8,128)}, u32[]{:S(2)}, u32[]{:S(2)}) collective-permute-start(f32[2,384,128]{2,1,0:T(8,128)} %get-tuple-element.120), channel_id=1, source_target_pairs={{0,8},{4,20},{8,0},{12,28},{16,24},{20,4},{24,16},{28,12},{1,9},{5... | collective-permute-start | bytes 1179656 | tf_op jit(solution)/shard_map/ppermute | solution.py:338
  21.0 9.8 %collective-permute-start.1 = (f32[2,496,128]{2,1,0:T(8,128)}, f32[2,496,128]{2,1,0:T(8,128)}, u32[]{:S(2)}, u32[]{:S(2)}) collective-permute-start(f32[2,496,128]{2,1,0:T(8,128)} %get-tuple-element.117), channel_id=1, source_target_pairs={{0,8},{4,20},{8,0},{12,28},{16,24},{20,4},{24,16},{28,12},{1,9},{5... | collective-permute-start | bytes 1523720 | tf_op jit(solution)/shard_map/ppermute | solution.py:338
  23.4 17.9 %collective-permute-start.4 = (f32[2,576,128]{2,1,0:T(8,128)S(1)}, f32[2,576,128]{2,1,0:T(8,128)S(1)}, u32[]{:S(2)}, u32[]{:S(2)}) collective-permute-start(f32[2,576,128]{2,1,0:T(8,128)S(1)} %get-tuple-element.124), channel_id=1, source_target_pairs={{0,8},{4,20},{8,0},{12,28},{16,24},{20,4},{24,16},{28,12},{1,9},{5... | collective-permute-start | bytes 1769480 | tf_op jit(solution)/shard_map/ppermute | solution.py:338
  29.2 7.9 %collective-permute-start.5 = (f32[384,128]{1,0:T(8,128)S(1)}, f32[384,128]{1,0:T(8,128)S(1)}, u32[]{:S(2)}, u32[]{:S(2)}) collective-permute-start(f32[384,128]{1,0:T(8,128)S(1)} %fusion.2), channel_id=1, source_target_pairs={{0,16},{4,12},{8,24},{12,4},{16,0},{20,28},{24,8},{28,20},{1,17},{... | collective-permute-start | bytes 589832 | tf_op jit(solution)/shard_map/ppermute | solution.py:342
  31.8 12.2 %collective-permute-start.3 = (f32[496,128]{1,0:T(8,128)S(1)}, f32[496,128]{1,0:T(8,128)S(1)}, u32[]{:S(2)}, u32[]{:S(2)}) collective-permute-start(f32[496,128]{1,0:T(8,128)S(1)} %add_bitcast_fusion.1), channel_id=1, source_target_pairs={{0,16},{4,12},{8,24},{12,4},{16,0},{20,28},{24,8},{28,20},{1,17},{... | collective-permute-start | bytes 761864 | tf_op jit(solution)/shard_map/ppermute | solution.py:342
  38.1 6.8 %collective-permute-start.8 = (f32[192,128]{1,0:T(8,128)S(1)}, f32[192,128]{1,0:T(8,128)S(1)}, u32[]{:S(2)}, u32[]{:S(2)}) collective-permute-start(f32[192,128]{1,0:T(8,128)S(1)} %slice_select_fusion.3), channel_id=1, source_target_pairs={{0,1},{1,0},{2,3},{3,2},{4,5},{5,4},{6,7},{7,6},{8,9},{9,8},{10,11... | collective-permute-start | bytes 294920 | tf_op jit(solution)/shard_map/ppermute | solution.py:346
  41.4 9.5 %collective-permute-start.7 = (f32[576,128]{1,0:T(8,128)S(1)}, f32[576,128]{1,0:T(8,128)S(1)}, u32[]{:S(2)}, u32[]{:S(2)}) collective-permute-start(f32[576,128]{1,0:T(8,128)S(1)} %add_bitcast_fusion), channel_id=1, source_target_pairs={{0,16},{4,12},{8,24},{12,4},{16,0},{20,28},{24,8},{28,20},{1,17},{... | collective-permute-start | bytes 884744 | tf_op jit(solution)/shard_map/ppermute | solution.py:342
  43.9 8.7 %collective-permute-start.11 = (f32[2,384,128]{2,1,0:T(8,128)S(1)}, f32[2,384,128]{2,1,0:T(8,128)S(1)}, u32[]{:S(2)}, u32[]{:S(2)}) collective-permute-start(f32[2,384,128]{2,1,0:T(8,128)S(1)} %get-tuple-element.142), channel_id=1, source_target_pairs={{0,8},{4,20},{8,0},{12,28},{16,24},{20,4},{24,16},{28,12},{1,9},{5... | collective-permute-start | bytes 1179656 | tf_op jit(solution)/shard_map/ppermute | solution.py:338
  45.0 10.4 %collective-permute-start.10 = (f32[192,128]{1,0:T(8,128)S(1)}, f32[192,128]{1,0:T(8,128)S(1)}, u32[]{:S(2)}, u32[]{:S(2)}) collective-permute-start(f32[192,128]{1,0:T(8,128)S(1)} %select_add_fusion.3), channel_id=1, source_target_pairs={{0,2},{1,3},{2,0},{3,1},{4,6},{5,7},{6,4},{7,5},{8,10},{9,11},{10,... | collective-permute-start | bytes 294920 | tf_op jit(solution)/shard_map/ppermute | solution.py:346
  51.0 9.1 %collective-permute-start.14 = (f32[288,128]{1,0:T(8,128)S(1)}, f32[288,128]{1,0:T(8,128)S(1)}, u32[]{:S(2)}, u32[]{:S(2)}) collective-permute-start(f32[288,128]{1,0:T(8,128)S(1)} %slice_select_fusion), channel_id=1, source_target_pairs={{0,1},{1,0},{2,3},{3,2},{4,5},{5,4},{6,7},{7,6},{8,9},{9,8},{10,11... | collective-permute-start | bytes 442376 | tf_op jit(solution)/shard_map/ppermute | solution.py:346
  52.6 7.4 %collective-permute-start.13 = (f32[384,128]{1,0:T(8,128)S(1)}, f32[384,128]{1,0:T(8,128)S(1)}, u32[]{:S(2)}, u32[]{:S(2)}) collective-permute-start(f32[384,128]{1,0:T(8,128)S(1)} %add_bitcast_fusion.2), channel_id=1, source_target_pairs={{0,16},{4,12},{8,24},{12,4},{16,0},{20,28},{24,8},{28,20},{1,17},{... | collective-permute-start | bytes 589832 | tf_op jit(solution)/shard_map/ppermute | solution.py:342
  54.1 7.8 %collective-permute-start.9 = (f32[248,128]{1,0:T(8,128)S(1)}, f32[248,128]{1,0:T(8,128)S(1)}, u32[]{:S(2)}, u32[]{:S(2)}) collective-permute-start(f32[248,128]{1,0:T(8,128)S(1)} %select_add_fusion.1), channel_id=1, source_target_pairs={{0,2},{1,3},{2,0},{3,1},{4,6},{5,7},{6,4},{7,5},{8,10},{9,11},{10,... | collective-permute-start | bytes 380936 | tf_op jit(solution)/shard_map/ppermute | solution.py:346
  55.4 6.6 %collective-permute-start.12 = (f32[192,128]{1,0:T(8,128)S(1)}, f32[192,128]{1,0:T(8,128)S(1)}, u32[]{:S(2)}, u32[]{:S(2)}) collective-permute-start(f32[192,128]{1,0:T(8,128)S(1)} %add.118), channel_id=1, source_target_pairs={{0,1},{1,0},{2,3},{3,2},{4,5},{5,4},{6,7},{7,6},{8,9},{9,8},{10,11... | collective-permute-start | bytes 294920 | tf_op jit(solution)/shard_map/ppermute | solution.py:346
  65.0 6.2 %collective-permute-start.16 = (f32[288,128]{1,0:T(8,128)S(1)}, f32[288,128]{1,0:T(8,128)S(1)}, u32[]{:S(2)}, u32[]{:S(2)}) collective-permute-start(f32[288,128]{1,0:T(8,128)S(1)} %select_add_fusion), channel_id=1, source_target_pairs={{0,2},{1,3},{2,0},{3,1},{4,6},{5,7},{6,4},{7,5},{8,10},{9,11},{10,... | collective-permute-start | bytes 442376 | tf_op jit(solution)/shard_map/ppermute | solution.py:346
  70.7 11.2 %collective-permute-start.21 = (f32[2,384,128]{2,1,0:T(8,128)S(1)}, f32[2,384,128]{2,1,0:T(8,128)S(1)}, u32[]{:S(2)}, u32[]{:S(2)}) collective-permute-start(f32[2,384,128]{2,1,0:T(8,128)S(1)} %pad_maximum_fusion.2.refs_0_), channel_id=1, source_target_pairs={{0,8},{4,20},{8,0},{12,28},{16,24},{20,4},{24,16},{28,12},{1,9},{5... | collective-permute-start | bytes 1179656 | tf_op jit(solution)/shard_map/ppermute | solution.py:338
  72.5 9.4 %collective-permute-start.20 = (f32[496,128]{1,0:T(8,128)S(1)}, f32[496,128]{1,0:T(8,128)S(1)}, u32[]{:S(2)}, u32[]{:S(2)}) collective-permute-start(f32[496,128]{1,0:T(8,128)S(1)} %get-tuple-element.163), channel_id=1, source_target_pairs={{0,16},{4,12},{8,24},{12,4},{16,0},{20,28},{24,8},{28,20},{1,17},{... | collective-permute-start | bytes 761864 | tf_op jit(solution)/shard_map/ppermute | solution.py:342
  74.8 7.2 %collective-permute-start.22 = (f32[288,128]{1,0:T(8,128)S(1)}, f32[288,128]{1,0:T(8,128)S(1)}, u32[]{:S(2)}, u32[]{:S(2)}) collective-permute-start(f32[288,128]{1,0:T(8,128)S(1)} %add.129), channel_id=1, source_target_pairs={{0,1},{1,0},{2,3},{3,2},{4,5},{5,4},{6,7},{7,6},{8,9},{9,8},{10,11... | collective-permute-start | bytes 442376 | tf_op jit(solution)/shard_map/ppermute | solution.py:346
  82.0 7.7 %collective-permute-start.24 = (f32[2,496,128]{2,1,0:T(8,128)S(1)}, f32[2,496,128]{2,1,0:T(8,128)S(1)}, u32[]{:S(2)}, u32[]{:S(2)}) collective-permute-start(f32[2,496,128]{2,1,0:T(8,128)S(1)} %pad_maximum_fusion.1.refs_0_), channel_id=1, source_target_pairs={{0,4},{4,0},{8,12},{12,8},{16,20},{20,16},{24,28},{28,24},{1,5},{5... | collective-permute-start | bytes 1523720 | tf_op jit(solution)/shard_map/ppermute | solution.py:334
  83.0 12.7 %collective-permute-start.27 = (f32[576,128]{1,0:T(8,128)S(1)}, f32[576,128]{1,0:T(8,128)S(1)}, u32[]{:S(2)}, u32[]{:S(2)}) collective-permute-start(f32[576,128]{1,0:T(8,128)S(1)} %get-tuple-element.178), channel_id=1, source_target_pairs={{0,16},{4,12},{8,24},{12,4},{16,0},{20,28},{24,8},{28,20},{1,17},{... | collective-permute-start | bytes 884744 | tf_op jit(solution)/shard_map/ppermute | solution.py:342
  87.5 8.2 %collective-permute-start.28 = (f32[384,128]{1,0:T(8,128)S(1)}, f32[384,128]{1,0:T(8,128)S(1)}, u32[]{:S(2)}, u32[]{:S(2)}) collective-permute-start(f32[384,128]{1,0:T(8,128)S(1)} %get-tuple-element.182), channel_id=1, source_target_pairs={{0,16},{4,12},{8,24},{12,4},{16,0},{20,28},{24,8},{28,20},{1,17},{... | collective-permute-start | bytes 589832 | tf_op jit(solution)/shard_map/ppermute | solution.py:342
  87.7 9.7 %collective-permute-start.31 = (f32[2,496,128]{2,1,0:T(8,128)S(1)}, f32[2,496,128]{2,1,0:T(8,128)S(1)}, u32[]{:S(2)}, u32[]{:S(2)}) collective-permute-start(f32[2,496,128]{2,1,0:T(8,128)S(1)} %pad_maximum_fusion.1.refs_0_), channel_id=1, source_target_pairs={{0,8},{4,20},{8,0},{12,28},{16,24},{20,4},{24,16},{28,12},{1,9},{5... | collective-permute-start | bytes 1523720 | tf_op jit(solution)/shard_map/ppermute | solution.py:338
  97.5 10.5 %collective-permute-start.29 = (f32[2,576,128]{2,1,0:T(8,128)S(1)}, f32[2,576,128]{2,1,0:T(8,128)S(1)}, u32[]{:S(2)}, u32[]{:S(2)}) collective-permute-start(f32[2,576,128]{2,1,0:T(8,128)S(1)} %pad_maximum_fusion.refs_0_), channel_id=1, source_target_pairs={{0,8},{4,20},{8,0},{12,28},{16,24},{20,4},{24,16},{28,12},{1,9},{5... | collective-permute-start | bytes 1769480 | tf_op jit(solution)/shard_map/ppermute | solution.py:338
  98.8 9.2 %collective-permute-start.32 = (f32[2,384,128]{2,1,0:T(8,128)S(1)}, f32[2,384,128]{2,1,0:T(8,128)S(1)}, u32[]{:S(2)}, u32[]{:S(2)}) collective-permute-start(f32[2,384,128]{2,1,0:T(8,128)S(1)} %pad_maximum_fusion.3.refs_0_), channel_id=1, source_target_pairs={{0,4},{4,0},{8,12},{12,8},{16,20},{20,16},{24,28},{28,24},{1,5},{5... | collective-permute-start | bytes 1179656 | tf_op jit(solution)/shard_map/ppermute | solution.py:334
  98.9 12.7 %collective-permute-start.35 = (f32[2,384,128]{2,1,0:T(8,128)S(1)}, f32[2,384,128]{2,1,0:T(8,128)S(1)}, u32[]{:S(2)}, u32[]{:S(2)}) collective-permute-start(f32[2,384,128]{2,1,0:T(8,128)S(1)} %pad_maximum_fusion.3.refs_0_), channel_id=1, source_target_pairs={{0,8},{4,20},{8,0},{12,28},{16,24},{20,4},{24,16},{28,12},{1,9},{5... | collective-permute-start | bytes 1179656 | tf_op jit(solution)/shard_map/ppermute | solution.py:338
  (33 other events, 135.7 us)

commit v5 on v4

--- a/solution.py
+++ b/solution.py
@@ -16,7 +16,6 @@
 LANES = 128
 F32 = jnp.float32
 BF16 = jnp.bfloat16
-VMEM_LIMIT = 28 * 1024 * 1024
 
 
 def rolled(block, shift):
@@ -112,44 +111,39 @@
     return [window_tiles(part, n * b, width) for part, b in zip(parts, blocks)]
 
 
-def factor_kernel(n, width, scale, lo, pos, other, y, o, state, send, keep, u):
-    D, samples = y.shape[1], y.shape[0]
-    tokens = other.shape[0] - 8
-    blocks = roles(pos[0], pos[1])
-    chosen = join(u, other, picker(other, tokens, samples), o, y, lo, lo + D)
-    place(send, keep, factor_tiles(u, chosen, state, n, blocks, width, scale))
-
-
-def gradient_kernel(n, pos, mine, other, o_q, send, keep, t_q):
-    D, tokens = o_q.shape
-    t_q[:, :tokens] = o_q[...]
-    t_q[:, tokens:] = turned(other[:tokens, :D])
-    ends = [ref[:tokens, D:2 * D].astype(BF16) for ref in (mine, other)]
-    sums = product(left_blocks(t_q, n, roles(pos[0], pos[1])), jnp.concatenate(ends, axis=0))
-    place(send, keep, [plain_tiles(part) for part in four(sums, n)])
-
-
-def keyval_sums_kernel(
+def gram_kernel(
     n, k, width, scale,
-    pos, mine, other, y_akv, y_gkv, o_akv, o_gkv, o_kv, st_akv, st_gkv,
-    send, keep, u_akv, u_gkv, t_kv, g_kv,
+    pos, mine, other, y_aq, y_gq, y_akv, y_gkv, o_aq, o_gq, o_akv, o_gkv, o_q, o_kv,
+    st_aq, st_gq, st_akv, st_gkv,
+    a_send, a_keep, k_send, k_keep, s_send, s_keep, g_send, g_keep,
+    u_aq, u_gq, u_akv, u_gkv, t_q, t_kv, g_kv,
 ):
     tokens, samples = o_kv.shape[1], o_akv.shape[1]
     D, KV = y_akv.shape[1], y_gkv.shape[1]
     blocks = roles(pos[0], pos[1])
     pick = picker(other, tokens, samples)
-    y = join(u_akv, other, pick, o_akv, y_akv, 2 * D, 3 * D)
-    at = place(send, keep, factor_tiles(u_akv, y, st_akv, n, blocks, width, scale))
-    t_kv[:, :tokens] = o_kv[...]
-    t_kv[:, tokens:] = turned(other[:tokens, 2 * D:3 * D])
-    ends = [ref[:tokens, 3 * D:].astype(BF16) for ref in (mine, other)]
-    sums = product(left_blocks(t_kv, n, blocks), jnp.concatenate(ends, axis=0))
-    at = place(send, keep, [[part] for part in four(sums, n)], at)
-    y = join(u_gkv, other, pick, o_gkv, y_gkv, 3 * D, 3 * D + KV)
-    g_kv[...] = product(u_gkv[...], y) * scale
+
+    def factor(u, o, y, state, lo):
+        chosen = join(u, other, pick, o, y, lo, lo + D)
+        return factor_tiles(u, chosen, state, n, blocks, width, scale)
+
+    def gradient(t, o, lo, first, last):
+        t[:, :tokens] = o[...]
+        t[:, tokens:] = turned(other[:tokens, lo:lo + D])
+        ends = [ref[:tokens, first:last].astype(BF16) for ref in (mine, other)]
+        return four(product(left_blocks(t, n, blocks), jnp.concatenate(ends, axis=0)), n)
+
+    place(a_send, a_keep, factor(u_aq, o_aq, y_aq, st_aq, 0))
+    at = place(k_send, k_keep, factor(u_akv, o_akv, y_akv, st_akv, 2 * D))
+    sums = gradient(t_kv, o_kv, 2 * D, 3 * D, 3 * D + KV)
+    at = place(k_send, k_keep, [[part] for part in sums], at)
+    chosen = join(u_gkv, other, pick, o_gkv, y_gkv, 3 * D, 3 * D + KV)
+    g_kv[...] = product(u_gkv[...], chosen) * scale
     small = [g_kv[pl.ds(pl.multiple_of(k * b, 8), k), :] for b in blocks]
     small[0] = small[0] + (BLEND_RATE / 4.0) * st_gkv[...]
-    place(send, keep, [[part] for part in small], at)
+    place(k_send, k_keep, [[part] for part in small], at)
+    place(s_send, s_keep, [plain_tiles(part) for part in gradient(t_q, o_q, 0, D, 2 * D)])
+    place(g_send, g_keep, factor(u_gq, o_gq, y_gq, st_gq, D))
 
 
 def identity_rows(rows, extent, start):
@@ -316,7 +310,7 @@
         outs[at][...] = weight[...] - LEARNING_RATE * fresh
 
 
-def call(kernel, outs, scratch, count, flops=0, scalars=1, kind=F32):
+def call(kernel, outs, scratch, count, flops=0, scalars=1, kind=F32, limit=24):
     vmem = pl.BlockSpec(memory_space=pltpu.VMEM)
     smem = pl.BlockSpec(memory_space=pltpu.SMEM)
     return pl.pallas_call(
@@ -325,7 +319,7 @@
         in_specs=[smem] * scalars + [vmem] * (count - scalars),
         out_specs=[vmem] * len(outs),
         scratch_shapes=[pltpu.VMEM(shape, kind) for shape, kind in scratch],
-        compiler_params=pltpu.CompilerParams(vmem_limit_bytes=VMEM_LIMIT),
+        compiler_params=pltpu.CompilerParams(vmem_limit_bytes=limit * 1024 * 1024),
         cost_estimate=pl.CostEstimate(flops=flops, bytes_accessed=4_000_000, transcendentals=0),
     )
 
@@ -448,7 +442,7 @@
     pos = jnp.stack([d // 2, d % 2]).astype(jnp.int32)
     scale = (1.0 - BLEND_RATE) / (samples * 32)
 
-    (mine,) = call(cast_kernel, [(tokens + 8, 3 * D + KV)], [], 5, scalars=0)(
+    (mine,) = call(cast_kernel, [(tokens + 8, 3 * D + KV)], [], 5, scalars=0, limit=8)(
         sample_rows.reshape(1, samples), act_query, grad_query, act_keyval, grad_keyval
     )
     other = core_flip(mine)
@@ -456,29 +450,24 @@
         functools.partial(own_kernel, tokens, samples, D),
         [(samples, D)] * 3 + [(samples, KV)] + [(D, samples)] * 3 + [(KV, samples)]
         + [(D, tokens)] * 2,
-        [], 1, 300_000_000, scalars=0, kind=BF16,
+        [], 1, 300_000_000, scalars=0, kind=BF16, limit=12,
     )(mine)
 
     r_f = n * (width // LANES)
-    both, all_tokens = ((D, 2 * samples), BF16), ((D, 2 * tokens), BF16)
-    sends, keeps = {}, {}
-    sends["A"], keeps["A"] = call(
-        functools.partial(factor_kernel, n, width, scale, 0), [(2, r_f, LANES)] * 2,
-        [both], 5, 300_000_000,
-    )(pos, other, y_aq, u_aq, state_aq)
-    sends["K"], keeps["K"] = call(
-        functools.partial(keyval_sums_kernel, n, k, width, scale),
-        [(2, r_f + n + k, LANES)] * 2,
-        [both, ((KV, 2 * samples), BF16), all_tokens, ((KV, KV), F32)], 10, 400_000_000,
-    )(pos, mine, other, y_akv, y_gkv, u_akv, u_gkv, t_kv, state_akv, state_gkv)
-    sends["S"], keeps["S"] = call(
-        functools.partial(gradient_kernel, n), [(2, n * (D // LANES), LANES)] * 2,
-        [all_tokens], 4, 500_000_000,
-    )(pos, mine, other, t_q)
-    sends["G"], keeps["G"] = call(
-        functools.partial(factor_kernel, n, width, scale, D), [(2, r_f, LANES)] * 2,
-        [both], 5, 300_000_000,
-    )(pos, other, y_gq, u_gq, state_gq)
+    sizes = (r_f, r_f + n + k, n * (D // LANES), r_f)
+    grams = call(
+        functools.partial(gram_kernel, n, k, width, scale),
+        [(2, size, LANES) for size in sizes for _ in range(2)],
+        [
+            *[((D, 2 * samples), BF16)] * 3, ((KV, 2 * samples), BF16),
+            *[((D, 2 * tokens), BF16)] * 2, ((KV, KV), F32),
+        ],
+        17, 2_000_000_000, limit=16,
+    )(
+        pos, mine, other, y_aq, y_gq, y_akv, y_gkv, u_aq, u_gq, u_akv, u_gkv, t_q, t_kv,
+        state_aq, state_gq, state_akv, state_gkv,
+    )
+    sends, keeps = dict(zip("AKSG", grams[0::2])), dict(zip("AKSG", grams[1::2]))
 
     rows = (4 * n, D)
     square = [((D, D), F32), ((D, D), BF16), ((D, D), BF16)]
@@ -515,7 +504,7 @@
 
     part = fit_q + fit_kv
     weight_q, weight_kv, moment_q, moment_kv = call(
-        update_kernel, [(n, D), (n, KV)] * 2, [], 8, scalars=0
+        update_kernel, [(n, D), (n, KV)] * 2, [], 8, scalars=0, limit=8
     )(
         part, core_flip(part), step_q, step_kv,
         weight_query, weight_keyval, moment_query, moment_keyval,

time: 125 us -> 128 us (1.024)
  starting transfers between devices: 38 us -> 47.6 us
  Pallas kernels: 38.3 us -> 31.3 us
  other arithmetic: 4.68 us -> 2.91 us
  waiting for transfers between devices: 35.8 us -> 37.3 us
    ppermute x8, waiting for transfers between devices: 6.63 us -> 19 us  [first_hop(): lax.ppermute(value, 'dp', [(i, i ^ (4 if i & 1 else 2)) for i in range(8)])]
    ppermute x12, starting transfers between devices: 15.9 us -> 23.8 us  [plane_flip(): return lax.ppermute(value, 'group', [(i, i ^ bit) for i in range(4)])]
    pallas_call x6 -> x3, Pallas kernels: 13.2 us -> 6.04 us  [the longest x1 4.95 us: fast_shards(): call(functools.partial(gram_kernel, n, k, width, scale), [(2, size, LANES...]
    ppermute x8, waiting for transfers between devices: 8.31 us -> 1.72 us  [second_hop(): lax.ppermute(value, 'dp', [(i, i ^ (2 if i & 1 else 4)) for i in range(8)])]
    ppermute x12, waiting for transfers between devices: 17.5 us -> 11.8 us  [plane_flip(): return lax.ppermute(value, 'group', [(i, i ^ bit) for i in range(4)])]
    ppermute x8, starting transfers between devices: 10.7 us -> 13.3 us  [second_hop(): lax.ppermute(value, 'dp', [(i, i ^ (2 if i & 1 else 4)) for i in range(8)])]
    add x4, other arithmetic: 2.06 us -> 0.18 us  [operand(): own = self.keeps[chunk][0] + got[chunk, 'rs1'][0] + got[chunk, 'rs2']]
    ppermute x8, starting transfers between devices: 9.6 us -> 8.24 us  [first_hop(): lax.ppermute(value, 'dp', [(i, i ^ (4 if i & 1 else 2)) for i in range(8)])]
  transfers between devices with their start and end apart: 38 -> 38, of which waited for: 17 -> 17; matrix products, arithmetic and copies ran while one was open for 4% -> 2% of each run, Pallas kernels for 21% -> 14%
where the time goes in v5:
time: 128 us
  starting transfers between devices  47.6 us (37%)
  waiting for transfers between devices  37.3 us (29%)
  Pallas kernels  31.3 us (24%)
  local copies, waits for them, and re-layouts  7.67 us (6%)
  other arithmetic  2.91 us (2%)
    ppermute x12, starting transfers between devices, plane_flip(): return lax.ppermute(value, 'group', [(i, i ^ bit) for i in range(4)])  23.8 us
    ppermute x8, waiting for transfers between devices, first_hop(): lax.ppermute(value, 'dp', [(i, i ^ (4 if i & 1 else 2)) for i in range(8)])  19 us
    ppermute x8, starting transfers between devices, second_hop(): lax.ppermute(value, 'dp', [(i, i ^ (2 if i & 1 else 4)) for i in range(8)])  13.3 us
    ppermute x12, waiting for transfers between devices, plane_flip(): return lax.ppermute(value, 'group', [(i, i ^ bit) for i in range(4)])  11.8 us
    ppermute x8, starting transfers between devices, first_hop(): lax.ppermute(value, 'dp', [(i, i ^ (4 if i & 1 else 2)) for i in range(8)])  8.24 us
    pallas_call x1, Pallas kernels, fast_shards(): call(functools.partial(keyval_kernel, n, k, width), [(n, D), (k, KV), (n,...  8.16 us
    pallas_call x1, Pallas kernels, fast_shards(): call(functools.partial(right_kernel, n, width), [(n, D), (n, D), fit], sq...  7.7 us
    unnamed x40, local copies, waits for them, and re-layouts  7.67 us
  transfers between devices with their start and end apart: 38, of which 17 were waited for; matrix products, arithmetic and copies ran while one was open for 2% of the time, Pallas kernels for 14%

profile of v5, /device:TPU:0, one launch (start us, length us, event | category | flops | bytes accessed | tf_op | source)
XLA Modules:
  0.0 127.6 jit_solution(7053019752193175188)
XLA Ops:
  6.5 3.9 %collective-permute-done.other = f32[264,2432]{1,0:T(8,128)} collective-permute-done((f32[264,2432]{1,0:T(8,128)S(1)}, f32[264,2432]{1,0:T(8,128)}, u32[]{:S(2)}, u32[]{:S(2)}) %collective-permute-start) | collective-permute-done | bytes 2568224 | tf_op jit(solution)/shard_map/ppermute | solution.py:328
  10.4 5.0 %shard_map.190 = (f32[2,384,128]{2,1,0:T(8,128)}, f32[2,384,128]{2,1,0:T(8,128)S(1)}, f32[2,496,128]{2,1,0:T(8,128)}, f32[2,496,128]{2,1,0:T(8,128)S(1)}, f32[2,...) custom-call(s32[2]{0:T(128)S(1)} %pad_add_fusion.pos, ...), custom_call_target="tpu_custom_call" | custom-call | flops 2000000000 | bytes 4000000 | tf_op jit(solution)/shard_map/pallas_call | solution.py:458
  18.5 2.9 %collective-permute-start.2 = (f32[2,384,128]{2,1,0:T(8,128)}, f32[2,384,128]{2,1,0:T(8,128)S(1)}, u32[]{:S(2)}, u32[]{:S(2)}) collective-permute-start(f32[2,384,128]{2,1,0:T(8,128)} %get-tuple-element.123), channel_id=1, source_target_pairs={{0,8},{4,20},{8,0},{12,28},{16,24},{20,4},{24,16},{28,12},{1,9},{5... | collective-permute-start | bytes 1179656 | tf_op jit(solution)/shard_map/ppermute | solution.py:332
  21.4 2.0 %collective-permute-start.4 = (f32[2,576,128]{2,1,0:T(8,128)}, f32[2,576,128]{2,1,0:T(8,128)S(1)}, u32[]{:S(2)}, u32[]{:S(2)}) collective-permute-start(f32[2,576,128]{2,1,0:T(8,128)} %copy-done.17), channel_id=1, source_target_pairs={{0,8},{4,20},{8,0},{12,28},{16,24},{20,4},{24,16},{28,12},{1,9},{5... | collective-permute-start | bytes 1769480 | tf_op jit(solution)/shard_map/ppermute | solution.py:332
  23.4 3.9 %collective-permute-done.2 = f32[2,384,128]{2,1,0:T(8,128)S(1)} collective-permute-done((f32[2,384,128]{2,1,0:T(8,128)}, f32[2,384,128]{2,1,0:T(8,128)S(1)}, u32[]{:S(2)}, u32[]{:S(2)}) %collective-permute-start.2) | collective-permute-done | bytes 393248 | tf_op jit(solution)/shard_map/ppermute | solution.py:332
  28.3 2.1 %collective-permute-start.5 = (f32[384,128]{1,0:T(8,128)S(1)}, f32[384,128]{1,0:T(8,128)S(1)}, u32[]{:S(2)}, u32[]{:S(2)}) collective-permute-start(f32[384,128]{1,0:T(8,128)S(1)} %fusion.2), channel_id=1, source_target_pairs={{0,16},{4,12},{8,24},{12,4},{16,0},{20,28},{24,8},{28,20},{1,17},{... | collective-permute-start | bytes 589832 | tf_op jit(solution)/shard_map/ppermute | solution.py:336
  30.4 4.5 %collective-permute-done.1 = f32[2,496,128]{2,1,0:T(8,128)S(1)} collective-permute-done((f32[2,496,128]{2,1,0:T(8,128)}, f32[2,496,128]{2,1,0:T(8,128)S(1)}, u32[]{:S(2)}, u32[]{:S(2)}) %collective-permute-start.1) | collective-permute-done | bytes 507936 | tf_op jit(solution)/shard_map/ppermute | solution.py:332
  36.0 2.1 %collective-permute-start.3 = (f32[496,128]{1,0:T(8,128)S(1)}, f32[496,128]{1,0:T(8,128)S(1)}, u32[]{:S(2)}, u32[]{:S(2)}) collective-permute-start(f32[496,128]{1,0:T(8,128)S(1)} %add_bitcast_fusion.1), channel_id=1, source_target_pairs={{0,16},{4,12},{8,24},{12,4},{16,0},{20,28},{24,8},{28,20},{1,17},{... | collective-permute-start | bytes 761864 | tf_op jit(solution)/shard_map/ppermute | solution.py:336
  39.8 4.2 %collective-permute-done.4 = f32[2,576,128]{2,1,0:T(8,128)S(1)} collective-permute-done((f32[2,576,128]{2,1,0:T(8,128)}, f32[2,576,128]{2,1,0:T(8,128)S(1)}, u32[]{:S(2)}, u32[]{:S(2)}) %collective-permute-start.4) | collective-permute-done | bytes 589856 | tf_op jit(solution)/shard_map/ppermute | solution.py:332
  44.0 2.1 %collective-permute-start.7 = (f32[576,128]{1,0:T(8,128)S(1)}, f32[576,128]{1,0:T(8,128)S(1)}, u32[]{:S(2)}, u32[]{:S(2)}) collective-permute-start(f32[576,128]{1,0:T(8,128)S(1)} %add_bitcast_fusion), channel_id=1, source_target_pairs={{0,16},{4,12},{8,24},{12,4},{16,0},{20,28},{24,8},{28,20},{1,17},{... | collective-permute-start | bytes 884744 | tf_op jit(solution)/shard_map/ppermute | solution.py:336
  47.7 2.7 %collective-permute-start.10 = (f32[192,128]{1,0:T(8,128)S(1)}, f32[192,128]{1,0:T(8,128)S(1)}, u32[]{:S(2)}, u32[]{:S(2)}) collective-permute-start(f32[192,128]{1,0:T(8,128)S(1)} %select_add_fusion.3), channel_id=1, source_target_pairs={{0,2},{1,3},{2,0},{3,1},{4,6},{5,7},{6,4},{7,5},{8,10},{9,11},{10,... | collective-permute-start | bytes 294920 | tf_op jit(solution)/shard_map/ppermute | solution.py:340
  56.4 2.7 %collective-permute-start.9 = (f32[248,128]{1,0:T(8,128)S(1)}, f32[248,128]{1,0:T(8,128)S(1)}, u32[]{:S(2)}, u32[]{:S(2)}) collective-permute-start(f32[248,128]{1,0:T(8,128)S(1)} %select_add_fusion.1), channel_id=1, source_target_pairs={{0,2},{1,3},{2,0},{3,1},{4,6},{5,7},{6,4},{7,5},{8,10},{9,11},{10,... | collective-permute-start | bytes 380936 | tf_op jit(solution)/shard_map/ppermute | solution.py:340
  67.0 3.1 %collective-permute-start.16 = (f32[288,128]{1,0:T(8,128)S(1)}, f32[288,128]{1,0:T(8,128)S(1)}, u32[]{:S(2)}, u32[]{:S(2)}) collective-permute-start(f32[288,128]{1,0:T(8,128)S(1)} %select_add_fusion), channel_id=1, source_target_pairs={{0,2},{1,3},{2,0},{3,1},{4,6},{5,7},{6,4},{7,5},{8,10},{9,11},{10,... | collective-permute-start | bytes 442376 | tf_op jit(solution)/shard_map/ppermute | solution.py:340
  70.0 2.3 %collective-permute-start.15 = (f32[248,128]{1,0:T(8,128)S(1)}, f32[248,128]{1,0:T(8,128)S(1)}, u32[]{:S(2)}, u32[]{:S(2)}) collective-permute-start(f32[248,128]{1,0:T(8,128)S(1)} %add.124), channel_id=1, source_target_pairs={{0,1},{1,0},{2,3},{3,2},{4,5},{5,4},{6,7},{7,6},{8,9},{9,8},{10,11... | collective-permute-start | bytes 380936 | tf_op jit(solution)/shard_map/ppermute | solution.py:340
  73.1 2.1 %collective-permute-done.15 = f32[248,128]{1,0:T(8,128)S(1)} collective-permute-done((f32[248,128]{1,0:T(8,128)S(1)}, f32[248,128]{1,0:T(8,128)S(1)}, u32[]{:S(2)}, u32[]{:S(2)}) %collective-permute-start.15) | collective-permute-done | bytes 127008 | tf_op jit(solution)/shard_map/ppermute | solution.py:340
  77.5 2.2 %collective-permute-start.23 = (f32[192,128]{1,0:T(8,128)S(1)}, f32[192,128]{1,0:T(8,128)S(1)}, u32[]{:S(2)}, u32[]{:S(2)}) collective-permute-start(f32[192,128]{1,0:T(8,128)S(1)} %get-tuple-element.165), channel_id=1, source_target_pairs={{0,2},{1,3},{2,0},{3,1},{4,6},{5,7},{6,4},{7,5},{8,10},{9,11},{10,... | collective-permute-start | bytes 294920 | tf_op jit(solution)/shard_map/ppermute | solution.py:340
  79.7 3.6 %collective-permute-done.23 = f32[192,128]{1,0:T(8,128)S(1)} collective-permute-done((f32[192,128]{1,0:T(8,128)S(1)}, f32[192,128]{1,0:T(8,128)S(1)}, u32[]{:S(2)}, u32[]{:S(2)}) %collective-permute-start.23) | collective-permute-done | bytes 98336 | tf_op jit(solution)/shard_map/ppermute | solution.py:340
  88.9 2.8 %collective-permute-start.28 = (f32[384,128]{1,0:T(8,128)S(1)}, f32[384,128]{1,0:T(8,128)S(1)}, u32[]{:S(2)}, u32[]{:S(2)}) collective-permute-start(f32[384,128]{1,0:T(8,128)S(1)} %get-tuple-element.182), channel_id=1, source_target_pairs={{0,16},{4,12},{8,24},{12,4},{16,0},{20,28},{24,8},{28,20},{1,17},{... | collective-permute-start | bytes 589832 | tf_op jit(solution)/shard_map/ppermute | solution.py:336
  91.7 6.0 %shard_map.191 = (f32[96,768]{1,0:T(8,128)}, f32[384,768]{1,0:T(8,128)S(1)}) custom-call(s32[2]{0:T(128)S(1)} %pad_add_fusion.pos, f32[2,384,128]{2,1,0:T(8,128)S(1)} %pad_maximum_fusion.2.refs_0_, f32[2,384,128]{2,1,0:T(8,128)S(1)} %collective-permute-done.21.refs_1_, f32[2,384,128]{2,1,0:T(8,128)S(1)} %collective-permute-done.19.refs_2_, ...), custom_call_target="tpu_custom_call" | custom-call | flops 2000000000 | bytes 4000000 | tf_op jit(solution)/shard_map/pallas_call | solution.py:482
  97.8 2.8 %collective-permute-done.31.refs_1_ = f32[2,496,128]{2,1,0:T(8,128)S(1)} collective-permute-done((f32[2,496,128]{2,1,0:T(8,128)S(1)}, f32[2,496,128]{2,1,0:T(8,128)S(1)}, u32[]{:S(2)}, u32[]{:S(2)}) %collective-permute-start.31) | collective-permute-done | bytes 507936 | tf_op jit(solution)/shard_map/ppermute | solution.py:332
  102.9 8.2 %shard_map.192 = (f32[96,768]{1,0:T(8,128)}, f32[16,128]{1,0:T(8,128)}, f32[96,128]{1,0:T(8,128)S(1)}, f32[8,128]{1,0:T(8,128)S(1)}) custom-call(s32[2]{0:T(128)S(1)} %pad_add_fusion.pos, f32[2,496,128]{2,1,0:T(8,128)S(1)} %pad_maximum_fusion.1.refs_0_, f32[2,496,128]{2,1,0:T(8,128)S(1)} %collective-permute-done.31.refs_1_, ...), custom_call_target="tpu_custom_call" | custom-call | flops 3000000000 | bytes 4000000 | tf_op jit(solution)/shard_map/pallas_call | solution.py:487
  111.1 3.6 %collective-permute-done.35.refs_1_ = f32[2,384,128]{2,1,0:T(8,128)S(1)} collective-permute-done((f32[2,384,128]{2,1,0:T(8,128)S(1)}, f32[2,384,128]{2,1,0:T(8,128)S(1)}, u32[]{:S(2)}, u32[]{:S(2)}) %collective-permute-start.35) | collective-permute-done | bytes 393248 | tf_op jit(solution)/shard_map/ppermute | solution.py:332
  114.8 2.7 %shard_map.193 = (f32[384,768]{1,0:T(8,128)S(1)}, f32[384,768]{1,0:T(8,128)S(1)}) custom-call(s32[2]{0:T(128)S(1)} %pad_add_fusion.pos, f32[384,768]{1,0:T(8,128)S(1)} %get-tuple-element.180.x_ref, f32[2,576,128]{2,1,0:T(8,128)S(1)} %pad_maximum_fusion.refs_0_, f32[2,576,128]{2,1,0:T(8,128)S(1)} %collective-permute-done.29.refs_1_, ...), custom_call_target="tpu_custom_call" | custom-call | flops 1000000000 | bytes 4000000 | tf_op jit(solution)/shard_map/pallas_call | solution.py:495
  117.6 7.7 %shard_map.194 = (f32[96,768]{1,0:T(8,128)}, f32[96,768]{1,0:T(8,128)S(1)}, f32[8,128]{1,0:T(8,128)S(1)}) custom-call(s32[2]{0:T(128)S(1)} %pad_add_fusion.pos, f32[384,768]{1,0:T(8,128)S(1)} %get-tuple-element.200.t_ref, f32[384,768]{1,0:T(8,128)S(1)} %get-tuple-element.201.rows_ref, f32[2,384,128]{2,1,0:T(8,128)S(1)} %pad_maximum_fusion.3.refs_0_, ...), custom_call_target="tpu_custom_call" | custom-call | flops 3000000000 | bytes 4000000 | tf_op jit(solution)/shard_map/pallas_call | solution.py:500
  (133 shorter events, 41.6 us)
Async XLA Ops:
  18.5 8.8 %collective-permute-start.2 = (f32[2,384,128]{2,1,0:T(8,128)}, f32[2,384,128]{2,1,0:T(8,128)S(1)}, u32[]{:S(2)}, u32[]{:S(2)}) collective-permute-start(f32[2,384,128]{2,1,0:T(8,128)} %get-tuple-element.123), channel_id=1, source_target_pairs={{0,8},{4,20},{8,0},{12,28},{16,24},{20,4},{24,16},{28,12},{1,9},{5... | collective-permute-start | bytes 1179656 | tf_op jit(solution)/shard_map/ppermute | solution.py:332
  21.4 13.5 %collective-permute-start.1 = (f32[2,496,128]{2,1,0:T(8,128)}, f32[2,496,128]{2,1,0:T(8,128)S(1)}, u32[]{:S(2)}, u32[]{:S(2)}) collective-permute-start(f32[2,496,128]{2,1,0:T(8,128)} %get-tuple-element.122), channel_id=1, source_target_pairs={{0,8},{4,20},{8,0},{12,28},{16,24},{20,4},{24,16},{28,12},{1,9},{5... | collective-permute-start | bytes 1523720 | tf_op jit(solution)/shard_map/ppermute | solution.py:332
  21.4 22.5 %collective-permute-start.4 = (f32[2,576,128]{2,1,0:T(8,128)}, f32[2,576,128]{2,1,0:T(8,128)S(1)}, u32[]{:S(2)}, u32[]{:S(2)}) collective-permute-start(f32[2,576,128]{2,1,0:T(8,128)} %copy-done.17), channel_id=1, source_target_pairs={{0,8},{4,20},{8,0},{12,28},{16,24},{20,4},{24,16},{28,12},{1,9},{5... | collective-permute-start | bytes 1769480 | tf_op jit(solution)/shard_map/ppermute | solution.py:332
  28.3 9.8 %collective-permute-start.5 = (f32[384,128]{1,0:T(8,128)S(1)}, f32[384,128]{1,0:T(8,128)S(1)}, u32[]{:S(2)}, u32[]{:S(2)}) collective-permute-start(f32[384,128]{1,0:T(8,128)S(1)} %fusion.2), channel_id=1, source_target_pairs={{0,16},{4,12},{8,24},{12,4},{16,0},{20,28},{24,8},{28,20},{1,17},{... | collective-permute-start | bytes 589832 | tf_op jit(solution)/shard_map/ppermute | solution.py:336
  36.0 11.6 %collective-permute-start.3 = (f32[496,128]{1,0:T(8,128)S(1)}, f32[496,128]{1,0:T(8,128)S(1)}, u32[]{:S(2)}, u32[]{:S(2)}) collective-permute-start(f32[496,128]{1,0:T(8,128)S(1)} %add_bitcast_fusion.1), channel_id=1, source_target_pairs={{0,16},{4,12},{8,24},{12,4},{16,0},{20,28},{24,8},{28,20},{1,17},{... | collective-permute-start | bytes 761864 | tf_op jit(solution)/shard_map/ppermute | solution.py:336
  38.1 9.5 %collective-permute-start.8 = (f32[192,128]{1,0:T(8,128)S(1)}, f32[192,128]{1,0:T(8,128)S(1)}, u32[]{:S(2)}, u32[]{:S(2)}) collective-permute-start(f32[192,128]{1,0:T(8,128)S(1)} %slice_select_fusion.3), channel_id=1, source_target_pairs={{0,1},{1,0},{2,3},{3,2},{4,5},{5,4},{6,7},{7,6},{8,9},{9,8},{10,11... | collective-permute-start | bytes 294920 | tf_op jit(solution)/shard_map/ppermute | solution.py:340
  44.0 9.1 %collective-permute-start.7 = (f32[576,128]{1,0:T(8,128)S(1)}, f32[576,128]{1,0:T(8,128)S(1)}, u32[]{:S(2)}, u32[]{:S(2)}) collective-permute-start(f32[576,128]{1,0:T(8,128)S(1)} %add_bitcast_fusion), channel_id=1, source_target_pairs={{0,16},{4,12},{8,24},{12,4},{16,0},{20,28},{24,8},{28,20},{1,17},{... | collective-permute-start | bytes 884744 | tf_op jit(solution)/shard_map/ppermute | solution.py:336
  46.1 9.2 %collective-permute-start.11 = (f32[2,384,128]{2,1,0:T(8,128)S(1)}, f32[2,384,128]{2,1,0:T(8,128)S(1)}, u32[]{:S(2)}, u32[]{:S(2)}) collective-permute-start(f32[2,384,128]{2,1,0:T(8,128)S(1)} %copy-done.19), channel_id=1, source_target_pairs={{0,8},{4,20},{8,0},{12,28},{16,24},{20,4},{24,16},{28,12},{1,9},{5... | collective-permute-start | bytes 1179656 | tf_op jit(solution)/shard_map/ppermute | solution.py:332
  47.7 11.4 %collective-permute-start.10 = (f32[192,128]{1,0:T(8,128)S(1)}, f32[192,128]{1,0:T(8,128)S(1)}, u32[]{:S(2)}, u32[]{:S(2)}) collective-permute-start(f32[192,128]{1,0:T(8,128)S(1)} %select_add_fusion.3), channel_id=1, source_target_pairs={{0,2},{1,3},{2,0},{3,1},{4,6},{5,7},{6,4},{7,5},{8,10},{9,11},{10,... | collective-permute-start | bytes 294920 | tf_op jit(solution)/shard_map/ppermute | solution.py:340
  53.1 7.3 %collective-permute-start.14 = (f32[288,128]{1,0:T(8,128)S(1)}, f32[288,128]{1,0:T(8,128)S(1)}, u32[]{:S(2)}, u32[]{:S(2)}) collective-permute-start(f32[288,128]{1,0:T(8,128)S(1)} %slice_select_fusion), channel_id=1, source_target_pairs={{0,1},{1,0},{2,3},{3,2},{4,5},{5,4},{6,7},{7,6},{8,9},{9,8},{10,11... | collective-permute-start | bytes 442376 | tf_op jit(solution)/shard_map/ppermute | solution.py:340
  56.4 7.6 %collective-permute-start.9 = (f32[248,128]{1,0:T(8,128)S(1)}, f32[248,128]{1,0:T(8,128)S(1)}, u32[]{:S(2)}, u32[]{:S(2)}) collective-permute-start(f32[248,128]{1,0:T(8,128)S(1)} %select_add_fusion.1), channel_id=1, source_target_pairs={{0,2},{1,3},{2,0},{3,1},{4,6},{5,7},{6,4},{7,5},{8,10},{9,11},{10,... | collective-permute-start | bytes 380936 | tf_op jit(solution)/shard_map/ppermute | solution.py:340
  65.9 6.4 %collective-permute-start.17 = (f32[384,128]{1,0:T(8,128)S(1)}, f32[384,128]{1,0:T(8,128)S(1)}, u32[]{:S(2)}, u32[]{:S(2)}) collective-permute-start(f32[384,128]{1,0:T(8,128)S(1)} %get-tuple-element.155), channel_id=1, source_target_pairs={{0,16},{4,12},{8,24},{12,4},{16,0},{20,28},{24,8},{28,20},{1,17},{... | collective-permute-start | bytes 589832 | tf_op jit(solution)/shard_map/ppermute | solution.py:336
  67.0 6.2 %collective-permute-start.16 = (f32[288,128]{1,0:T(8,128)S(1)}, f32[288,128]{1,0:T(8,128)S(1)}, u32[]{:S(2)}, u32[]{:S(2)}) collective-permute-start(f32[288,128]{1,0:T(8,128)S(1)} %select_add_fusion), channel_id=1, source_target_pairs={{0,2},{1,3},{2,0},{3,1},{4,6},{5,7},{6,4},{7,5},{8,10},{9,11},{10,... | collective-permute-start | bytes 442376 | tf_op jit(solution)/shard_map/ppermute | solution.py:340
  72.4 10.9 %collective-permute-start.21 = (f32[2,384,128]{2,1,0:T(8,128)S(1)}, f32[2,384,128]{2,1,0:T(8,128)S(1)}, u32[]{:S(2)}, u32[]{:S(2)}) collective-permute-start(f32[2,384,128]{2,1,0:T(8,128)S(1)} %pad_maximum_fusion.2.refs_0_), channel_id=1, source_target_pairs={{0,8},{4,20},{8,0},{12,28},{16,24},{20,4},{24,16},{28,12},{1,9},{5... | collective-permute-start | bytes 1179656 | tf_op jit(solution)/shard_map/ppermute | solution.py:332
  75.3 8.0 %collective-permute-start.20 = (f32[496,128]{1,0:T(8,128)S(1)}, f32[496,128]{1,0:T(8,128)S(1)}, u32[]{:S(2)}, u32[]{:S(2)}) collective-permute-start(f32[496,128]{1,0:T(8,128)S(1)} %get-tuple-element.163), channel_id=1, source_target_pairs={{0,16},{4,12},{8,24},{12,4},{16,0},{20,28},{24,8},{28,20},{1,17},{... | collective-permute-start | bytes 761864 | tf_op jit(solution)/shard_map/ppermute | solution.py:336
  75.9 7.4 %collective-permute-start.22 = (f32[288,128]{1,0:T(8,128)S(1)}, f32[288,128]{1,0:T(8,128)S(1)}, u32[]{:S(2)}, u32[]{:S(2)}) collective-permute-start(f32[288,128]{1,0:T(8,128)S(1)} %add.129), channel_id=1, source_target_pairs={{0,1},{1,0},{2,3},{3,2},{4,5},{5,4},{6,7},{7,6},{8,9},{9,8},{10,11... | collective-permute-start | bytes 442376 | tf_op jit(solution)/shard_map/ppermute | solution.py:340
  77.5 5.8 %collective-permute-start.23 = (f32[192,128]{1,0:T(8,128)S(1)}, f32[192,128]{1,0:T(8,128)S(1)}, u32[]{:S(2)}, u32[]{:S(2)}) collective-permute-start(f32[192,128]{1,0:T(8,128)S(1)} %get-tuple-element.165), channel_id=1, source_target_pairs={{0,2},{1,3},{2,0},{3,1},{4,6},{5,7},{6,4},{7,5},{8,10},{9,11},{10,... | collective-permute-start | bytes 294920 | tf_op jit(solution)/shard_map/ppermute | solution.py:340
  83.4 8.3 %collective-permute-start.24 = (f32[2,496,128]{2,1,0:T(8,128)S(1)}, f32[2,496,128]{2,1,0:T(8,128)S(1)}, u32[]{:S(2)}, u32[]{:S(2)}) collective-permute-start(f32[2,496,128]{2,1,0:T(8,128)S(1)} %pad_maximum_fusion.1.refs_0_), channel_id=1, source_target_pairs={{0,4},{4,0},{8,12},{12,8},{16,20},{20,16},{24,28},{28,24},{1,5},{5... | collective-permute-start | bytes 1523720 | tf_op jit(solution)/shard_map/ppermute | solution.py:328
  85.5 12.2 %collective-permute-start.27 = (f32[576,128]{1,0:T(8,128)S(1)}, f32[576,128]{1,0:T(8,128)S(1)}, u32[]{:S(2)}, u32[]{:S(2)}) collective-permute-start(f32[576,128]{1,0:T(8,128)S(1)} %get-tuple-element.178), channel_id=1, source_target_pairs={{0,16},{4,12},{8,24},{12,4},{16,0},{20,28},{24,8},{28,20},{1,17},{... | collective-permute-start | bytes 884744 | tf_op jit(solution)/shard_map/ppermute | solution.py:336
  88.9 8.8 %collective-permute-start.28 = (f32[384,128]{1,0:T(8,128)S(1)}, f32[384,128]{1,0:T(8,128)S(1)}, u32[]{:S(2)}, u32[]{:S(2)}) collective-permute-start(f32[384,128]{1,0:T(8,128)S(1)} %get-tuple-element.182), channel_id=1, source_target_pairs={{0,16},{4,12},{8,24},{12,4},{16,0},{20,28},{24,8},{28,20},{1,17},{... | collective-permute-start | bytes 589832 | tf_op jit(solution)/shard_map/ppermute | solution.py:336
  91.7 9.0 %collective-permute-start.31 = (f32[2,496,128]{2,1,0:T(8,128)S(1)}, f32[2,496,128]{2,1,0:T(8,128)S(1)}, u32[]{:S(2)}, u32[]{:S(2)}) collective-permute-start(f32[2,496,128]{2,1,0:T(8,128)S(1)} %pad_maximum_fusion.1.refs_0_), channel_id=1, source_target_pairs={{0,8},{4,20},{8,0},{12,28},{16,24},{20,4},{24,16},{28,12},{1,9},{5... | collective-permute-start | bytes 1523720 | tf_op jit(solution)/shard_map/ppermute | solution.py:332
  100.7 10.4 %collective-permute-start.29 = (f32[2,576,128]{2,1,0:T(8,128)S(1)}, f32[2,576,128]{2,1,0:T(8,128)S(1)}, u32[]{:S(2)}, u32[]{:S(2)}) collective-permute-start(f32[2,576,128]{2,1,0:T(8,128)S(1)} %pad_maximum_fusion.refs_0_), channel_id=1, source_target_pairs={{0,8},{4,20},{8,0},{12,28},{16,24},{20,4},{24,16},{28,12},{1,9},{5... | collective-permute-start | bytes 1769480 | tf_op jit(solution)/shard_map/ppermute | solution.py:332
  101.2 9.8 %collective-permute-start.32 = (f32[2,384,128]{2,1,0:T(8,128)S(1)}, f32[2,384,128]{2,1,0:T(8,128)S(1)}, u32[]{:S(2)}, u32[]{:S(2)}) collective-permute-start(f32[2,384,128]{2,1,0:T(8,128)S(1)} %pad_maximum_fusion.3.refs_0_), channel_id=1, source_target_pairs={{0,4},{4,0},{8,12},{12,8},{16,20},{20,16},{24,28},{28,24},{1,5},{5... | collective-permute-start | bytes 1179656 | tf_op jit(solution)/shard_map/ppermute | solution.py:328
  101.9 12.9 %collective-permute-start.35 = (f32[2,384,128]{2,1,0:T(8,128)S(1)}, f32[2,384,128]{2,1,0:T(8,128)S(1)}, u32[]{:S(2)}, u32[]{:S(2)}) collective-permute-start(f32[2,384,128]{2,1,0:T(8,128)S(1)} %pad_maximum_fusion.3.refs_0_), channel_id=1, source_target_pairs={{0,8},{4,20},{8,0},{12,28},{16,24},{20,4},{24,16},{28,12},{1,9},{5... | collective-permute-start | bytes 1179656 | tf_op jit(solution)/shard_map/ppermute | solution.py:332
  (34 other events, 162.1 us)

commit v6 on v5

--- a/solution.py
+++ b/solution.py
@@ -65,7 +65,10 @@
     return values.astype(F32).T.astype(BF16)
 
 
-def own_kernel(tokens, samples, D, mine, y_aq, y_gq, y_akv, y_gkv, u_aq, u_gq, u_akv, u_gkv, t_q, t_kv):
+def own_kernel(
+    tokens, samples, D,
+    mine, y_aq, y_gq, y_akv, y_gkv, u_aq, u_gq, u_akv, u_gkv, t_q, t_kv, e_q, e_kv,
+):
     pick = picker(mine, tokens, samples)
     at = 0
     for y, u in ((y_aq, u_aq), (y_gq, u_gq), (y_akv, u_akv), (y_gkv, u_gkv)):
@@ -75,6 +78,8 @@
         at += y.shape[1]
     t_q[...] = turned(mine[:tokens, :D])
     t_kv[...] = turned(mine[:tokens, 2 * D:3 * D])
+    e_q[...] = mine[:tokens, D:2 * D].astype(BF16)
+    e_kv[...] = mine[:tokens, 3 * D:].astype(BF16)
 
 
 def roles(q, c):
@@ -113,7 +118,7 @@
 
 def gram_kernel(
     n, k, width, scale,
-    pos, mine, other, y_aq, y_gq, y_akv, y_gkv, o_aq, o_gq, o_akv, o_gkv, o_q, o_kv,
+    pos, e_q, e_kv, other, y_aq, y_gq, y_akv, y_gkv, o_aq, o_gq, o_akv, o_gkv, o_q, o_kv,
     st_aq, st_gq, st_akv, st_gkv,
     a_send, a_keep, k_send, k_keep, s_send, s_keep, g_send, g_keep,
     u_aq, u_gq, u_akv, u_gkv, t_q, t_kv, g_kv,
@@ -127,22 +132,22 @@
         chosen = join(u, other, pick, o, y, lo, lo + D)
         return factor_tiles(u, chosen, state, n, blocks, width, scale)
 
-    def gradient(t, o, lo, first, last):
+    def gradient(t, o, lo, end, first, last):
         t[:, :tokens] = o[...]
         t[:, tokens:] = turned(other[:tokens, lo:lo + D])
-        ends = [ref[:tokens, first:last].astype(BF16) for ref in (mine, other)]
+        ends = [end[...], other[:tokens, first:last].astype(BF16)]
         return four(product(left_blocks(t, n, blocks), jnp.concatenate(ends, axis=0)), n)
 
     place(a_send, a_keep, factor(u_aq, o_aq, y_aq, st_aq, 0))
     at = place(k_send, k_keep, factor(u_akv, o_akv, y_akv, st_akv, 2 * D))
-    sums = gradient(t_kv, o_kv, 2 * D, 3 * D, 3 * D + KV)
+    sums = gradient(t_kv, o_kv, 2 * D, e_kv, 3 * D, 3 * D + KV)
     at = place(k_send, k_keep, [[part] for part in sums], at)
     chosen = join(u_gkv, other, pick, o_gkv, y_gkv, 3 * D, 3 * D + KV)
     g_kv[...] = product(u_gkv[...], chosen) * scale
     small = [g_kv[pl.ds(pl.multiple_of(k * b, 8), k), :] for b in blocks]
     small[0] = small[0] + (BLEND_RATE / 4.0) * st_gkv[...]
     place(k_send, k_keep, [[part] for part in small], at)
-    place(s_send, s_keep, [plain_tiles(part) for part in gradient(t_q, o_q, 0, D, 2 * D)])
+    place(s_send, s_keep, [plain_tiles(part) for part in gradient(t_q, o_q, 0, e_q, D, 2 * D)])
     place(g_send, g_keep, factor(u_gq, o_gq, y_gq, st_gq, D))
 
 
@@ -446,10 +451,10 @@
         sample_rows.reshape(1, samples), act_query, grad_query, act_keyval, grad_keyval
     )
     other = core_flip(mine)
-    y_aq, y_gq, y_akv, y_gkv, u_aq, u_gq, u_akv, u_gkv, t_q, t_kv = call(
+    y_aq, y_gq, y_akv, y_gkv, u_aq, u_gq, u_akv, u_gkv, t_q, t_kv, e_q, e_kv = call(
         functools.partial(own_kernel, tokens, samples, D),
         [(samples, D)] * 3 + [(samples, KV)] + [(D, samples)] * 3 + [(KV, samples)]
-        + [(D, tokens)] * 2,
+        + [(D, tokens)] * 2 + [(tokens, D), (tokens, KV)],
         [], 1, 300_000_000, scalars=0, kind=BF16, limit=12,
     )(mine)
 
@@ -462,9 +467,9 @@
             *[((D, 2 * samples), BF16)] * 3, ((KV, 2 * samples), BF16),
             *[((D, 2 * tokens), BF16)] * 2, ((KV, KV), F32),
         ],
-        17, 2_000_000_000, limit=16,
+        18, 2_000_000_000, limit=16,
     )(
-        pos, mine, other, y_aq, y_gq, y_akv, y_gkv, u_aq, u_gq, u_akv, u_gkv, t_q, t_kv,
+        pos, e_q, e_kv, other, y_aq, y_gq, y_akv, y_gkv, u_aq, u_gq, u_akv, u_gkv, t_q, t_kv,
         state_aq, state_gq, state_akv, state_gkv,
     )
     sends, keeps = dict(zip("AKSG", grams[0::2])), dict(zip("AKSG", grams[1::2]))

time: 128 us -> 127 us (level)
  waiting for transfers between devices: 37.3 us -> 51.8 us
  starting transfers between devices: 47.6 us -> 33.4 us
  local copies, waits for them, and re-layouts: 7.67 us -> 4.51 us
  other arithmetic: 2.91 us -> 4.7 us
    ppermute x12, starting transfers between devices: 23.8 us -> 12.9 us  [plane_flip(): return lax.ppermute(value, 'group', [(i, i ^ bit) for i in range(4)])]
    ppermute x12, waiting for transfers between devices: 11.8 us -> 20.3 us  [plane_flip(): return lax.ppermute(value, 'group', [(i, i ^ bit) for i in range(4)])]
    ppermute x8, waiting for transfers between devices: 1.72 us -> 8.03 us  [second_hop(): lax.ppermute(value, 'dp', [(i, i ^ (2 if i & 1 else 4)) for i in range(8)])]
    ppermute x8, starting transfers between devices: 13.3 us -> 8.6 us  [second_hop(): lax.ppermute(value, 'dp', [(i, i ^ (2 if i & 1 else 4)) for i in range(8)])]
    unnamed x40 -> x26, local copies, waits for them, and re-layouts: 7.67 us -> 4.51 us
    add x4, other arithmetic: 0.18 us -> 2.05 us  [operand(): own = self.keeps[chunk][0] + got[chunk, 'rs1'][0] + got[chunk, 'rs2']]
    ppermute x8, starting transfers between devices: 8.24 us -> 10.1 us  [first_hop(): lax.ppermute(value, 'dp', [(i, i ^ (4 if i & 1 else 2)) for i in range(8)])]
  transfers between devices with their start and end apart: 38 -> 38, of which waited for: 17 -> 21; matrix products, arithmetic and copies ran while one was open for 2% -> 4% of each run, Pallas kernels for 14% -> 14%
where the time goes in v6:
time: 127 us
  waiting for transfers between devices  51.8 us (41%)
  starting transfers between devices  33.4 us (26%)
  Pallas kernels  31.1 us (24%)
  other arithmetic  4.7 us (4%)
  local copies, waits for them, and re-layouts  4.51 us (4%)
    ppermute x12, waiting for transfers between devices, plane_flip(): return lax.ppermute(value, 'group', [(i, i ^ bit) for i in range(4)])  20.3 us
    ppermute x8, waiting for transfers between devices, first_hop(): lax.ppermute(value, 'dp', [(i, i ^ (4 if i & 1 else 2)) for i in range(8)])  18.1 us
    ppermute x12, starting transfers between devices, plane_flip(): return lax.ppermute(value, 'group', [(i, i ^ bit) for i in range(4)])  12.9 us
    ppermute x8, starting transfers between devices, first_hop(): lax.ppermute(value, 'dp', [(i, i ^ (4 if i & 1 else 2)) for i in range(8)])  10.1 us
    ppermute x8, starting transfers between devices, second_hop(): lax.ppermute(value, 'dp', [(i, i ^ (2 if i & 1 else 4)) for i in range(8)])  8.6 us
    pallas_call x1, Pallas kernels, fast_shards(): call(functools.partial(keyval_kernel, n, k, width), [(n, D), (k, KV), (n,...  8.13 us
    ppermute x8, waiting for transfers between devices, second_hop(): lax.ppermute(value, 'dp', [(i, i ^ (2 if i & 1 else 4)) for i in range(8)])  8.03 us
    pallas_call x1, Pallas kernels, fast_shards(): call(functools.partial(right_kernel, n, width), [(n, D), (n, D), fit], sq...  7.68 us
  transfers between devices with their start and end apart: 38, of which 21 were waited for; matrix products, arithmetic and copies ran while one was open for 4% of the time, Pallas kernels for 14%

profile of v6, /device:TPU:0, one launch (start us, length us, event | category | flops | bytes accessed | tf_op | source)
XLA Modules:
  0.0 126.5 jit_solution(15269923610786838080)
XLA Ops:
  6.5 3.9 %collective-permute-done.other = f32[264,2432]{1,0:T(8,128)} collective-permute-done((f32[264,2432]{1,0:T(8,128)S(1)}, f32[264,2432]{1,0:T(8,128)}, u32[]{:S(2)}, u32[]{:S(2)}) %collective-permute-start) | collective-permute-done | bytes 2568224 | tf_op jit(solution)/shard_map/ppermute | solution.py:333
  10.4 4.8 %shard_map.190 = (f32[2,384,128]{2,1,0:T(8,128)}, f32[2,384,128]{2,1,0:T(8,128)S(1)}, f32[2,496,128]{2,1,0:T(8,128)S(1)}, f32[2,496,128]{2,1,0:T(8,128)S(1)}, f3...) custom-call(s32[2]{0:T(128)S(1)} %pad_add_fusion.pos, ...), custom_call_target="tpu_custom_call" | custom-call | flops 2000000000 | bytes 4000000 | tf_op jit(solution)/shard_map/pallas_call | solution.py:463
  15.3 2.9 %collective-permute-start.2 = (f32[2,384,128]{2,1,0:T(8,128)}, f32[2,384,128]{2,1,0:T(8,128)}, u32[]{:S(2)}, u32[]{:S(2)}) collective-permute-start(f32[2,384,128]{2,1,0:T(8,128)} %get-tuple-element.127), channel_id=1, source_target_pairs={{0,8},{4,20},{8,0},{12,28},{16,24},{20,4},{24,16},{28,12},{1,9},{5... | collective-permute-start | bytes 1179656 | tf_op jit(solution)/shard_map/ppermute | solution.py:337
  18.2 2.0 %collective-permute-start.4 = (f32[2,576,128]{2,1,0:T(8,128)S(1)}, f32[2,576,128]{2,1,0:T(8,128)S(1)}, u32[]{:S(2)}, u32[]{:S(2)}) collective-permute-start(f32[2,576,128]{2,1,0:T(8,128)S(1)} %get-tuple-element.130), channel_id=1, source_target_pairs={{0,8},{4,20},{8,0},{12,28},{16,24},{20,4},{24,16},{28,12},{1,9},{5... | collective-permute-start | bytes 1769480 | tf_op jit(solution)/shard_map/ppermute | solution.py:337
  20.2 4.0 %collective-permute-done.2 = f32[2,384,128]{2,1,0:T(8,128)} collective-permute-done((f32[2,384,128]{2,1,0:T(8,128)}, f32[2,384,128]{2,1,0:T(8,128)}, u32[]{:S(2)}, u32[]{:S(2)}) %collective-permute-start.2) | collective-permute-done | bytes 393248 | tf_op jit(solution)/shard_map/ppermute | solution.py:337
  25.1 2.1 %collective-permute-start.5 = (f32[384,128]{1,0:T(8,128)S(1)}, f32[384,128]{1,0:T(8,128)S(1)}, u32[]{:S(2)}, u32[]{:S(2)}) collective-permute-start(f32[384,128]{1,0:T(8,128)S(1)} %fusion.2), channel_id=1, source_target_pairs={{0,16},{4,12},{8,24},{12,4},{16,0},{20,28},{24,8},{28,20},{1,17},{... | collective-permute-start | bytes 589832 | tf_op jit(solution)/shard_map/ppermute | solution.py:341
  27.3 4.4 %collective-permute-done.1 = f32[2,496,128]{2,1,0:T(8,128)} collective-permute-done((f32[2,496,128]{2,1,0:T(8,128)S(1)}, f32[2,496,128]{2,1,0:T(8,128)}, u32[]{:S(2)}, u32[]{:S(2)}) %collective-permute-start.1) | collective-permute-done | bytes 507936 | tf_op jit(solution)/shard_map/ppermute | solution.py:337
  32.7 2.1 %collective-permute-start.3 = (f32[496,128]{1,0:T(8,128)S(1)}, f32[496,128]{1,0:T(8,128)S(1)}, u32[]{:S(2)}, u32[]{:S(2)}) collective-permute-start(f32[496,128]{1,0:T(8,128)S(1)} %add_bitcast_fusion.1), channel_id=1, source_target_pairs={{0,16},{4,12},{8,24},{12,4},{16,0},{20,28},{24,8},{28,20},{1,17},{... | collective-permute-start | bytes 761864 | tf_op jit(solution)/shard_map/ppermute | solution.py:341
  37.5 3.2 %collective-permute-done.4 = f32[2,576,128]{2,1,0:T(8,128)S(1)} collective-permute-done((f32[2,576,128]{2,1,0:T(8,128)S(1)}, f32[2,576,128]{2,1,0:T(8,128)S(1)}, u32[]{:S(2)}, u32[]{:S(2)}) %collective-permute-start.4) | collective-permute-done | bytes 589856 | tf_op jit(solution)/shard_map/ppermute | solution.py:337
  40.7 2.1 %collective-permute-start.7 = (f32[576,128]{1,0:T(8,128)S(1)}, f32[576,128]{1,0:T(8,128)S(1)}, u32[]{:S(2)}, u32[]{:S(2)}) collective-permute-start(f32[576,128]{1,0:T(8,128)S(1)} %add_bitcast_fusion), channel_id=1, source_target_pairs={{0,16},{4,12},{8,24},{12,4},{16,0},{20,28},{24,8},{28,20},{1,17},{... | collective-permute-start | bytes 884744 | tf_op jit(solution)/shard_map/ppermute | solution.py:341
  45.4 2.7 %collective-permute-start.10 = (f32[192,128]{1,0:T(8,128)S(1)}, f32[192,128]{1,0:T(8,128)S(1)}, u32[]{:S(2)}, u32[]{:S(2)}) collective-permute-start(f32[192,128]{1,0:T(8,128)S(1)} %select_add_fusion.3), channel_id=1, source_target_pairs={{0,2},{1,3},{2,0},{3,1},{4,6},{5,7},{6,4},{7,5},{8,10},{9,11},{10,... | collective-permute-start | bytes 294920 | tf_op jit(solution)/shard_map/ppermute | solution.py:345
  48.0 1.6 %collective-permute-start.6 = (f32[248,128]{1,0:T(8,128)S(1)}, f32[248,128]{1,0:T(8,128)S(1)}, u32[]{:S(2)}, u32[]{:S(2)}) collective-permute-start(f32[248,128]{1,0:T(8,128)S(1)} %slice_select_fusion.1), channel_id=1, source_target_pairs={{0,1},{1,0},{2,3},{3,2},{4,5},{5,4},{6,7},{7,6},{8,9},{9,8},{10,11... | collective-permute-start | bytes 380936 | tf_op jit(solution)/shard_map/ppermute | solution.py:345
  51.5 2.9 %collective-permute-done.6 = f32[248,128]{1,0:T(8,128)S(1)} collective-permute-done((f32[248,128]{1,0:T(8,128)S(1)}, f32[248,128]{1,0:T(8,128)S(1)}, u32[]{:S(2)}, u32[]{:S(2)}) %collective-permute-start.6) | collective-permute-done | bytes 127008 | tf_op jit(solution)/shard_map/ppermute | solution.py:345
  57.5 2.7 %collective-permute-done.13 = f32[384,128]{1,0:T(8,128)S(1)} collective-permute-done((f32[384,128]{1,0:T(8,128)S(1)}, f32[384,128]{1,0:T(8,128)S(1)}, u32[]{:S(2)}, u32[]{:S(2)}) %collective-permute-start.13) | collective-permute-done | bytes 196640 | tf_op jit(solution)/shard_map/ppermute | solution.py:341
  61.8 5.7 %collective-permute-done.18 = f32[192,128]{1,0:T(8,128)S(1)} collective-permute-done((f32[192,128]{1,0:T(8,128)S(1)}, f32[192,128]{1,0:T(8,128)S(1)}, u32[]{:S(2)}, u32[]{:S(2)}) %collective-permute-start.18) | collective-permute-done | bytes 98336 | tf_op jit(solution)/shard_map/ppermute | solution.py:345
  68.3 5.0 %collective-permute-done.17 = f32[384,128]{1,0:T(8,128)S(1)} collective-permute-done((f32[384,128]{1,0:T(8,128)S(1)}, f32[384,128]{1,0:T(8,128)S(1)}, u32[]{:S(2)}, u32[]{:S(2)}) %collective-permute-start.17) | collective-permute-done | bytes 196640 | tf_op jit(solution)/shard_map/ppermute | solution.py:341
  78.0 4.4 %collective-permute-done.23 = f32[192,128]{1,0:T(8,128)S(1)} collective-permute-done((f32[192,128]{1,0:T(8,128)S(1)}, f32[192,128]{1,0:T(8,128)S(1)}, u32[]{:S(2)}, u32[]{:S(2)}) %collective-permute-start.23) | collective-permute-done | bytes 98336 | tf_op jit(solution)/shard_map/ppermute | solution.py:345
  85.5 4.0 %collective-permute-done.26 = f32[192,128]{1,0:T(8,128)S(1)} collective-permute-done((f32[192,128]{1,0:T(8,128)S(1)}, f32[192,128]{1,0:T(8,128)S(1)}, u32[]{:S(2)}, u32[]{:S(2)}) %collective-permute-start.26) | collective-permute-done | bytes 98336 | tf_op jit(solution)/shard_map/ppermute | solution.py:345
  91.1 6.0 %shard_map.191 = (f32[96,768]{1,0:T(8,128)}, f32[384,768]{1,0:T(8,128)S(1)}) custom-call(s32[2]{0:T(128)S(1)} %pad_add_fusion.pos, f32[2,384,128]{2,1,0:T(8,128)S(1)} %pad_maximum_fusion.2.refs_0_, f32[2,384,128]{2,1,0:T(8,128)S(1)} %collective-permute-done.21.refs_1_, f32[2,384,128]{2,1,0:T(8,128)S(1)} %collective-permute-done.19.refs_2_, ...), custom_call_target="tpu_custom_call" | custom-call | flops 2000000000 | bytes 4000000 | tf_op jit(solution)/shard_map/pallas_call | solution.py:487
  97.5 1.9 %collective-permute-done.31.refs_1_ = f32[2,496,128]{2,1,0:T(8,128)S(1)} collective-permute-done((f32[2,496,128]{2,1,0:T(8,128)S(1)}, f32[2,496,128]{2,1,0:T(8,128)S(1)}, u32[]{:S(2)}, u32[]{:S(2)}) %collective-permute-start.31) | collective-permute-done | bytes 507936 | tf_op jit(solution)/shard_map/ppermute | solution.py:337
  101.8 8.1 %shard_map.192 = (f32[96,768]{1,0:T(8,128)}, f32[16,128]{1,0:T(8,128)}, f32[96,128]{1,0:T(8,128)S(1)}, f32[8,128]{1,0:T(8,128)S(1)}) custom-call(s32[2]{0:T(128)S(1)} %pad_add_fusion.pos, f32[2,496,128]{2,1,0:T(8,128)S(1)} %pad_maximum_fusion.1.refs_0_, f32[2,496,128]{2,1,0:T(8,128)S(1)} %collective-permute-done.31.refs_1_, ...), custom_call_target="tpu_custom_call" | custom-call | flops 3000000000 | bytes 4000000 | tf_op jit(solution)/shard_map/pallas_call | solution.py:492
  110.0 3.6 %collective-permute-done.35.refs_1_ = f32[2,384,128]{2,1,0:T(8,128)S(1)} collective-permute-done((f32[2,384,128]{2,1,0:T(8,128)S(1)}, f32[2,384,128]{2,1,0:T(8,128)S(1)}, u32[]{:S(2)}, u32[]{:S(2)}) %collective-permute-start.35) | collective-permute-done | bytes 393248 | tf_op jit(solution)/shard_map/ppermute | solution.py:337
  113.7 2.7 %shard_map.193 = (f32[384,768]{1,0:T(8,128)S(1)}, f32[384,768]{1,0:T(8,128)S(1)}) custom-call(s32[2]{0:T(128)S(1)} %pad_add_fusion.pos, f32[384,768]{1,0:T(8,128)S(1)} %get-tuple-element.184.x_ref, f32[2,576,128]{2,1,0:T(8,128)S(1)} %pad_maximum_fusion.refs_0_, f32[2,576,128]{2,1,0:T(8,128)S(1)} %collective-permute-done.29.refs_1_, ...), custom_call_target="tpu_custom_call" | custom-call | flops 1000000000 | bytes 4000000 | tf_op jit(solution)/shard_map/pallas_call | solution.py:500
  116.5 7.7 %shard_map.194 = (f32[96,768]{1,0:T(8,128)}, f32[96,768]{1,0:T(8,128)S(1)}, f32[8,128]{1,0:T(8,128)S(1)}) custom-call(s32[2]{0:T(128)S(1)} %pad_add_fusion.pos, f32[384,768]{1,0:T(8,128)S(1)} %get-tuple-element.204.t_ref, f32[384,768]{1,0:T(8,128)S(1)} %get-tuple-element.205.rows_ref, f32[2,384,128]{2,1,0:T(8,128)S(1)} %pad_maximum_fusion.3.refs_0_, ...), custom_call_target="tpu_custom_call" | custom-call | flops 3000000000 | bytes 4000000 | tf_op jit(solution)/shard_map/pallas_call | solution.py:505
  (119 shorter events, 34.6 us)
Async XLA Ops:
  15.3 8.9 %collective-permute-start.2 = (f32[2,384,128]{2,1,0:T(8,128)}, f32[2,384,128]{2,1,0:T(8,128)}, u32[]{:S(2)}, u32[]{:S(2)}) collective-permute-start(f32[2,384,128]{2,1,0:T(8,128)} %get-tuple-element.127), channel_id=1, source_target_pairs={{0,8},{4,20},{8,0},{12,28},{16,24},{20,4},{24,16},{28,12},{1,9},{5... | collective-permute-start | bytes 1179656 | tf_op jit(solution)/shard_map/ppermute | solution.py:337
  18.1 13.6 %collective-permute-start.1 = (f32[2,496,128]{2,1,0:T(8,128)S(1)}, f32[2,496,128]{2,1,0:T(8,128)}, u32[]{:S(2)}, u32[]{:S(2)}) collective-permute-start(f32[2,496,128]{2,1,0:T(8,128)S(1)} %get-tuple-element.126), channel_id=1, source_target_pairs={{0,8},{4,20},{8,0},{12,28},{16,24},{20,4},{24,16},{28,12},{1,9},{5... | collective-permute-start | bytes 1523720 | tf_op jit(solution)/shard_map/ppermute | solution.py:337
  18.2 22.5 %collective-permute-start.4 = (f32[2,576,128]{2,1,0:T(8,128)S(1)}, f32[2,576,128]{2,1,0:T(8,128)S(1)}, u32[]{:S(2)}, u32[]{:S(2)}) collective-permute-start(f32[2,576,128]{2,1,0:T(8,128)S(1)} %get-tuple-element.130), channel_id=1, source_target_pairs={{0,8},{4,20},{8,0},{12,28},{16,24},{20,4},{24,16},{28,12},{1,9},{5... | collective-permute-start | bytes 1769480 | tf_op jit(solution)/shard_map/ppermute | solution.py:337
  25.1 9.7 %collective-permute-start.5 = (f32[384,128]{1,0:T(8,128)S(1)}, f32[384,128]{1,0:T(8,128)S(1)}, u32[]{:S(2)}, u32[]{:S(2)}) collective-permute-start(f32[384,128]{1,0:T(8,128)S(1)} %fusion.2), channel_id=1, source_target_pairs={{0,16},{4,12},{8,24},{12,4},{16,0},{20,28},{24,8},{28,20},{1,17},{... | collective-permute-start | bytes 589832 | tf_op jit(solution)/shard_map/ppermute | solution.py:341
  32.7 11.6 %collective-permute-start.3 = (f32[496,128]{1,0:T(8,128)S(1)}, f32[496,128]{1,0:T(8,128)S(1)}, u32[]{:S(2)}, u32[]{:S(2)}) collective-permute-start(f32[496,128]{1,0:T(8,128)S(1)} %add_bitcast_fusion.1), channel_id=1, source_target_pairs={{0,16},{4,12},{8,24},{12,4},{16,0},{20,28},{24,8},{28,20},{1,17},{... | collective-permute-start | bytes 761864 | tf_op jit(solution)/shard_map/ppermute | solution.py:341
  35.8 9.5 %collective-permute-start.8 = (f32[192,128]{1,0:T(8,128)S(1)}, f32[192,128]{1,0:T(8,128)S(1)}, u32[]{:S(2)}, u32[]{:S(2)}) collective-permute-start(f32[192,128]{1,0:T(8,128)S(1)} %slice_select_fusion.3), channel_id=1, source_target_pairs={{0,1},{1,0},{2,3},{3,2},{4,5},{5,4},{6,7},{7,6},{8,9},{9,8},{10,11... | collective-permute-start | bytes 294920 | tf_op jit(solution)/shard_map/ppermute | solution.py:345
  40.7 9.0 %collective-permute-start.7 = (f32[576,128]{1,0:T(8,128)S(1)}, f32[576,128]{1,0:T(8,128)S(1)}, u32[]{:S(2)}, u32[]{:S(2)}) collective-permute-start(f32[576,128]{1,0:T(8,128)S(1)} %add_bitcast_fusion), channel_id=1, source_target_pairs={{0,16},{4,12},{8,24},{12,4},{16,0},{20,28},{24,8},{28,20},{1,17},{... | collective-permute-start | bytes 884744 | tf_op jit(solution)/shard_map/ppermute | solution.py:341
  42.8 11.6 %collective-permute-start.11 = (f32[2,384,128]{2,1,0:T(8,128)S(1)}, f32[2,384,128]{2,1,0:T(8,128)S(1)}, u32[]{:S(2)}, u32[]{:S(2)}) collective-permute-start(f32[2,384,128]{2,1,0:T(8,128)S(1)} %get-tuple-element.146), channel_id=1, source_target_pairs={{0,8},{4,20},{8,0},{12,28},{16,24},{20,4},{24,16},{28,12},{1,9},{5... | collective-permute-start | bytes 1179656 | tf_op jit(solution)/shard_map/ppermute | solution.py:337
  45.4 10.4 %collective-permute-start.10 = (f32[192,128]{1,0:T(8,128)S(1)}, f32[192,128]{1,0:T(8,128)S(1)}, u32[]{:S(2)}, u32[]{:S(2)}) collective-permute-start(f32[192,128]{1,0:T(8,128)S(1)} %select_add_fusion.3), channel_id=1, source_target_pairs={{0,2},{1,3},{2,0},{3,1},{4,6},{5,7},{6,4},{7,5},{8,10},{9,11},{10,... | collective-permute-start | bytes 294920 | tf_op jit(solution)/shard_map/ppermute | solution.py:345
  49.8 7.6 %collective-permute-start.14 = (f32[288,128]{1,0:T(8,128)S(1)}, f32[288,128]{1,0:T(8,128)S(1)}, u32[]{:S(2)}, u32[]{:S(2)}) collective-permute-start(f32[288,128]{1,0:T(8,128)S(1)} %slice_select_fusion), channel_id=1, source_target_pairs={{0,1},{1,0},{2,3},{3,2},{4,5},{5,4},{6,7},{7,6},{8,9},{9,8},{10,11... | collective-permute-start | bytes 442376 | tf_op jit(solution)/shard_map/ppermute | solution.py:345
  54.5 7.2 %collective-permute-start.9 = (f32[248,128]{1,0:T(8,128)S(1)}, f32[248,128]{1,0:T(8,128)S(1)}, u32[]{:S(2)}, u32[]{:S(2)}) collective-permute-start(f32[248,128]{1,0:T(8,128)S(1)} %select_add_fusion.1), channel_id=1, source_target_pairs={{0,2},{1,3},{2,0},{3,1},{4,6},{5,7},{6,4},{7,5},{8,10},{9,11},{10,... | collective-permute-start | bytes 380936 | tf_op jit(solution)/shard_map/ppermute | solution.py:345
  60.2 7.3 %collective-permute-start.18 = (f32[192,128]{1,0:T(8,128)S(1)}, f32[192,128]{1,0:T(8,128)S(1)}, u32[]{:S(2)}, u32[]{:S(2)}) collective-permute-start(f32[192,128]{1,0:T(8,128)S(1)} %slice_select_fusion.2), channel_id=1, source_target_pairs={{0,1},{1,0},{2,3},{3,2},{4,5},{5,4},{6,7},{7,6},{8,9},{9,8},{10,11... | collective-permute-start | bytes 294920 | tf_op jit(solution)/shard_map/ppermute | solution.py:345
  67.7 6.7 %collective-permute-start.16 = (f32[288,128]{1,0:T(8,128)S(1)}, f32[288,128]{1,0:T(8,128)S(1)}, u32[]{:S(2)}, u32[]{:S(2)}) collective-permute-start(f32[288,128]{1,0:T(8,128)S(1)} %select_add_fusion), channel_id=1, source_target_pairs={{0,2},{1,3},{2,0},{3,1},{4,6},{5,7},{6,4},{7,5},{8,10},{9,11},{10,... | collective-permute-start | bytes 442376 | tf_op jit(solution)/shard_map/ppermute | solution.py:345
  67.8 6.6 %collective-permute-start.15 = (f32[248,128]{1,0:T(8,128)S(1)}, f32[248,128]{1,0:T(8,128)S(1)}, u32[]{:S(2)}, u32[]{:S(2)}) collective-permute-start(f32[248,128]{1,0:T(8,128)S(1)} %add.124), channel_id=1, source_target_pairs={{0,1},{1,0},{2,3},{3,2},{4,5},{5,4},{6,7},{7,6},{8,9},{9,8},{10,11... | collective-permute-start | bytes 380936 | tf_op jit(solution)/shard_map/ppermute | solution.py:345
  73.5 10.6 %collective-permute-start.21 = (f32[2,384,128]{2,1,0:T(8,128)S(1)}, f32[2,384,128]{2,1,0:T(8,128)S(1)}, u32[]{:S(2)}, u32[]{:S(2)}) collective-permute-start(f32[2,384,128]{2,1,0:T(8,128)S(1)} %pad_maximum_fusion.2.refs_0_), channel_id=1, source_target_pairs={{0,8},{4,20},{8,0},{12,28},{16,24},{20,4},{24,16},{28,12},{1,9},{5... | collective-permute-start | bytes 1179656 | tf_op jit(solution)/shard_map/ppermute | solution.py:337
  75.2 8.9 %collective-permute-start.20 = (f32[496,128]{1,0:T(8,128)S(1)}, f32[496,128]{1,0:T(8,128)S(1)}, u32[]{:S(2)}, u32[]{:S(2)}) collective-permute-start(f32[496,128]{1,0:T(8,128)S(1)} %get-tuple-element.167), channel_id=1, source_target_pairs={{0,16},{4,12},{8,24},{12,4},{16,0},{20,28},{24,8},{28,20},{1,17},{... | collective-permute-start | bytes 761864 | tf_op jit(solution)/shard_map/ppermute | solution.py:341
  76.6 6.6 %collective-permute-start.22 = (f32[288,128]{1,0:T(8,128)S(1)}, f32[288,128]{1,0:T(8,128)S(1)}, u32[]{:S(2)}, u32[]{:S(2)}) collective-permute-start(f32[288,128]{1,0:T(8,128)S(1)} %add.129), channel_id=1, source_target_pairs={{0,1},{1,0},{2,3},{3,2},{4,5},{5,4},{6,7},{7,6},{8,9},{9,8},{10,11... | collective-permute-start | bytes 442376 | tf_op jit(solution)/shard_map/ppermute | solution.py:345
  84.1 7.1 %collective-permute-start.24 = (f32[2,496,128]{2,1,0:T(8,128)S(1)}, f32[2,496,128]{2,1,0:T(8,128)S(1)}, u32[]{:S(2)}, u32[]{:S(2)}) collective-permute-start(f32[2,496,128]{2,1,0:T(8,128)S(1)} %pad_maximum_fusion.1.refs_0_), channel_id=1, source_target_pairs={{0,4},{4,0},{8,12},{12,8},{16,20},{20,16},{24,28},{28,24},{1,5},{5... | collective-permute-start | bytes 1523720 | tf_op jit(solution)/shard_map/ppermute | solution.py:333
  84.9 12.2 %collective-permute-start.27 = (f32[576,128]{1,0:T(8,128)S(1)}, f32[576,128]{1,0:T(8,128)S(1)}, u32[]{:S(2)}, u32[]{:S(2)}) collective-permute-start(f32[576,128]{1,0:T(8,128)S(1)} %get-tuple-element.182), channel_id=1, source_target_pairs={{0,16},{4,12},{8,24},{12,4},{16,0},{20,28},{24,8},{28,20},{1,17},{... | collective-permute-start | bytes 884744 | tf_op jit(solution)/shard_map/ppermute | solution.py:341
  89.5 7.9 %collective-permute-start.28 = (f32[384,128]{1,0:T(8,128)S(1)}, f32[384,128]{1,0:T(8,128)S(1)}, u32[]{:S(2)}, u32[]{:S(2)}) collective-permute-start(f32[384,128]{1,0:T(8,128)S(1)} %get-tuple-element.186), channel_id=1, source_target_pairs={{0,16},{4,12},{8,24},{12,4},{16,0},{20,28},{24,8},{28,20},{1,17},{... | collective-permute-start | bytes 589832 | tf_op jit(solution)/shard_map/ppermute | solution.py:341
  89.6 9.8 %collective-permute-start.31 = (f32[2,496,128]{2,1,0:T(8,128)S(1)}, f32[2,496,128]{2,1,0:T(8,128)S(1)}, u32[]{:S(2)}, u32[]{:S(2)}) collective-permute-start(f32[2,496,128]{2,1,0:T(8,128)S(1)} %pad_maximum_fusion.1.refs_0_), channel_id=1, source_target_pairs={{0,8},{4,20},{8,0},{12,28},{16,24},{20,4},{24,16},{28,12},{1,9},{5... | collective-permute-start | bytes 1523720 | tf_op jit(solution)/shard_map/ppermute | solution.py:337
  99.5 10.4 %collective-permute-start.29 = (f32[2,576,128]{2,1,0:T(8,128)S(1)}, f32[2,576,128]{2,1,0:T(8,128)S(1)}, u32[]{:S(2)}, u32[]{:S(2)}) collective-permute-start(f32[2,576,128]{2,1,0:T(8,128)S(1)} %pad_maximum_fusion.refs_0_), channel_id=1, source_target_pairs={{0,8},{4,20},{8,0},{12,28},{16,24},{20,4},{24,16},{28,12},{1,9},{5... | collective-permute-start | bytes 1769480 | tf_op jit(solution)/shard_map/ppermute | solution.py:337
  100.9 9.0 %collective-permute-start.32 = (f32[2,384,128]{2,1,0:T(8,128)S(1)}, f32[2,384,128]{2,1,0:T(8,128)S(1)}, u32[]{:S(2)}, u32[]{:S(2)}) collective-permute-start(f32[2,384,128]{2,1,0:T(8,128)S(1)} %pad_maximum_fusion.3.refs_0_), channel_id=1, source_target_pairs={{0,4},{4,0},{8,12},{12,8},{16,20},{20,16},{24,28},{28,24},{1,5},{5... | collective-permute-start | bytes 1179656 | tf_op jit(solution)/shard_map/ppermute | solution.py:333
  101.0 12.6 %collective-permute-start.35 = (f32[2,384,128]{2,1,0:T(8,128)S(1)}, f32[2,384,128]{2,1,0:T(8,128)S(1)}, u32[]{:S(2)}, u32[]{:S(2)}) collective-permute-start(f32[2,384,128]{2,1,0:T(8,128)S(1)} %pad_maximum_fusion.3.refs_0_), channel_id=1, source_target_pairs={{0,8},{4,20},{8,0},{12,28},{16,24},{20,4},{24,16},{28,12},{1,9},{5... | collective-permute-start | bytes 1179656 | tf_op jit(solution)/shard_map/ppermute | solution.py:337
  (27 other events, 119.4 us)
